TPU v7x, 32 devices: a whole 2x2x4 slice. The times are simulated.
32 devices in a mesh: ctx: 8 (over y, x, core), chan: 4 (over z).
Axes of the slice: x: 2, y: 2, z: 4, core: 2. Of those that a mesh axis runs over, the one named last changes fastest.
Arguments:
- features: bfloat16 [3, 2048, 4096], P(None, 'ctx', 'chan'), may hold values from -6 to 6
- saved_conv: bfloat16 [2048, 4096], P('ctx', 'chan'), may hold values from -6 to 6
- grad_out: bfloat16 [2048, 4096], P('ctx', 'chan'), may hold values from -6 to 6
- out_weight: bfloat16 [4096, 4096], P('chan'), may hold values from -0.09375 to 0.09375
- in_weight: bfloat16 [3, 4096, 4096], P(None, None, 'chan'), may hold values from -0.09375 to 0.09375
- short_taps: float32 [3, 3, 4096], P(None, None, 'chan'), may hold values from -3.5 to 3.5
- residues: float32 [16, 4096], P(None, 'chan'), may hold values from -1 to 1
- decay_time: float32 [16, 4096], P(None, 'chan'), may hold values from 25 to 10240
Outputs:
- grad_input: bfloat16 [4096, 2048], P('chan', 'ctx')
- grad_residue: float32 [16, 4096], P(None, 'chan')
All inputs are finite; a program needn't handle non-finite values.
Results may differ from a plain program's by a relative error of at most 0.019.
Values may be sent and summed in bfloat16 or wider, within the bound.
No kernel may reach another device: no remote copies, remote signals or barrier semaphores. Data moves between devices by JAX's collectives and lax.ppermute only.
A program may use at most 192 MiB of HBM per device.

v0:
```python
import jax
import jax.numpy as jnp
from jax import lax
from jax.sharding import PartitionSpec as P


def passed_along(value, axis, steps):
    count = lax.axis_size(axis)
    leading, last = (max(0, -steps), min(count, count - steps))
    return lax.ppermute(value, axis, [(source, source + steps) for source in range(leading, last)])


def local(features, saved_conv, grad_out, out_weight, in_weight, short_taps, residues, decay_time):
    highest = lax.Precision.HIGHEST
    length = features.shape[1]
    width = features.shape[2]
    poles = residues.shape[0]
    taps = short_taps.shape[1]
    span_rows = 128
    blocks = length // span_rows
    query_act = features[0].astype(jnp.float32)
    key_act = features[1].astype(jnp.float32)
    value_act = features[2].astype(jnp.float32)
    contract = (((1,), (1,)), ((), ()))
    everything = lax.all_gather(grad_out, "chan", axis=1, tiled=True)
    grad_gate = lax.dot_general(
        everything, out_weight, contract, preferred_element_type=jnp.float32
    )
    grad_conv = grad_gate * query_act
    grad_query = grad_gate * saved_conv.astype(jnp.float32)
    product = key_act * value_act
    rate = 1.0 / decay_time
    offset = jnp.arange(span_rows, dtype=jnp.float32)
    falling = jnp.exp(-rate[None] * offset[:, None, None])
    rising = jnp.exp(rate[None] * offset[:, None, None])
    closing = jnp.exp(-rate[None] * (span_rows - offset)[:, None, None])
    weighted = grad_conv.reshape(blocks, span_rows, 1, width) * falling[None]
    upper = (offset[None, :] >= offset[:, None]).astype(jnp.float32)
    tails = jnp.einsum(
        "st,btx->bsx",
        upper,
        weighted.reshape(blocks, span_rows, poles * width),
        precision=highest,
        preferred_element_type=jnp.float32,
    )
    tails = tails.reshape(blocks, span_rows, poles, width)
    starts = tails[:, 0]
    order = jnp.arange(blocks)
    gap = order[None, :] - order[:, None] - 1
    distance = (span_rows * jnp.maximum(gap, 0)).astype(jnp.float32)
    factor = jnp.where(
        gap[:, :, None, None] >= 0, jnp.exp(-rate[None, None] * distance[:, :, None, None]), 0.0
    )
    beyond = jnp.sum(factor * starts[None], axis=1)
    block_span = jnp.exp(-rate * span_rows)
    own_start = starts[0] + block_span * beyond[0]
    device_span = jnp.exp(-rate * length)
    empty = jnp.zeros_like(rate)

    def relay(step, incoming):
        return passed_along(own_start + device_span * incoming, "ctx", -1)

    incoming = lax.fori_loop(0, lax.axis_size("ctx") - 1, relay, empty)
    remain = (blocks - 1 - order).astype(jnp.float32)
    entering = beyond + jnp.exp(-rate[None] * span_rows * remain[:, None, None]) * incoming[None]
    state = tails * rising[None] + closing[None] * entering[:, None]
    grad_product = jnp.sum(residues[None, None] * state, axis=2).reshape(length, width)
    partial_res = jnp.sum(product.reshape(blocks, span_rows, 1, width) * state, axis=(0, 1))
    grad_key = grad_product * value_act
    grad_value = grad_product * key_act
    grad_acts = jnp.stack([grad_query, grad_key, grad_value])
    after = passed_along(grad_acts[:, : taps - 1, :], "ctx", -1)
    extended = jnp.concatenate([grad_acts, after], axis=1)
    filtered = short_taps[:, 0, None, :] * extended[:, 0:length, :]
    for lag in range(1, taps):
        filtered = filtered + short_taps[:, lag, None, :] * extended[:, lag : lag + length, :]
    grad_proj = filtered.astype(jnp.bfloat16)
    grad_input = lax.psum_scatter(
        jnp.einsum("jdc,jtc->dt", in_weight, grad_proj, preferred_element_type=jnp.float32).astype(
            jnp.bfloat16
        ),
        "chan",
        scatter_dimension=0,
        tiled=True,
    )
    grad_residue = lax.psum(partial_res, "ctx") / (length * lax.axis_size("ctx"))
    return (grad_input, grad_residue)


def solution(mesh):
    return jax.shard_map(
        local,
        mesh=mesh,
        in_specs=(
            P(None, "ctx", "chan"),
            P("ctx", "chan"),
            P("ctx", "chan"),
            P("chan", None),
            P(None, None, "chan"),
            P(None, None, "chan"),
            P(None, "chan"),
            P(None, "chan"),
        ),
        out_specs=(P("chan", "ctx"), P(None, "chan")),
        check_vma=False,
    )
```

profile of v0, /device:TPU:0, one launch (start us, length us, event | category | flops | bytes accessed | tf_op | source)
XLA Modules:
  0.0 299.6 jit_solution(4924021004675958790)
XLA Ops:
  9.9 9.4 %multiply_exponential_fusion = (f32[128,16384]{0,1:T(8,128)}, f32[128,16384]{0,1:T(8,128)}) fusion(f32[128]{0:T(128)S(1)} %iota_subtract_fusion, f32[16384]{0:T(1024)S(1)} %bitcast.81), kind=kLoop, calls=%fused_computation.7 | loop fusion | flops 4194304 | bytes 16843264 | tf_op jit(solution)/shard_map/exp | solution.py:36
  19.3 8.5 %multiply_exponential_fusion.2 = (f32[128,16,1024]{0,2,1:T(8,128)}, f32[128,16,1024]{0,2,1:T(8,128)}) fusion(f32[128]{0:T(128)S(1)} %iota_subtract_fusion, f32[16,1024]{1,0:T(8,128)S(1)} %get-tuple-element.47, f32[16,1024]{1,0:T(8,128)S(1)} %get-tuple-element.52), kind=kLoop, calls=%fused_computation.9 | loop fusion | flops 4194304 | bytes 16908800 | tf_op jit(solution)/shard_map/exp | solution.py:36
  27.8 8.1 %multiply_exponential_fusion.1 = f32[128,16384]{0,1:T(8,128)} fusion(f32[16384]{0:T(1024)S(1)} %bitcast.80), kind=kLoop, calls=%fused_computation.8 | loop fusion | flops 2097152 | bytes 8454144 | tf_op jit(solution)/shard_map/exp | solution.py:35
  35.9 22.3 %all-gather.2.cloned.1.call-done = bf16[256,4096]{1,0:T(8,128)(2,1)} async-done(((bf16[256,1024]{1,0:T(8,128)(2,1)}), bf16[256,4096]{1,0:T(8,128)(2,1)}) %all-gather.2.cloned.1.call-update) | async-done | bytes 2097168 | tf_op jit(solution)/shard_map/all_gather | solution.py:25
  58.2 7.4 %multiply_bitcast_fusion = (f32[1,256,1024]{2,1,0:T(8,128)}, f32[256,1024]{1,0:T(8,128)S(1)}) fusion(bf16[256,1024]{1,0:T(8,128)(2,1)S(1)} %copy-done.3, bf16[3,256,1024]{2,1,0:T(8,128)(2,1)} %param.10, bf16[256,4096]{1,0:T(8,128)(2,1)} %all-gather.2.cloned.1.call-done, bf16[1024,4096]{1,0:T(8,128)(2,1)} %param.13), kind=kOutput, calls=%fused_computation.29 | convolution fusion | flops 2148532224 | bytes 13631488 | tf_op jit(solution)/shard_map/dot_general | solution.py:26
  65.9 9.6 %bitcast_multiply_fusion.2 = f32[2,128,16384]{1,2,0:T(8,128)} fusion(f32[128,16384]{0,1:T(8,128)} %get-tuple-element.54, f32[2,128,1024]{1,2,0:T(8,128)S(1)} %copy.25), kind=kLoop, calls=%fused_computation.5 | loop fusion | flops 4194304 | bytes 26214400 | tf_op jit(solution)/shard_map/mul | solution.py:37
  75.5 14.7 %fusion.14 = f32[2,16384,128]{2,1,0:T(8,128)} fusion(f32[2,128,16384]{1,2,0:T(8,128)} %bitcast_multiply_fusion.2), kind=kOutput, calls=%fused_computation.39 | convolution fusion | flops 6442467328 | bytes 33554432 | tf_op jit(solution)/shard_map/st,btx->bsx/dot_general | solution.py:39
  90.2 7.4 %slice.51 = f32[1,1,16,1024]{1,3,2,0:T(8,128)} slice(f32[2,128,16,1024]{1,3,2,0:T(8,128)} %bitcast.70), slice={[0:1], [0:1], [0:16], [0:1024]} | slice | bytes 131072 | tf_op jit(solution)/shard_map/slice | solution.py:56
  97.6 10.0 %copy.34 = f32[2,1,16,1024]{3,2,0,1:T(8,128)S(1)} copy(f32[2,1,16,1024]{1,3,2,0:T(8,128)} %bitcast.71) | data formatting | bytes 262144
  107.6 5.3 %copy.35 = f32[1,1,16,1024]{3,2,1,0:T(8,128)S(1)} copy(f32[1,1,16,1024]{1,3,2,0:T(8,128)} %slice.51) | data formatting | bytes 131072
  113.0 36.7 %while.10 = (s32[]{:T(128)}, f32[16,1024]{1,0:T(8,128)S(1)}, f32[16,1024]{1,0:T(8,128)S(1)}, f32[16,1024]{1,0:T(8,128)S(1)}, s32[]{:T(128)}) while((s32[]{:T(128)}, f32[16,1024]{1,0:T(8,128)S(1)}, f32[16,1024]{1,0:T(8,128)S(1)}, f32[16,1024]{1,0:T(8,128)S(1)}, s32[]{:T(128)}) %tuple.40), condition=%wide.region_2.3_spmd, body=%wide.region_1.2_spmd.sunk | while | flops 32770 | bytes 524389 | solution.py:63
  117.5 3.7 %collective-permute-done = f32[16,1024]{1,0:T(8,128)S(1)} collective-permute-done((f32[16,1024]{1,0:T(8,128)S(1)}, f32[16,1024]{1,0:T(8,128)S(1)}, u32[]{:S(2)}, u32[]{:S(2)}) %collective-permute-start) | collective-permute-done | bytes 65568 | tf_op jit(solution)/shard_map/while/body/eval_jaxpr/ppermute | solution.py:10
  122.6 4.3 %collective-permute-done = f32[16,1024]{1,0:T(8,128)S(1)} collective-permute-done((f32[16,1024]{1,0:T(8,128)S(1)}, f32[16,1024]{1,0:T(8,128)S(1)}, u32[]{:S(2)}, u32[]{:S(2)}) %collective-permute-start) | collective-permute-done | bytes 65568 | tf_op jit(solution)/shard_map/while/body/eval_jaxpr/ppermute | solution.py:10
  128.2 4.3 %collective-permute-done = f32[16,1024]{1,0:T(8,128)S(1)} collective-permute-done((f32[16,1024]{1,0:T(8,128)S(1)}, f32[16,1024]{1,0:T(8,128)S(1)}, u32[]{:S(2)}, u32[]{:S(2)}) %collective-permute-start) | collective-permute-done | bytes 65568 | tf_op jit(solution)/shard_map/while/body/eval_jaxpr/ppermute | solution.py:10
  133.8 4.3 %collective-permute-done = f32[16,1024]{1,0:T(8,128)S(1)} collective-permute-done((f32[16,1024]{1,0:T(8,128)S(1)}, f32[16,1024]{1,0:T(8,128)S(1)}, u32[]{:S(2)}, u32[]{:S(2)}) %collective-permute-start) | collective-permute-done | bytes 65568 | tf_op jit(solution)/shard_map/while/body/eval_jaxpr/ppermute | solution.py:10
  139.4 4.3 %collective-permute-done = f32[16,1024]{1,0:T(8,128)S(1)} collective-permute-done((f32[16,1024]{1,0:T(8,128)S(1)}, f32[16,1024]{1,0:T(8,128)S(1)}, u32[]{:S(2)}, u32[]{:S(2)}) %collective-permute-start) | collective-permute-done | bytes 65568 | tf_op jit(solution)/shard_map/while/body/eval_jaxpr/ppermute | solution.py:10
  145.0 4.7 %collective-permute-done = f32[16,1024]{1,0:T(8,128)S(1)} collective-permute-done((f32[16,1024]{1,0:T(8,128)S(1)}, f32[16,1024]{1,0:T(8,128)S(1)}, u32[]{:S(2)}, u32[]{:S(2)}) %collective-permute-start) | collective-permute-done | bytes 65568 | tf_op jit(solution)/shard_map/while/body/eval_jaxpr/ppermute | solution.py:10
  149.8 11.3 %multiply_reduce_fusion = f32[2,128,1024]{1,2,0:T(8,128)S(1)} fusion(f32[2,128,16,1024]{1,3,2,0:T(8,128)} %bitcast.72, f32[2,16,1024]{2,1,0:T(8,128)S(1)} %multiply_add_fusion.2, f32[128,16,1024]{0,2,1:T(8,128)} %get-tuple-element.58, f32[128,16,1024]{0,2,1:T(8,128)} %get-tuple-element.59, f32[16,1024]{1,0:T(8,128)S(1)} %copy-done.2), kind=kLoop, calls=%fused_computation.6 | loop fusion | flops 20709376 | bytes 34799616 | tf_op jit(solution)/shard_map/reduce_sum | solution.py:67
  162.5 1.9 convert_multiply_fusion.2
  168.8 14.7 %fusion = f32[16384]{0:T(1024)S(1)} fusion(f32[2,16384,128]{2,1,0:T(8,128)} %fusion.14, f32[2,16384]{1,0:T(2,128)S(1)} %multiply_add_fusion.1, f32[128,16384]{0,1:T(8,128)} %get-tuple-element.53, f32[128,16384]{0,1:T(8,128)} %multiply_exponential_fusion.1, f32[2,128,1024]{1,2,0:T(8,128)} %copy.29), kind=kLoop, calls=%fused_computation.2 | loop fusion | flops 20955136 | bytes 34799616 | tf_op jit(solution)/shard_map/reduce_sum | solution.py:68
  184.6 13.2 %fusion.3 = bf16[4096,256]{0,1:T(8,128)(2,1)} fusion(bf16[3,4096,1024]{2,1,0:T(8,128)(2,1)} %param.14, f32[3,258,1024]{2,1,0:T(8,128)S(1)} %pad_maximum_fusion, f32[3,1024]{1,0:T(4,128)S(1)} %get-tuple-element.60, f32[3,1024]{1,0:T(4,128)S(1)} %get-tuple-element.61, f32[3,1024]{1,0:T(4,128)S(1)} %bitcast.84, f32[1,256,1024]{2,1,0:T(8,128)S(1)} %get-tuple-element.42, ...), kind=kOutput, calls=%fused_computation.14 | convolution fusion | flops 6449790976 | bytes 36749312 | tf_op jit(solution)/shard_map/jdc,jtc->dt/dot_general | solution.py:79
  197.8 47.6 %all-reduce.2.cloned.1.call-done = f32[16,1024]{1,0:T(8,128)} async-done(((f32[16,1024]{1,0:T(8,128)}), f32[16,1024]{1,0:T(8,128)}) %all-reduce.2.cloned.1.call-update) | async-done | bytes 65552 | tf_op jit(solution)/shard_map/psum | solution.py:86
  246.8 44.2 %reduce-scatter.2.cloned.1.call-done = bf16[1024,256]{0,1:T(8,128)(2,1)} async-done(((bf16[4096,256]{0,1:T(8,128)(2,1)}), bf16[1024,256]{0,1:T(8,128)(2,1)}) %reduce-scatter.2.cloned.1.call-update) | async-done | bytes 524304 | tf_op jit(solution)/shard_map/reduce_scatter | solution.py:78
  291.0 2.0 copy.30
  (57 shorter events, 22.4 us)
Async XLA Ops:
  7.2 51.0 %all-gather.2.cloned.1.call-start = ((), (), s32[]{:S(2)}) async-start(), calls=%async_computation.1 | async-start | bytes 2621440 | tf_op jit(solution)/shard_map/all_gather | solution.py:25
  7.9 237.4 %all-reduce.2.cloned.1.call-start = ((), (), s32[]{:S(2)}) async-start(), calls=%async_computation.3 | async-start | bytes 131072 | tf_op jit(solution)/shard_map/psum | solution.py:86
  27.8 30.4 %copy-start.3 = (bf16[256,1024]{1,0:T(8,128)(2,1)S(1)}, bf16[256,1024]{1,0:T(8,128)(2,1)}, u32[]{:S(2)}) copy-start(bf16[256,1024]{1,0:T(8,128)(2,1)} %param.11) | copy-start | bytes 1572868
  107.6 5.4 %copy-start.1 = (f32[16,1024]{1,0:T(8,128)S(1)}, f32[16,1024]{1,0:T(8,128)}, u32[]{:S(2)}) copy-start(f32[16,1024]{1,0:T(8,128)} %param.17) | copy-start | bytes 196612
  107.6 42.2 %copy-start.2 = (f32[16,1024]{1,0:T(8,128)S(1)}, f32[16,1024]{1,0:T(8,128)}, u32[]{:S(2)}) copy-start(f32[16,1024]{1,0:T(8,128)} %param.16) | copy-start | bytes 196612
  113.1 3.1 %collective-permute-start = (f32[16,1024]{1,0:T(8,128)S(1)}, f32[16,1024]{1,0:T(8,128)S(1)}, u32[]{:S(2)}, u32[]{:S(2)}) collective-permute-start(f32[16,1024]{1,0:T(8,128)S(1)} %multiply_add_fusion.4), channel_id=1, source_target_pairs={{4,0},{8,4},{12,8},{16,12},{20,16},{24,20},{28,24},{5,1},{9,5},{13... | collective-permute-start | bytes 196616 | tf_op jit(solution)/shard_map/while/body/eval_jaxpr/ppermute | solution.py:10
  116.2 5.0 %collective-permute-start = (f32[16,1024]{1,0:T(8,128)S(1)}, f32[16,1024]{1,0:T(8,128)S(1)}, u32[]{:S(2)}, u32[]{:S(2)}) collective-permute-start(f32[16,1024]{1,0:T(8,128)S(1)} %multiply_add_fusion.4), channel_id=1, source_target_pairs={{4,0},{8,4},{12,8},{16,12},{20,16},{24,20},{28,24},{5,1},{9,5},{13... | collective-permute-start | bytes 196616 | tf_op jit(solution)/shard_map/while/body/eval_jaxpr/ppermute | solution.py:10
  121.3 5.6 %collective-permute-start = (f32[16,1024]{1,0:T(8,128)S(1)}, f32[16,1024]{1,0:T(8,128)S(1)}, u32[]{:S(2)}, u32[]{:S(2)}) collective-permute-start(f32[16,1024]{1,0:T(8,128)S(1)} %multiply_add_fusion.4), channel_id=1, source_target_pairs={{4,0},{8,4},{12,8},{16,12},{20,16},{24,20},{28,24},{5,1},{9,5},{13... | collective-permute-start | bytes 196616 | tf_op jit(solution)/shard_map/while/body/eval_jaxpr/ppermute | solution.py:10
  126.9 5.6 %collective-permute-start = (f32[16,1024]{1,0:T(8,128)S(1)}, f32[16,1024]{1,0:T(8,128)S(1)}, u32[]{:S(2)}, u32[]{:S(2)}) collective-permute-start(f32[16,1024]{1,0:T(8,128)S(1)} %multiply_add_fusion.4), channel_id=1, source_target_pairs={{4,0},{8,4},{12,8},{16,12},{20,16},{24,20},{28,24},{5,1},{9,5},{13... | collective-permute-start | bytes 196616 | tf_op jit(solution)/shard_map/while/body/eval_jaxpr/ppermute | solution.py:10
  132.5 5.6 %collective-permute-start = (f32[16,1024]{1,0:T(8,128)S(1)}, f32[16,1024]{1,0:T(8,128)S(1)}, u32[]{:S(2)}, u32[]{:S(2)}) collective-permute-start(f32[16,1024]{1,0:T(8,128)S(1)} %multiply_add_fusion.4), channel_id=1, source_target_pairs={{4,0},{8,4},{12,8},{16,12},{20,16},{24,20},{28,24},{5,1},{9,5},{13... | collective-permute-start | bytes 196616 | tf_op jit(solution)/shard_map/while/body/eval_jaxpr/ppermute | solution.py:10
  138.1 5.6 %collective-permute-start = (f32[16,1024]{1,0:T(8,128)S(1)}, f32[16,1024]{1,0:T(8,128)S(1)}, u32[]{:S(2)}, u32[]{:S(2)}) collective-permute-start(f32[16,1024]{1,0:T(8,128)S(1)} %multiply_add_fusion.4), channel_id=1, source_target_pairs={{4,0},{8,4},{12,8},{16,12},{20,16},{24,20},{28,24},{5,1},{9,5},{13... | collective-permute-start | bytes 196616 | tf_op jit(solution)/shard_map/while/body/eval_jaxpr/ppermute | solution.py:10
  143.7 6.0 %collective-permute-start = (f32[16,1024]{1,0:T(8,128)S(1)}, f32[16,1024]{1,0:T(8,128)S(1)}, u32[]{:S(2)}, u32[]{:S(2)}) collective-permute-start(f32[16,1024]{1,0:T(8,128)S(1)} %multiply_add_fusion.4), channel_id=1, source_target_pairs={{4,0},{8,4},{12,8},{16,12},{20,16},{24,20},{28,24},{5,1},{9,5},{13... | collective-permute-start | bytes 196616 | tf_op jit(solution)/shard_map/while/body/eval_jaxpr/ppermute | solution.py:10
  166.0 18.3 %collective-permute-start.1 = (f32[3,2,1024]{2,1,0:T(2,128)S(1)}, f32[3,2,1024]{2,1,0:T(2,128)S(1)}, u32[]{:S(2)}, u32[]{:S(2)}) collective-permute-start(f32[3,2,1024]{2,1,0:T(2,128)S(1)} %slice.53), channel_id=1, source_target_pairs={{4,0},{8,4},{12,8},{16,12},{20,16},{24,20},{28,24},{5,1},{9,5},{13... | collective-permute-start | bytes 73736 | tf_op jit(solution)/shard_map/ppermute | solution.py:10
  168.8 15.5 %copy-start = (f32[1,256,1024]{2,1,0:T(8,128)S(1)}, f32[1,256,1024]{2,1,0:T(8,128)}, u32[]{:S(2)}) copy-start(f32[1,256,1024]{2,1,0:T(8,128)} %get-tuple-element.44) | copy-start | bytes 3145732
  184.3 106.8 %reduce-scatter.2.cloned.1.call-start = ((), (), s32[]{:S(2)}) async-start(), calls=%async_computation.2 | async-start | bytes 2621440 | tf_op jit(solution)/shard_map/reduce_scatter | solution.py:78
Sparse Core Ops, SparseCore 0:
  9.6 48.5 all-gather.1
  184.4 60.9 all-reduce.1
  247.7 43.2 reduce-scatter.1
where the time goes:
time: 300 us
  waiting for transfers between devices  142 us (47%)
  other arithmetic  68.2 us (23%)
  matrix products  35.2 us (12%)
  local copies, waits for them, and re-layouts  29.4 us (10%)
  between operations  14 us (5%)
  starting transfers between devices  10.5 us (4%)
    psum x1, waiting for transfers between devices, local(): lax.psum(partial_res, 'ctx') / (length * lax.axis_size('ctx'))  47.6 us
    reduce_scatter x1, waiting for transfers between devices, local(): lax.psum_scatter(jnp.einsum('jdc,jtc->dt', in_weight, grad_proj, preferre...  44.2 us
    ppermute x8, waiting for transfers between devices, passed_along(): lax.ppermute(value, axis, [(source, source + steps) for source in range(l...  27.4 us
    all_gather x1, waiting for transfers between devices, local(): everything = lax.all_gather(grad_out, 'chan', axis=1, tiled=True)  22.3 us
    exp x2, other arithmetic, local(): closing = jnp.exp(-rate[None] * (span_rows - offset)[:, None, None])  17.9 us
    unnamed x18, local copies, waits for them, and re-layouts  17.4 us
    reduce_sum x1, other arithmetic, local(): jnp.sum(product.reshape(blocks, span_rows, 1, width) * state, axis=(0, 1))  14.7 us
    dot_general x1, matrix products, local(): jnp.einsum('st,btx->bsx', upper, weighted.reshape(blocks, span_rows, pole...  14.7 us
  transfers between devices with their start and end apart: 11, of which 10 were waited for; matrix products, arithmetic and copies ran while one was open for 20% of the time, Pallas kernels for 0%

commit v1 on v0

v1 whole, which is shorter than its diff:
```python
import functools

import jax
import jax.numpy as jnp
from jax import lax
from jax.experimental import pallas as pl
from jax.experimental.pallas import tpu as pltpu
from jax.sharding import PartitionSpec as P

LANES = 128
ROWS = 8
NT = (((1,), (1,)), ((), ()))


def params(mib):
    return pltpu.CompilerParams(vmem_limit_bytes=mib * 2**20)


def whole(shape):
    return pl.BlockSpec(shape, lambda *_: (0,) * len(shape))


def tile(token):
    return pl.ds(pl.multiple_of(token * ROWS, ROWS), ROWS)


def tree_sum(terms):
    terms = list(terms)
    while len(terms) > 1:
        paired = [a + b for a, b in zip(terms[::2], terms[1::2])]
        terms = paired + terms[2 * len(paired):]
    return terms[0]


def spread_kernel(features, saved, out):
    tokens, width = saved.shape
    if width < ROWS * LANES:
        out[...] = jnp.zeros(out.shape, out.dtype)
    for group in range(width // LANES):
        columns = pl.ds(group * LANES, LANES)
        rows = pl.ds(group, tokens, stride=ROWS)
        for which in range(3):
            out[which, rows, :] = features[which, :, columns].astype(jnp.float32)
        out[3, rows, :] = saved[:, columns].astype(jnp.float32)


def spread_acts(features, saved):
    tokens = saved.shape[0]
    return pl.pallas_call(
        spread_kernel,
        out_shape=jax.ShapeDtypeStruct((4, tokens * ROWS, LANES), jnp.float32),
        compiler_params=params(24),
        name="spread",
    )(features, saved)


def gate_kernel(has_acc, shards, single, scal, *refs):
    acc = refs[0] if has_acc else None
    pieces = refs[has_acc:-1 - shards]
    weights = refs[-1 - shards:-1]
    out = refs[-1]
    half = pieces[0].shape[0]
    for part in range(2):
        rows = pl.ds(part * half, half)
        if single:
            lhs = [jnp.where(scal[shards] > 0, pieces[part][...], pieces[2 + part][...])]
        else:
            lhs = [pieces[2 * shard + part][...] for shard in range(shards)]
        terms = [
            lax.dot_general(x, w[...], NT, preferred_element_type=jnp.float32)
            for x, w in zip(lhs, weights)
        ]
        if has_acc:
            terms.append(acc[rows, :])
        out[rows, :] = tree_sum(terms)


def gate_step(acc, pieces, scalars, weight, shards, single):
    half, deep = pieces[0].shape
    width = weight.shape[0]
    block = min(256, width)
    tokens = 2 * half
    has_acc = acc is not None

    def weight_spec(shard):
        return pl.BlockSpec((block, deep), lambda i, s: (i, s[shard]))

    out_spec = pl.BlockSpec((tokens, block), lambda i, s: (0, i))
    return pl.pallas_call(
        functools.partial(gate_kernel, has_acc, shards, single),
        grid_spec=pltpu.PrefetchScalarGridSpec(
            num_scalar_prefetch=1,
            grid=(width // block,),
            in_specs=([out_spec] if has_acc else [])
            + [whole((half, deep)) for _ in pieces]
            + [weight_spec(shard) for shard in range(shards)],
            out_specs=out_spec,
        ),
        out_shape=jax.ShapeDtypeStruct((tokens, width), jnp.float32),
        compiler_params=params(24),
        cost_estimate=pl.CostEstimate(
            flops=2 * tokens * width * deep * shards,
            bytes_accessed=2 * shards * width * deep,
            transcendentals=0,
        ),
        name="gate_step",
    )(scalars, *([acc] if has_acc else []), *pieces, *([weight] * shards))


def close_kernel(extra, scal, acc, early, late, weight, acts, lam, gconv, gquery, packet, gate):
    step = pl.program_id(0)
    half = early.shape[0]
    tokens = 2 * half
    poles = lam.shape[0]
    groups = weight.shape[0] // LANES
    if groups * pl.num_programs(0) < ROWS:

        @pl.when(step == 0)
        def _():
            gate[...] = jnp.zeros(gate.shape, gate.dtype)

    for part, piece in enumerate((early, late)):
        value = acc[pl.ds(part * half, half), :] + lax.dot_general(
            piece[...], weight[...], NT, preferred_element_type=jnp.float32
        )
        for group in range(groups):
            start = part * half * ROWS + step * groups + group
            gate[pl.ds(start, half, stride=ROWS), :] = value[:, group * LANES:(group + 1) * LANES]

    @pl.when(step == pl.num_programs(0) - 1)
    def _():
        def body(n, state):
            at = tile(tokens - 1 - n)
            grad = gate[at, :]
            conv = grad * acts[0, at, :]
            gconv[at, :] = conv
            gquery[at, :] = grad * acts[3, at, :]
            return tuple(lam[m] * state[m] + conv for m in range(poles))

        zero = jnp.zeros((ROWS, LANES), jnp.float32)
        state = lax.fori_loop(0, tokens, body, (zero,) * poles, unroll=8)
        for m in range(poles):
            packet[m] = state[m]
        for row in range(extra - 1):
            packet[poles + row] = gconv[tile(row), :]
        for row in range(extra):
            packet[poles + extra - 1 + row] = gquery[tile(row), :]


def close_gate(acc, pieces, scalars, weight, acts, lam, extra):
    half, deep = pieces[0].shape
    width = weight.shape[0]
    block = min(256, width)
    tokens = 2 * half
    poles = lam.shape[0]
    flat = (tokens * ROWS, LANES)
    packed = (poles + 2 * extra - 1, ROWS, LANES)
    return pl.pallas_call(
        functools.partial(close_kernel, extra),
        grid_spec=pltpu.PrefetchScalarGridSpec(
            num_scalar_prefetch=1,
            grid=(width // block,),
            in_specs=[
                pl.BlockSpec((tokens, block), lambda i, s: (0, i)),
                whole((half, deep)),
                whole((half, deep)),
                pl.BlockSpec((block, deep), lambda i, s: (i, s[0])),
                whole(acts.shape),
                whole(lam.shape),
            ],
            out_specs=[whole(flat), whole(flat), whole(packed)],
            scratch_shapes=[pltpu.VMEM(flat, jnp.float32)],
        ),
        out_shape=[
            jax.ShapeDtypeStruct(flat, jnp.float32),
            jax.ShapeDtypeStruct(flat, jnp.float32),
            jax.ShapeDtypeStruct(packed, jnp.float32),
        ],
        compiler_params=params(32),
        cost_estimate=pl.CostEstimate(
            flops=2 * tokens * width * deep, bytes_accessed=8 * width * deep, transcendentals=0
        ),
        name="close_gate",
    )(scalars, acc, *pieces, weight, acts, lam)


def scan_kernel(
    taps, scal, gconv, gquery, acts, lam, grow, residues, filters, entering, halo, kv_halo,
    weight, proj, total, first, second, spread, buffer, sem,
):
    extra = taps - 1
    tokens, width = proj.shape[1:]
    poles = lam.shape[0]
    deep = buffer.shape[1]
    copy = pltpu.make_async_copy(
        weight.at[:, pl.ds(pl.multiple_of(scal[0] * deep, deep), deep), :], buffer, sem
    )
    copy.start()

    state = [entering[m] for m in range(poles)]
    keys, values, queries = [], [], []
    for row in range(extra):
        if row:
            state = [(state[m] - halo[row - 1]) * grow[m] for m in range(poles)]
        product = tree_sum([residues[m] * state[m] for m in range(poles)])
        keys.append(product * kv_halo[1, row])
        values.append(product * kv_halo[0, row])
        queries.append(halo[extra - 1 + row])

    def body(n, carry):
        state, sums, later = carry
        at = tile(tokens - 1 - n)
        conv = gconv[at, :]
        key = acts[1, at, :]
        value = acts[2, at, :]
        both = key * value
        state = tuple(lam[m] * state[m] + conv for m in range(poles))
        product = tree_sum([residues[m] * state[m] for m in range(poles)])
        sums = tuple(sums[m] + both * state[m] for m in range(poles))
        now = (gquery[at, :], product * value, product * key)
        for which in range(3):
            spread[which, at, :] = tree_sum(
                [filters[which, 0] * now[which]]
                + [filters[which, lag] * later[which][lag - 1] for lag in range(1, taps)]
            )
        later = tuple((now[which],) + later[which][:-1] for which in range(3))
        return state, sums, later

    zero = jnp.zeros((ROWS, LANES), jnp.float32)
    carry = (
        tuple(entering[m] for m in range(poles)),
        (zero,) * poles,
        (tuple(queries), tuple(keys), tuple(values)),
    )
    _, sums, _ = lax.fori_loop(0, tokens, body, carry, unroll=4)
    for m in range(poles):
        total[m] = sums[m]
    for which in range(3):
        for group in range(width // LANES):
            proj[which, :, pl.ds(group * LANES, LANES)] = spread[
                which, pl.ds(group, tokens, stride=ROWS), :
            ].astype(jnp.bfloat16)
    copy.wait()
    half = deep // 2
    block = min(256, half)
    for part, out in enumerate((first, second)):
        for start in range(0, half, block):
            value = tree_sum([
                lax.dot_general(
                    buffer[which, pl.ds(part * half + start, block), :], proj[which],
                    NT, preferred_element_type=jnp.float32,
                )
                for which in range(3)
            ])
            out[pl.ds(start, block), :] = value.astype(jnp.bfloat16)


def scan_block(chunk, gconv, gquery, acts, lam, grow, residues, filters, entering, halo, kv_halo,
               weight, deep, width):
    tokens = gconv.shape[0] // ROWS
    poles = lam.shape[0]
    taps = filters.shape[1]
    vmem = pl.BlockSpec(memory_space=pltpu.VMEM)
    return pl.pallas_call(
        functools.partial(scan_kernel, taps),
        in_specs=[pl.BlockSpec(memory_space=pltpu.SMEM)] + [vmem] * 10
        + [pl.BlockSpec(memory_space=pl.ANY)],
        out_specs=[vmem] * 4,
        out_shape=[
            jax.ShapeDtypeStruct((3, tokens, width), jnp.bfloat16),
            jax.ShapeDtypeStruct((poles, ROWS, LANES), jnp.float32),
            jax.ShapeDtypeStruct((deep // 2, tokens), jnp.bfloat16),
            jax.ShapeDtypeStruct((deep // 2, tokens), jnp.bfloat16),
        ],
        scratch_shapes=[
            pltpu.VMEM((3, tokens * ROWS, LANES), jnp.float32),
            pltpu.VMEM((3, deep, width), jnp.bfloat16),
            pltpu.SemaphoreType.DMA,
        ],
        compiler_params=params(36),
        cost_estimate=pl.CostEstimate(
            flops=6 * tokens * width * deep, bytes_accessed=16 * width * deep, transcendentals=0
        ),
        name="scan",
    )(chunk, gconv, gquery, acts, lam, grow, residues, filters, entering, halo, kv_halo, weight)


def project_kernel(scal, proj, weight, out):
    out[0] = tree_sum([
        lax.dot_general(weight[which], proj[which], NT, preferred_element_type=jnp.float32)
        for which in range(3)
    ]).astype(out.dtype)


def project(chunks, proj, weight, deep):
    _, tokens, width = proj.shape
    half = deep // 2
    count = 2 * chunks.shape[0]
    return pl.pallas_call(
        project_kernel,
        grid_spec=pltpu.PrefetchScalarGridSpec(
            num_scalar_prefetch=1,
            grid=(count,),
            in_specs=[
                whole(proj.shape),
                pl.BlockSpec((3, half, width), lambda i, s: (0, 2 * s[i // 2] + i % 2, 0)),
            ],
            out_specs=pl.BlockSpec((1, half, tokens), lambda i, s: (i, 0, 0)),
        ),
        out_shape=jax.ShapeDtypeStruct((count, half, tokens), jnp.bfloat16),
        compiler_params=params(24),
        cost_estimate=pl.CostEstimate(
            flops=6 * tokens * width * half * count,
            bytes_accessed=6 * width * half * count,
            transcendentals=0,
        ),
        name="project",
    )(chunks, proj, weight)


def scalars(*values):
    return jnp.stack([jnp.asarray(value, jnp.int32) for value in values])


def tiles(array):
    lead = array.shape[:-1]
    groups = array.shape[-1] // LANES
    array = array.reshape(lead + (groups, LANES))
    if groups < ROWS:
        array = jnp.pad(array, [(0, 0)] * len(lead) + [(0, ROWS - groups), (0, 0)])
    return array


def local(features, saved_conv, grad_out, out_weight, in_weight, short_taps, residues, decay_time):
    f32, bf16 = jnp.float32, jnp.bfloat16
    tokens, width = saved_conv.shape
    taps = short_taps.shape[1]
    extra = taps - 1
    poles = residues.shape[0]
    count = lax.axis_size("chan")
    me = lax.axis_index("chan")
    upper = (me >= count // 2).astype(jnp.int32)
    deep = in_weight.shape[1] // count
    blocks = lax.axis_size("ctx")
    core = lax.axis_index("ctx") % 2

    rate = tiles(1.0 / decay_time)
    lam = jnp.exp(-rate)
    grow = jnp.exp(rate)
    span = jnp.exp(-rate * tokens)
    res = tiles(residues)
    filters = tiles(short_taps)

    half = tokens // 2
    right = left = [grad_out[:half], grad_out[half:]]
    acts = spread_acts(features, saved_conv)
    acc = gate_step(None, right, scalars(me), out_weight, 1, False)
    kv_halo = acts[1:3].reshape(2, tokens, ROWS, LANES)[:, :extra]
    kv_halo = lax.ppermute(kv_halo, "ctx", [(i, i - 1) for i in range(1, blocks)])
    for phase in range(1, count - 1):
        to_right = [(i, i + 1) for i in range(phase - 1, count - 1)]
        to_left = [(i, i - 1) for i in range(1, count - phase + 1)]
        right = [lax.ppermute(piece, "chan", to_right) for piece in right]
        left = [lax.ppermute(piece, "chan", to_left) for piece in left]
        below = jnp.maximum(me - phase, 0)
        above = jnp.minimum(me + phase, count - 1)
        if 2 * phase < count:
            acc = gate_step(acc, right + left, scalars(below, above), out_weight, 2, False)
        else:
            which = jnp.where(upper > 0, below, above)
            acc = gate_step(acc, right + left, scalars(which, upper), out_weight, 1, True)
    last = [
        lax.ppermute(jnp.where(upper > 0, a, b), "chan", [(count - 2, count - 1), (1, 0)])
        for a, b in zip(right, left)
    ]
    which = jnp.where(upper > 0, jnp.maximum(me - count + 1, 0), jnp.minimum(me + count - 1, count - 1))
    gconv, gquery, packet = close_gate(acc, last, scalars(which), out_weight, acts, lam, extra)

    other = lax.ppermute(packet, "ctx", [(i, i ^ 1) for i in range(blocks)])
    first = jnp.where(core == 0, packet, other)
    second = jnp.where(core == 0, other, packet)
    chip = jnp.concatenate([first[:poles] + span * second[:poles], first[poles:]])
    chips = blocks // 2
    arrived = [
        lax.ppermute(
            chip if hop == 1 else chip[:poles], "ctx",
            [(i, i - 2 * hop) for i in range(2 * hop, blocks)],
        )
        for hop in range(1, chips)
    ]
    beyond = sum(
        jnp.exp(-rate * (2 * tokens * (hop - 1))) * arrived[hop - 1][:poles]
        for hop in range(1, chips)
    )
    entering = jnp.where(core == 0, second[:poles] + span * beyond, beyond)
    halo = jnp.where(core == 0, second[poles:], arrived[0][poles:])

    def single(phase):
        return jnp.where(
            upper > 0, jnp.maximum(me - (count - phase), 0), jnp.minimum(me + count - phase, count - 1)
        )

    proj, total, *sent = scan_block(
        scalars(single(1)), gconv, gquery, acts, lam, grow, res, filters, entering, halo, kv_halo,
        in_weight, deep, width,
    )
    order = []
    for phase in range(2, count):
        if 2 * phase <= count:
            order.append(single(phase))
        else:
            order.append(jnp.minimum(me + count - phase, count - 1))
            order.append(jnp.maximum(me - (count - phase), 0))
    order.append(me)
    parts = project(scalars(*order), proj, in_weight, deep)

    come = [lax.ppermute(piece, "chan", [(0, 1), (count - 1, count - 2)]) for piece in sent]
    from_left, from_right = come, [None, None]

    def added(*values):
        return sum(value.astype(f32) for value in values if value is not None).astype(bf16)

    place = 0
    for phase in range(2, count):
        to_right = [(i, i + 1) for i in range(phase)]
        to_left = [(i, i - 1) for i in range(count - phase, count)]
        for piece in range(2):
            if 2 * phase <= count:
                go = back = added(parts[2 * place + piece], from_left[piece], from_right[piece])
            else:
                if from_right[piece] is None:
                    from_right[piece] = from_left[piece]
                go = added(parts[2 * place + piece], from_left[piece])
                back = added(parts[2 * place + 2 + piece], from_right[piece])
            from_left[piece] = lax.ppermute(go, "chan", to_right)
            from_right[piece] = lax.ppermute(back, "chan", to_left)
        place += 1 if 2 * phase <= count else 2
    grad_input = jnp.concatenate(
        [added(parts[2 * place + piece], from_left[piece], from_right[piece]) for piece in range(2)]
    )

    step = 1
    while step < blocks:
        total = total + lax.ppermute(total, "ctx", [(i, i ^ step) for i in range(blocks)])
        step *= 2
    grad_residue = total[:, :width // LANES].reshape(poles, width) / (tokens * blocks)
    return grad_input, grad_residue


def solution(mesh):
    return jax.shard_map(
        local,
        mesh=mesh,
        in_specs=(
            P(None, "ctx", "chan"),
            P("ctx", "chan"),
            P("ctx", "chan"),
            P("chan", None),
            P(None, None, "chan"),
            P(None, None, "chan"),
            P(None, "chan"),
            P(None, "chan"),
        ),
        out_specs=(P("chan", "ctx"), P(None, "chan")),
        check_vma=False,
    )
```

time: 300 us -> 147 us (0.49)
  waiting for transfers between devices: 142 us -> 23.5 us
  other arithmetic: 68.2 us -> 4.43 us
  starting transfers between devices: 10.5 us -> 60.2 us
  matrix products: 35.2 us -> 0 us
  Pallas kernels: 0 us -> 34.3 us
  between operations: 14 us -> 1.3 us
  local copies, waits for them, and re-layouts: 29.4 us -> 21.9 us
    ppermute x8 -> x28, starting transfers between devices: 10.3 us -> 60.2 us  [the longest x4 17 us: local(): from_left[piece] = lax.ppermute(go, 'chan', to_right)]
    psum x1 -> x0, waiting for transfers between devices: 47.6 us -> none  [local(): lax.psum(partial_res, 'ctx') / (length * lax.axis_size('ctx'))]
    reduce_scatter x1 -> x0, waiting for transfers between devices: 44.2 us -> none  [local(): lax.psum_scatter(jnp.einsum('jdc,jtc->dt', in_weight, grad_proj, preferre...]
    dot_general x3 -> x0, matrix products: 35.2 us -> none  [the longest x1 14.7 us: local(): jnp.einsum('st,btx->bsx', upper, weighted.reshape(blocks, span_rows, pole...]
    pallas_call x0 -> x7, Pallas kernels: none -> 34.3 us  [the longest x3 11.9 us: gate_step(): pl.pallas_call(functools.partial(gate_kernel, has_acc, shards, single), g...]
    reduce_sum x3 -> x0, other arithmetic: 26.2 us -> none  [the longest x1 14.7 us: local(): jnp.sum(product.reshape(blocks, span_rows, 1, width) * state, axis=(0, 1))]
    exp x3 -> x0, other arithmetic: 26 us -> none  [the longest x2 17.9 us: local(): closing = jnp.exp(-rate[None] * (span_rows - offset)[:, None, None])]
    all_gather x1 -> x0, waiting for transfers between devices: 22.3 us -> none  [local(): everything = lax.all_gather(grad_out, 'chan', axis=1, tiled=True)]
  transfers between devices with their start and end apart: 11 -> 28, of which waited for: 10 -> 10; matrix products, arithmetic and copies ran while one was open for 20% -> 3% of each run, Pallas kernels for 0% -> 16%
where the time goes in v1:
time: 147 us; the launch traced here: 146 us
  starting transfers between devices  60.2 us (41%)
  Pallas kernels  34.3 us (23%)
  waiting for transfers between devices  23.5 us (16%)
  local copies, waits for them, and re-layouts  21.9 us (15%)
  other arithmetic  4.43 us (3%)
    unnamed x40, local copies, waits for them, and re-layouts  20.7 us
    ppermute x4, starting transfers between devices, local(): from_left[piece] = lax.ppermute(go, 'chan', to_right)  17 us
    ppermute x4, starting transfers between devices, local(): right = [lax.ppermute(piece, 'chan', to_right) for piece in right]  13.6 us
    pallas_call x3, Pallas kernels, gate_step(): pl.pallas_call(functools.partial(gate_kernel, has_acc, shards, single), g...  11.9 us
    pallas_call x1, Pallas kernels, project(): pl.pallas_call(project_kernel, grid_spec=pltpu.PrefetchScalarGridSpec(num...  10.5 us
    ppermute x2, starting transfers between devices, local(): lax.ppermute(piece, 'chan', [(0, 1), (count - 1, count - 2)])  8.88 us
    pallas_call x1, Pallas kernels, scan_block(): pl.pallas_call(functools.partial(scan_kernel, taps), in_specs=[pl.BlockSp...  7.24 us
    ppermute x4, waiting for transfers between devices, local(): from_left[piece] = lax.ppermute(go, 'chan', to_right)  7 us
  transfers between devices with their start and end apart: 28, of which 10 were waited for; matrix products, arithmetic and copies ran while one was open for 3% of the time, Pallas kernels for 16%

profile of v1, /device:TPU:0, one launch (start us, length us, event | category | flops | bytes accessed | tf_op | source)
XLA Modules:
  0.0 145.7 jit_solution(14611895643918014686)
XLA Ops:
  3.0 6.3 %collective-permute-start.1 = (bf16[128,1024]{1,0:T(8,128)(2,1)S(1)}, bf16[128,1024]{1,0:T(8,128)(2,1)}, u32[]{:S(2)}, u32[]{:S(2)}) collective-permute-start(bf16[128,1024]{1,0:T(8,128)(2,1)S(1)} %get-tuple-element.22.refs_1_), channel_id=1, source_target_pairs={{0,1},{1,2},{2,3},{4,5},{5,6},{6,7},{8,9},{9,10},{10,11},{12,13},{... | collective-permute-start | bytes 786440 | tf_op jit(solution)/shard_map/ppermute | solution.py:363
  10.6 5.3 %collective-permute-start = (bf16[128,1024]{1,0:T(8,128)(2,1)S(1)}, bf16[128,1024]{1,0:T(8,128)(2,1)}, u32[]{:S(2)}, u32[]{:S(2)}) collective-permute-start(bf16[128,1024]{1,0:T(8,128)(2,1)S(1)} %get-tuple-element.23.refs_0_), channel_id=1, source_target_pairs={{0,1},{1,2},{2,3},{4,5},{5,6},{6,7},{8,9},{9,10},{10,11},{12,13},{... | collective-permute-start | bytes 786440 | tf_op jit(solution)/shard_map/ppermute | solution.py:363
  17.9 1.6 %exponential_bitcast_fusion.2 = (f32[2,8,8,128]{3,1,2,0:T(8,128)}, f32[2,8,8,128]{3,1,2,0:T(8,128)}, f32[2,8,8,128]{3,1,2,0:T(8,128)S(1)}, f32[2,8,8,128]{3,1,2,...) fusion(f32[16,1024]{1,0:T(8,128)} %param.15), kind=kLoop, calls=%fused_computation.45 | loop fusion | flops 98304 | bytes 458752
  22.2 3.4 %copy-done = bf16[1024,4096]{1,0:T(8,128)(2,1)S(1)} copy-done((bf16[1024,4096]{1,0:T(8,128)(2,1)S(1)}, bf16[1024,4096]{1,0:T(8,128)(2,1)}, u32[]{:S(2)}) %copy-start) | copy-done | bytes 8388632
  26.5 2.2 %gate_step.3.refs_0_ = f32[256,1024]{1,0:T(8,128)S(1)} custom-call(s32[1]{0:T(128)} %bitcast.3.scal, bf16[128,1024]{1,0:T(8,128)(2,1)S(1)} %copy-done.7, bf16[128,1024]{1,0:T(8,128)(2,1)S(1)} %get-tuple-element.22.refs_1_, bf16[1024,4096]{1,0:T(8,128)(2,1)S(1)} %copy-done), custom_call_target="tpu_custom_call" | custom-call | flops 536870912 | bytes 2097152 | tf_op jit(solution)/shard_map/gate_step/pallas_call | solution.py:89
  35.7 3.4 %copy-done.1 = bf16[1024,4096]{1,0:T(8,128)(2,1)S(1)} copy-done((bf16[1024,4096]{1,0:T(8,128)(2,1)S(1)}, bf16[1024,4096]{1,0:T(8,128)(2,1)}, u32[]{:S(2)}) %copy-start.1) | copy-done | bytes 8388632
  39.0 5.9 %gate_step.4.refs_0_ = f32[256,1024]{1,0:T(8,128)S(1)} custom-call(s32[2]{0:T(128)S(1)} %pad_add_fusion.2.scal, f32[256,1024]{1,0:T(8,128)S(1)} %gate_step.3.refs_0_, bf16[128,1024]{1,0:T(8,128)(2,1)} %collective-permute-done.refs_1_, bf16[128,1024]{1,0:T(8,128)(2,1)} %collective-permute-done.1.refs_2_, bf16[128,1024]{1,0:T(8,128)(2,1)} %collective-permute-done.2.refs_3_, ...), custom_call_target="tpu_custom_call" | custom-call | flops 1073741824 | bytes 4194304 | tf_op jit(solution)/shard_map/gate_step/pallas_call | solution.py:89
  44.9 3.8 %gate_step.5.acc = f32[256,1024]{1,0:T(8,128)S(1)} custom-call(s32[2]{0:T(128)S(1)} %pad_add_fusion.1.scal, f32[256,1024]{1,0:T(8,128)S(1)} %gate_step.4.refs_0_, bf16[128,1024]{1,0:T(8,128)(2,1)} %collective-permute-done.4.refs_1_, bf16[128,1024]{1,0:T(8,128)(2,1)S(1)} %collective-permute-done.5.refs_2_, bf16[128,1024]{1,0:T(8,128)(2,1)} %collective-permute-done.6.refs_3_, ...), custom_call_target="tpu_custom_call" | custom-call | flops 536870912 | bytes 2097152 | tf_op jit(solution)/shard_map/gate_step/pallas_call | solution.py:89
  49.8 2.8 %collective-permute-done.8.early = bf16[128,1024]{1,0:T(8,128)(2,1)S(1)} collective-permute-done((bf16[128,1024]{1,0:T(8,128)(2,1)S(1)}, bf16[128,1024]{1,0:T(8,128)(2,1)S(1)}, u32[]{:S(2)}, u32[]{:S(2)}) %collective-permute-start.8) | collective-permute-done | bytes 262176 | tf_op jit(solution)/shard_map/ppermute | solution.py:373
  52.6 3.6 %close_gate.1 = (f32[2048,128]{1,0:T(8,128)S(1)}, f32[2048,128]{1,0:T(8,128)S(1)}, f32[19,8,128]{2,1,0:T(8,128)S(1)}) custom-call(s32[1]{0:T(128)} %bitcast.4.scal, f32[256,1024]{1,0:T(8,128)S(1)} %gate_step.5.acc, bf16[128,1024]{1,0:T(8,128)(2,1)S(1)} %collective-permute-done.8.early, bf16[128,1024]{1,0:T(8,128)(2,1)S(1)} %collective-permute-done.9.late, ...), custom_call_target="tpu_custom_call" | custom-call | flops 536870912 | bytes 8388608 | tf_op jit(solution)/shard_map/close_gate/pallas_call | solution.py:158
  62.1 4.0 %collective-permute-done.13 = f32[16,8,128]{2,1,0:T(8,128)S(1)} collective-permute-done((f32[16,8,128]{2,1,0:T(8,128)S(1)}, f32[16,8,128]{2,1,0:T(8,128)S(1)}, u32[]{:S(2)}, u32[]{:S(2)}) %collective-permute-start.13) | collective-permute-done | bytes 65568 | tf_op jit(solution)/shard_map/ppermute | solution.py:385
  67.9 2.2 %copy-done.4 = f32[4,2048,128]{2,1,0:T(8,128)S(1)} copy-done((f32[4,2048,128]{2,1,0:T(8,128)S(1)}, f32[4,2048,128]{2,1,0:T(8,128)}, u32[]{:S(2)}) %copy-start.4) | copy-done | bytes 4194328
  70.1 7.2 %scan.1 = (bf16[3,256,1024]{2,1,0:T(8,128)(2,1)S(1)}, f32[16,8,128]{2,1,0:T(8,128)S(1)}, bf16[512,256]{1,0:T(8,128)(2,1)S(1)}, bf16[512,256]{1,0:T(8,128)(2,1)S(1)}) custom-call(s32[1]{0:T(128)} %bitcast.4.scal, f32[2048,128]{1,0:T(8,128)S(1)} %get-tuple-element.9.gconv, f32[2048,128]{1,0:T(8,128)S(1)} %get-tuple-element.10.gquery, ...), custom_call_target="tpu_custom_call" | custom-call | flops 1610612736 | bytes 16777216 | tf_op jit(solution)/shard_map/scan/pallas_call | solution.py:264
  77.3 7.6 %collective-permute-start.15 = (bf16[512,256]{1,0:T(8,128)(2,1)S(1)}, bf16[512,256]{1,0:T(8,128)(2,1)S(1)}, u32[]{:S(2)}, u32[]{:S(2)}) collective-permute-start(bf16[512,256]{1,0:T(8,128)(2,1)S(1)} %get-tuple-element.13), channel_id=1, source_target_pairs={{0,1},{3,2},{4,5},{7,6},{8,9},{11,10},{12,13},{15,14},{16,17},{19,... | collective-permute-start | bytes 786440 | tf_op jit(solution)/shard_map/ppermute | solution.py:417
  86.2 8.1 %copy-done.2 = bf16[3,4096,1024]{2,1,0:T(8,128)(2,1)S(1)} copy-done((bf16[3,4096,1024]{2,1,0:T(8,128)(2,1)S(1)}, bf16[3,4096,1024]{2,1,0:T(8,128)(2,1)}, u32[]{:S(2)}) %copy-start.2) | copy-done | bytes 25165848
  94.4 10.5 %project.1 = bf16[8,512,256]{2,1,0:T(8,128)(2,1)S(1)} custom-call(s32[4]{0:T(128)S(1)} %pad_add_fusion.scal, bf16[3,256,1024]{2,1,0:T(8,128)(2,1)S(1)} %get-tuple-element.12.proj, bf16[3,4096,1024]{2,1,0:T(8,128)(2,1)S(1)} %copy-done.2), custom_call_target="tpu_custom_call" | custom-call | flops 6442450944 | bytes 25165824 | tf_op jit(solution)/shard_map/project/pallas_call | solution.py:299
  105.7 1.9 %collective-permute-start.16 = (bf16[512,256]{1,0:T(8,128)(2,1)S(1)}, bf16[512,256]{1,0:T(8,128)(2,1)S(1)}, u32[]{:S(2)}, u32[]{:S(2)}) collective-permute-start(bf16[512,256]{1,0:T(8,128)(2,1)S(1)} %fusion.6), channel_id=1, source_target_pairs={{0,1},{1,2},{4,5},{5,6},{8,9},{9,10},{12,13},{13,14},{16,17},{17,1... | collective-permute-start | bytes 786440 | tf_op jit(solution)/shard_map/ppermute | solution.py:435
  107.6 5.8 %collective-permute-done.16 = bf16[512,256]{1,0:T(8,128)(2,1)S(1)} collective-permute-done((bf16[512,256]{1,0:T(8,128)(2,1)S(1)}, bf16[512,256]{1,0:T(8,128)(2,1)S(1)}, u32[]{:S(2)}, u32[]{:S(2)}) %collective-permute-start.16) | collective-permute-done | bytes 262176 | tf_op jit(solution)/shard_map/ppermute | solution.py:435
  113.6 4.4 %collective-permute-start.17 = (bf16[512,256]{1,0:T(8,128)(2,1)S(1)}, bf16[512,256]{1,0:T(8,128)(2,1)S(1)}, u32[]{:S(2)}, u32[]{:S(2)}) collective-permute-start(bf16[512,256]{1,0:T(8,128)(2,1)S(1)} %get-tuple-element.19), channel_id=1, source_target_pairs={{0,1},{1,2},{2,3},{4,5},{5,6},{6,7},{8,9},{9,10},{10,11},{12,13},{... | collective-permute-start | bytes 786440 | tf_op jit(solution)/shard_map/ppermute | solution.py:435
  120.0 5.5 %collective-permute-start.21 = (bf16[512,256]{1,0:T(8,128)(2,1)S(1)}, bf16[512,256]{1,0:T(8,128)(2,1)S(1)}, u32[]{:S(2)}, u32[]{:S(2)}) collective-permute-start(bf16[512,256]{1,0:T(8,128)(2,1)S(1)} %get-tuple-element.20), channel_id=1, source_target_pairs={{0,1},{1,2},{4,5},{5,6},{8,9},{9,10},{12,13},{13,14},{16,17},{17,1... | collective-permute-start | bytes 786440 | tf_op jit(solution)/shard_map/ppermute | solution.py:435
  128.4 2.8 %collective-permute-done.26 = f32[16,8,128]{2,1,0:T(8,128)S(1)} collective-permute-done((f32[16,8,128]{2,1,0:T(8,128)S(1)}, f32[16,8,128]{2,1,0:T(8,128)S(1)}, u32[]{:S(2)}, u32[]{:S(2)}) %collective-permute-start.26) | collective-permute-done | bytes 65568 | tf_op jit(solution)/shard_map/ppermute | solution.py:444
  131.2 2.1 %collective-permute-start.27 = (f32[16,8,128]{2,1,0:T(8,128)S(1)}, f32[16,8,128]{2,1,0:T(8,128)S(1)}, u32[]{:S(2)}, u32[]{:S(2)}) collective-permute-start(f32[16,8,128]{2,1,0:T(8,128)S(1)} %add.93), channel_id=1, source_target_pairs={{0,16},{4,20},{8,24},{12,28},{16,0},{20,4},{24,8},{28,12},{1,17},{... | collective-permute-start | bytes 196616 | tf_op jit(solution)/shard_map/ppermute | solution.py:444
  134.9 5.2 %collective-permute-start.22 = (bf16[512,256]{1,0:T(8,128)(2,1)S(1)}, bf16[512,256]{1,0:T(8,128)(2,1)S(1)}, u32[]{:S(2)}, u32[]{:S(2)}) collective-permute-start(bf16[512,256]{1,0:T(8,128)(2,1)S(1)} %get-tuple-element.18), channel_id=1, source_target_pairs={{0,1},{1,2},{2,3},{4,5},{5,6},{6,7},{8,9},{9,10},{10,11},{12,13},{... | collective-permute-start | bytes 786440 | tf_op jit(solution)/shard_map/ppermute | solution.py:435
  140.7 2.9 %collective-permute-done.24 = bf16[512,256]{1,0:T(8,128)(2,1)S(1)} collective-permute-done((bf16[512,256]{1,0:T(8,128)(2,1)S(1)}, bf16[512,256]{1,0:T(8,128)(2,1)S(1)}, u32[]{:S(2)}, u32[]{:S(2)}) %collective-permute-start.24) | collective-permute-done | bytes 262176 | tf_op jit(solution)/shard_map/ppermute | solution.py:436
  (104 shorter events, 36.1 us)
Async XLA Ops:
  1.7 14.2 %collective-permute-start.3 = (bf16[128,1024]{1,0:T(8,128)(2,1)S(1)}, bf16[128,1024]{1,0:T(8,128)(2,1)}, u32[]{:S(2)}, u32[]{:S(2)}) collective-permute-start(bf16[128,1024]{1,0:T(8,128)(2,1)S(1)} %get-tuple-element.22.refs_1_), channel_id=1, source_target_pairs={{1,0},{2,1},{3,2},{5,4},{6,5},{7,6},{9,8},{10,9},{11,10},{13,12},{... | collective-permute-start | bytes 786440 | tf_op jit(solution)/shard_map/ppermute | solution.py:364
  3.0 14.2 %collective-permute-start.1 = (bf16[128,1024]{1,0:T(8,128)(2,1)S(1)}, bf16[128,1024]{1,0:T(8,128)(2,1)}, u32[]{:S(2)}, u32[]{:S(2)}) collective-permute-start(bf16[128,1024]{1,0:T(8,128)(2,1)S(1)} %get-tuple-element.22.refs_1_), channel_id=1, source_target_pairs={{0,1},{1,2},{2,3},{4,5},{5,6},{6,7},{8,9},{9,10},{10,11},{12,13},{... | collective-permute-start | bytes 786440 | tf_op jit(solution)/shard_map/ppermute | solution.py:363
  9.3 10.2 %collective-permute-start.2 = (bf16[128,1024]{1,0:T(8,128)(2,1)S(1)}, bf16[128,1024]{1,0:T(8,128)(2,1)}, u32[]{:S(2)}, u32[]{:S(2)}) collective-permute-start(bf16[128,1024]{1,0:T(8,128)(2,1)S(1)} %get-tuple-element.23.refs_0_), channel_id=1, source_target_pairs={{1,0},{2,1},{3,2},{5,4},{6,5},{7,6},{9,8},{10,9},{11,10},{13,12},{... | collective-permute-start | bytes 786440 | tf_op jit(solution)/shard_map/ppermute | solution.py:364
  10.6 10.2 %collective-permute-start = (bf16[128,1024]{1,0:T(8,128)(2,1)S(1)}, bf16[128,1024]{1,0:T(8,128)(2,1)}, u32[]{:S(2)}, u32[]{:S(2)}) collective-permute-start(bf16[128,1024]{1,0:T(8,128)(2,1)S(1)} %get-tuple-element.23.refs_0_), channel_id=1, source_target_pairs={{0,1},{1,2},{2,3},{4,5},{5,6},{6,7},{8,9},{9,10},{10,11},{12,13},{... | collective-permute-start | bytes 786440 | tf_op jit(solution)/shard_map/ppermute | solution.py:363
  15.9 15.8 %collective-permute-start.7 = (bf16[128,1024]{1,0:T(8,128)(2,1)}, bf16[128,1024]{1,0:T(8,128)(2,1)S(1)}, u32[]{:S(2)}, u32[]{:S(2)}) collective-permute-start(bf16[128,1024]{1,0:T(8,128)(2,1)} %collective-permute-done.3.refs_4_), channel_id=1, source_target_pairs={{1,0},{2,1},{5,4},{6,5},{9,8},{10,9},{13,12},{14,13},{17,16},{18,1... | collective-permute-start | bytes 786440 | tf_op jit(solution)/shard_map/ppermute | solution.py:364
  17.2 14.5 %collective-permute-start.5 = (bf16[128,1024]{1,0:T(8,128)(2,1)}, bf16[128,1024]{1,0:T(8,128)(2,1)S(1)}, u32[]{:S(2)}, u32[]{:S(2)}) collective-permute-start(bf16[128,1024]{1,0:T(8,128)(2,1)} %collective-permute-done.1.refs_2_), channel_id=1, source_target_pairs={{1,2},{2,3},{5,6},{6,7},{9,10},{10,11},{13,14},{14,15},{17,18},{18... | collective-permute-start | bytes 786440 | tf_op jit(solution)/shard_map/ppermute | solution.py:363
  19.5 13.7 %collective-permute-start.6 = (bf16[128,1024]{1,0:T(8,128)(2,1)}, bf16[128,1024]{1,0:T(8,128)(2,1)}, u32[]{:S(2)}, u32[]{:S(2)}) collective-permute-start(bf16[128,1024]{1,0:T(8,128)(2,1)} %collective-permute-done.2.refs_3_), channel_id=1, source_target_pairs={{1,0},{2,1},{5,4},{6,5},{9,8},{10,9},{13,12},{14,13},{17,16},{18,1... | collective-permute-start | bytes 786440 | tf_op jit(solution)/shard_map/ppermute | solution.py:364
  20.8 12.5 %collective-permute-start.4 = (bf16[128,1024]{1,0:T(8,128)(2,1)}, bf16[128,1024]{1,0:T(8,128)(2,1)}, u32[]{:S(2)}, u32[]{:S(2)}) collective-permute-start(bf16[128,1024]{1,0:T(8,128)(2,1)} %collective-permute-done.refs_1_), channel_id=1, source_target_pairs={{1,2},{2,3},{5,6},{6,7},{9,10},{10,11},{13,14},{14,15},{17,18},{18... | collective-permute-start | bytes 786440 | tf_op jit(solution)/shard_map/ppermute | solution.py:363
  31.8 18.0 %collective-permute-start.9 = (bf16[128,1024]{1,0:T(8,128)(2,1)S(1)}, bf16[128,1024]{1,0:T(8,128)(2,1)S(1)}, u32[]{:S(2)}, u32[]{:S(2)}) collective-permute-start(bf16[128,1024]{1,0:T(8,128)(2,1)S(1)} %broadcast_select_fusion), channel_id=1, source_target_pairs={{2,3},{1,0},{6,7},{5,4},{10,11},{9,8},{14,15},{13,12},{18,19},{17,... | collective-permute-start | bytes 786440 | tf_op jit(solution)/shard_map/ppermute | solution.py:373
  34.3 18.3 %collective-permute-start.8 = (bf16[128,1024]{1,0:T(8,128)(2,1)S(1)}, bf16[128,1024]{1,0:T(8,128)(2,1)S(1)}, u32[]{:S(2)}, u32[]{:S(2)}) collective-permute-start(bf16[128,1024]{1,0:T(8,128)(2,1)S(1)} %broadcast_select_fusion.1), channel_id=1, source_target_pairs={{2,3},{1,0},{6,7},{5,4},{10,11},{9,8},{14,15},{13,12},{18,19},{17,... | collective-permute-start | bytes 786440 | tf_op jit(solution)/shard_map/ppermute | solution.py:373
  56.5 11.4 %collective-permute-start.14 = (f32[2,2,8,128]{3,2,1,0:T(8,128)S(1)}, f32[2,2,8,128]{3,2,1,0:T(8,128)S(1)}, u32[]{:S(2)}, u32[]{:S(2)}) collective-permute-start(f32[2,2,8,128]{3,2,1,0:T(8,128)S(1)} %slice.80), channel_id=1, source_target_pairs={{4,0},{8,4},{12,8},{16,12},{20,16},{24,20},{28,24},{5,1},{9,5},{13... | collective-permute-start | bytes 49160 | tf_op jit(solution)/shard_map/ppermute | solution.py:359
  58.1 8.0 %collective-permute-start.13 = (f32[16,8,128]{2,1,0:T(8,128)S(1)}, f32[16,8,128]{2,1,0:T(8,128)S(1)}, u32[]{:S(2)}, u32[]{:S(2)}) collective-permute-start(f32[16,8,128]{2,1,0:T(8,128)S(1)} %fusion.12), channel_id=1, source_target_pairs={{24,0},{28,4},{25,1},{29,5},{26,2},{30,6},{27,3},{31,7}} | collective-permute-start | bytes 196616 | tf_op jit(solution)/shard_map/ppermute | solution.py:385
  59.4 8.0 %collective-permute-start.12 = (f32[16,8,128]{2,1,0:T(8,128)S(1)}, f32[16,8,128]{2,1,0:T(8,128)S(1)}, u32[]{:S(2)}, u32[]{:S(2)}) collective-permute-start(f32[16,8,128]{2,1,0:T(8,128)S(1)} %fusion.12), channel_id=1, source_target_pairs={{16,0},{20,4},{24,8},{28,12},{17,1},{21,5},{25,9},{29,13},{18,2},{... | collective-permute-start | bytes 196616 | tf_op jit(solution)/shard_map/ppermute | solution.py:385
  60.7 7.1 %collective-permute-start.11 = (f32[19,8,128]{2,1,0:T(8,128)S(1)}, f32[19,8,128]{2,1,0:T(8,128)S(1)}, u32[]{:S(2)}, u32[]{:S(2)}) collective-permute-start(f32[19,8,128]{2,1,0:T(8,128)S(1)} %pad_maximum_fusion.1), channel_id=1, source_target_pairs={{8,0},{12,4},{16,8},{20,12},{24,16},{28,20},{9,1},{13,5},{17,9},{2... | collective-permute-start | bytes 233480 | tf_op jit(solution)/shard_map/ppermute | solution.py:385
  77.3 27.6 %collective-permute-start.15 = (bf16[512,256]{1,0:T(8,128)(2,1)S(1)}, bf16[512,256]{1,0:T(8,128)(2,1)S(1)}, u32[]{:S(2)}, u32[]{:S(2)}) collective-permute-start(bf16[512,256]{1,0:T(8,128)(2,1)S(1)} %get-tuple-element.13), channel_id=1, source_target_pairs={{0,1},{3,2},{4,5},{7,6},{8,9},{11,10},{12,13},{15,14},{16,17},{19,... | collective-permute-start | bytes 786440 | tf_op jit(solution)/shard_map/ppermute | solution.py:417
  84.9 22.7 %collective-permute-start.20 = (bf16[512,256]{1,0:T(8,128)(2,1)S(1)}, bf16[512,256]{1,0:T(8,128)(2,1)S(1)}, u32[]{:S(2)}, u32[]{:S(2)}) collective-permute-start(bf16[512,256]{1,0:T(8,128)(2,1)S(1)} %get-tuple-element.14), channel_id=1, source_target_pairs={{0,1},{3,2},{4,5},{7,6},{8,9},{11,10},{12,13},{15,14},{16,17},{19,... | collective-permute-start | bytes 786440 | tf_op jit(solution)/shard_map/ppermute | solution.py:417
  105.7 7.7 %collective-permute-start.16 = (bf16[512,256]{1,0:T(8,128)(2,1)S(1)}, bf16[512,256]{1,0:T(8,128)(2,1)S(1)}, u32[]{:S(2)}, u32[]{:S(2)}) collective-permute-start(bf16[512,256]{1,0:T(8,128)(2,1)S(1)} %fusion.6), channel_id=1, source_target_pairs={{0,1},{1,2},{4,5},{5,6},{8,9},{9,10},{12,13},{13,14},{16,17},{17,1... | collective-permute-start | bytes 786440 | tf_op jit(solution)/shard_map/ppermute | solution.py:435
  113.6 19.7 %collective-permute-start.17 = (bf16[512,256]{1,0:T(8,128)(2,1)S(1)}, bf16[512,256]{1,0:T(8,128)(2,1)S(1)}, u32[]{:S(2)}, u32[]{:S(2)}) collective-permute-start(bf16[512,256]{1,0:T(8,128)(2,1)S(1)} %get-tuple-element.19), channel_id=1, source_target_pairs={{0,1},{1,2},{2,3},{4,5},{5,6},{6,7},{8,9},{9,10},{10,11},{12,13},{... | collective-permute-start | bytes 786440 | tf_op jit(solution)/shard_map/ppermute | solution.py:435
  118.0 15.3 %collective-permute-start.19 = (bf16[512,256]{1,0:T(8,128)(2,1)S(1)}, bf16[512,256]{1,0:T(8,128)(2,1)S(1)}, u32[]{:S(2)}, u32[]{:S(2)}) collective-permute-start(bf16[512,256]{1,0:T(8,128)(2,1)S(1)} %get-tuple-element.21), channel_id=1, source_target_pairs={{1,0},{2,1},{3,2},{5,4},{6,5},{7,6},{9,8},{10,9},{11,10},{13,12},{... | collective-permute-start | bytes 786440 | tf_op jit(solution)/shard_map/ppermute | solution.py:436
  119.3 14.0 %collective-permute-start.23 = (bf16[512,256]{1,0:T(8,128)(2,1)S(1)}, bf16[512,256]{1,0:T(8,128)(2,1)S(1)}, u32[]{:S(2)}, u32[]{:S(2)}) collective-permute-start(bf16[512,256]{1,0:T(8,128)(2,1)S(1)} %get-tuple-element.20), channel_id=1, source_target_pairs={{2,1},{3,2},{6,5},{7,6},{10,9},{11,10},{14,13},{15,14},{18,17},{19... | collective-permute-start | bytes 786440 | tf_op jit(solution)/shard_map/ppermute | solution.py:436
  120.0 13.3 %collective-permute-start.21 = (bf16[512,256]{1,0:T(8,128)(2,1)S(1)}, bf16[512,256]{1,0:T(8,128)(2,1)S(1)}, u32[]{:S(2)}, u32[]{:S(2)}) collective-permute-start(bf16[512,256]{1,0:T(8,128)(2,1)S(1)} %get-tuple-element.20), channel_id=1, source_target_pairs={{0,1},{1,2},{4,5},{5,6},{8,9},{9,10},{12,13},{13,14},{16,17},{17,1... | collective-permute-start | bytes 786440 | tf_op jit(solution)/shard_map/ppermute | solution.py:435
  131.2 8.9 %collective-permute-start.27 = (f32[16,8,128]{2,1,0:T(8,128)S(1)}, f32[16,8,128]{2,1,0:T(8,128)S(1)}, u32[]{:S(2)}, u32[]{:S(2)}) collective-permute-start(f32[16,8,128]{2,1,0:T(8,128)S(1)} %add.93), channel_id=1, source_target_pairs={{0,16},{4,20},{8,24},{12,28},{16,0},{20,4},{24,8},{28,12},{1,17},{... | collective-permute-start | bytes 196616 | tf_op jit(solution)/shard_map/ppermute | solution.py:444
  133.6 10.0 %collective-permute-start.24 = (bf16[512,256]{1,0:T(8,128)(2,1)S(1)}, bf16[512,256]{1,0:T(8,128)(2,1)S(1)}, u32[]{:S(2)}, u32[]{:S(2)}) collective-permute-start(bf16[512,256]{1,0:T(8,128)(2,1)S(1)} %get-tuple-element.17), channel_id=1, source_target_pairs={{1,0},{2,1},{3,2},{5,4},{6,5},{7,6},{9,8},{10,9},{11,10},{13,12},{... | collective-permute-start | bytes 786440 | tf_op jit(solution)/shard_map/ppermute | solution.py:436
  134.9 9.9 %collective-permute-start.22 = (bf16[512,256]{1,0:T(8,128)(2,1)S(1)}, bf16[512,256]{1,0:T(8,128)(2,1)S(1)}, u32[]{:S(2)}, u32[]{:S(2)}) collective-permute-start(bf16[512,256]{1,0:T(8,128)(2,1)S(1)} %get-tuple-element.18), channel_id=1, source_target_pairs={{0,1},{1,2},{2,3},{4,5},{5,6},{6,7},{8,9},{9,10},{10,11},{12,13},{... | collective-permute-start | bytes 786440 | tf_op jit(solution)/shard_map/ppermute | solution.py:435
  (20 other events, 121.1 us)

commit v2 on v0

v2 whole, which is shorter than its diff:
```python
import functools

import jax
import jax.numpy as jnp
from jax import lax
from jax.experimental import pallas as pl
from jax.experimental.pallas import tpu as pltpu
from jax.sharding import PartitionSpec as P

LANES = 128
ROWS = 8
NT = (((1,), (1,)), ((), ()))
VMEM = pl.BlockSpec(memory_space=pltpu.VMEM)
HBM = pl.BlockSpec(memory_space=pltpu.HBM)
SMEM = pl.BlockSpec(memory_space=pltpu.SMEM)
GRANT = 46 * 2**20


def tile(token):
    return pl.ds(pl.multiple_of(token * ROWS, ROWS), ROWS)


def tree_sum(terms):
    terms = list(terms)
    while len(terms) > 1:
        paired = [a + b for a, b in zip(terms[::2], terms[1::2])]
        terms = paired + terms[2 * len(paired):]
    return terms[0]


def spread_kernel(features, saved, *outs):
    tokens, width = saved.shape
    if width < ROWS * LANES:
        for out in outs:
            out[...] = jnp.zeros(out.shape, out.dtype)
    for group in range(width // LANES):
        columns = pl.ds(group * LANES, LANES)
        rows = pl.ds(group, tokens, stride=ROWS)
        for which in range(3):
            outs[which][rows, :] = features[which, :, columns].astype(jnp.float32)
        outs[3][rows, :] = saved[:, columns].astype(jnp.float32)
        outs[4][rows, :] = (
            features[1, :, columns].astype(jnp.float32) * features[2, :, columns].astype(jnp.float32)
        )


def spread_acts(features, saved):
    flat = jax.ShapeDtypeStruct((saved.shape[0] * ROWS, LANES), jnp.float32)
    return pl.pallas_call(
        spread_kernel,
        in_specs=[VMEM] * 2,
        out_specs=[VMEM] * 5,
        out_shape=[flat] * 5,
        compiler_params=pltpu.CompilerParams(vmem_limit_bytes=GRANT),
        name="spread",
    )(features, saved)


def gate_kernel(at, has_acc, shards, count, plan, *refs):
    scal = [plan[at + i] for i in range(2 * shards)]
    acc = refs[0] if has_acc else None
    pieces = [piece[...] for piece in refs[has_acc:has_acc + count]]
    weight, out, buffer, sems = refs[has_acc + count:]
    width, deep = buffer.shape[2:]
    block = min(256, width)
    copies = []
    for shard in range(shards):
        columns = pl.ds(pl.multiple_of(scal[shard] * deep, deep), deep)
        copies.append(
            pltpu.make_async_copy(weight.at[:, columns], buffer.at[shard, 0], sems.at[shard])
        )
        copies[-1].start()
    if shards < count:
        pieces = [jnp.where(scal[1] > 0, *pieces)]
    elif shards > 1:
        pieces = [
            jnp.where(scal[shards + i] > 0, piece, jnp.zeros_like(piece))
            for i, piece in enumerate(pieces)
        ]
    for shard in range(shards):
        copies[shard].wait()
        for start in range(0, width, block):
            rows = pl.ds(start, block)
            value = lax.dot_general(
                pieces[shard], buffer[shard, 0, rows, :], NT, preferred_element_type=jnp.float32
            )
            if shard:
                value = value + out[:, rows]
            elif has_acc:
                value = value + acc[:, rows]
            out[:, rows] = value


def gate_step(plan, at, acc, pieces, weight, shards):
    tokens, deep = pieces[0].shape
    width = weight.shape[0]
    has_acc = acc is not None
    return pl.pallas_call(
        functools.partial(gate_kernel, at, has_acc, shards, len(pieces)),
        in_specs=[SMEM] + [VMEM] * (has_acc + len(pieces))
        + [HBM],
        out_specs=VMEM,
        out_shape=jax.ShapeDtypeStruct((tokens, width), jnp.float32),
        scratch_shapes=[
            pltpu.VMEM((shards, 1, width, deep), jnp.bfloat16),
            pltpu.SemaphoreType.DMA((shards,)),
        ],
        compiler_params=pltpu.CompilerParams(vmem_limit_bytes=GRANT),
        cost_estimate=pl.CostEstimate(
            flops=2 * tokens * width * deep * shards,
            bytes_accessed=2 * shards * width * deep,
            transcendentals=0,
        ),
        name="gate_step",
    )(plan, *([acc] if has_acc else []), *pieces, weight)


def close_kernel(at_plan, extra, plan, acc, piece, weight, query, saved, lam, gconv, gquery, packet, gate):
    tokens, width = acc.shape
    poles = lam.shape[0]
    block = min(256, width)
    if width < ROWS * LANES:
        gate[...] = jnp.zeros(gate.shape, gate.dtype)
    arrived = jnp.where(plan[at_plan] > 0, piece[...], jnp.zeros(piece.shape, piece.dtype))
    for start in range(0, width, block):
        columns = pl.ds(start, block)
        value = acc[:, columns] + lax.dot_general(
            arrived, weight[columns, :], NT, preferred_element_type=jnp.float32
        )
        for group in range(block // LANES):
            rows = pl.ds(start // LANES + group, tokens, stride=ROWS)
            gate[rows, :] = value[:, group * LANES:(group + 1) * LANES]

    def body(n, state):
        at = tile(tokens - 1 - n)
        grad = gate[at, :]
        conv = grad * query[at, :]
        gconv[at, :] = conv
        gquery[at, :] = grad * saved[at, :]
        return tuple(lam[m] * state[m] + conv for m in range(poles))

    zero = jnp.zeros((ROWS, LANES), jnp.float32)
    state = lax.fori_loop(0, tokens, body, (zero,) * poles, unroll=8)
    for m in range(poles):
        packet[m] = state[m]
    for row in range(extra - 1):
        packet[poles + row] = gconv[tile(row), :]
    for row in range(extra):
        packet[poles + extra - 1 + row] = gquery[tile(row), :]


def close_gate(plan, at, acc, piece, weight, query, saved, lam, extra):
    tokens, deep = piece.shape
    width = weight.shape[0]
    poles = lam.shape[0]
    flat = (tokens * ROWS, LANES)
    return pl.pallas_call(
        functools.partial(close_kernel, at, extra),
        in_specs=[SMEM] + [VMEM] * 6,
        out_specs=[VMEM] * 3,
        out_shape=[
            jax.ShapeDtypeStruct(flat, jnp.float32),
            jax.ShapeDtypeStruct(flat, jnp.float32),
            jax.ShapeDtypeStruct((poles + 2 * extra - 1, ROWS, LANES), jnp.float32),
        ],
        scratch_shapes=[pltpu.VMEM(flat, jnp.float32)],
        compiler_params=pltpu.CompilerParams(vmem_limit_bytes=GRANT),
        cost_estimate=pl.CostEstimate(
            flops=2 * tokens * width * deep, bytes_accessed=8 * width * deep, transcendentals=0
        ),
        name="close_gate",
    )(plan, acc, piece, weight, query, saved, lam)


def fold_kernel(plan, own, other, span, chip):
    poles = span.shape[0]
    first = plan[0] % 2 == 0
    for row in range(own.shape[0]):
        value = jnp.where(first, own[row], other[row])
        if row < poles:
            value = value + span[row] * jnp.where(first, other[row], own[row])
        chip[row] = value.astype(chip.dtype)


def fold(plan, own, other, span):
    return pl.pallas_call(
        fold_kernel,
        in_specs=[SMEM] + [VMEM] * 3,
        out_specs=VMEM,
        out_shape=jax.ShapeDtypeStruct(own.shape, jnp.bfloat16),
        compiler_params=pltpu.CompilerParams(vmem_limit_bytes=GRANT),
        name="fold",
    )(plan, own, other, span)


def scan_kernel(
    at_plan, taps, chips, plan, gconv, gquery, key_acts, value_acts, lam, rate, residues, filters, kv_halo,
    own, other, *refs,
):
    arrived = refs[:chips - 1]
    weight, proj, chunk, entering, passed, spread, buffer, sem = refs[chips - 1:]
    extra = taps - 1
    tokens, width = proj.shape[1:]
    poles = lam.shape[0]
    deep = buffer.shape[1]
    copy = pltpu.make_async_copy(
        weight.at[:, pl.ds(pl.multiple_of(plan[at_plan] * deep, deep), deep), :], buffer, sem
    )
    copy.start()

    block = plan[0]
    core, here = block % 2, block // 2
    for m in range(poles):
        beyond = []
        for mask in range(1, chips):
            there = here ^ mask
            distance = (2 * tokens * jnp.maximum(there - here - 1, 0)).astype(jnp.float32)
            term = jnp.exp(-rate[m] * distance) * arrived[mask - 1][m].astype(jnp.float32)
            beyond.append(jnp.where(there > here, term, jnp.zeros_like(term)))
        beyond = tree_sum(beyond)
        entering[m] = jnp.where(
            core == 0, other[m] + jnp.exp(-rate[m] * tokens) * beyond, beyond
        )
    halo = []
    for row in range(poles, poles + 2 * extra - 1):
        value = jnp.where(core == 0, other[row], jnp.zeros_like(other[row]))
        for mask in range(1, chips):
            there = here ^ mask
            value = jnp.where(
                (core == 1) & (there == here + 1), arrived[mask - 1][row].astype(jnp.float32), value
            )
        halo.append(value)

    state = [entering[m] for m in range(poles)]
    keys, values, queries = [], [], []
    for row in range(extra):
        if row:
            state = [(state[m] - halo[row - 1]) * jnp.exp(rate[m]) for m in range(poles)]
        product = tree_sum([residues[m] * state[m] for m in range(poles)])
        keys.append(product * kv_halo[1, row])
        values.append(product * kv_halo[0, row])
        queries.append(halo[extra - 1 + row])

    def body(n, carry):
        state, later = carry
        at = tile(tokens - 1 - n)
        conv = gconv[at, :]
        passed[at, :] = conv
        state = tuple(lam[m] * state[m] + conv for m in range(poles))
        product = tree_sum([residues[m] * state[m] for m in range(poles)])
        now = (gquery[at, :], product * value_acts[at, :], product * key_acts[at, :])
        for which in range(3):
            spread[which, at, :] = tree_sum(
                [filters[which, 0] * now[which]]
                + [filters[which, lag] * later[which][lag - 1] for lag in range(1, taps)]
            )
        return state, tuple((now[which],) + later[which][:-1] for which in range(3))

    carry = (
        tuple(entering[m] for m in range(poles)),
        (tuple(queries), tuple(keys), tuple(values)),
    )
    lax.fori_loop(0, tokens, body, carry, unroll=8)
    for which in range(3):
        for group in range(width // LANES):
            proj[which, :, pl.ds(group * LANES, LANES)] = spread[
                which, pl.ds(group, tokens, stride=ROWS), :
            ].astype(jnp.bfloat16)
    copy.wait()
    project_rows(buffer, proj, chunk)


def project_rows(weight, proj, out):
    rows = out.shape[0]
    block = min(256, rows)
    for start in range(0, rows, block):
        value = tree_sum([
            lax.dot_general(
                weight[which, pl.ds(start, block), :], proj[which],
                NT, preferred_element_type=jnp.float32,
            )
            for which in range(3)
        ])
        out[pl.ds(start, block), :] = value.astype(out.dtype)


def scan_block(plan, at, gconv, gquery, keys, values, lam, rate, residues, filters, kv_halo, own, other,
               arrived, weight, deep, width):
    tokens = gconv.shape[0] // ROWS
    taps = filters.shape[1]
    return pl.pallas_call(
        functools.partial(scan_kernel, at, taps, len(arrived) + 1),
        in_specs=[SMEM] + [VMEM] * (11 + len(arrived))
        + [HBM],
        out_specs=[VMEM] * 4,
        out_shape=[
            jax.ShapeDtypeStruct((3, tokens, width), jnp.bfloat16),
            jax.ShapeDtypeStruct((deep, tokens), jnp.bfloat16),
            jax.ShapeDtypeStruct(lam.shape, jnp.float32),
            jax.ShapeDtypeStruct(gconv.shape, jnp.float32),
        ],
        scratch_shapes=[
            pltpu.VMEM((3, tokens * ROWS, LANES), jnp.float32),
            pltpu.VMEM((3, deep, width), jnp.bfloat16),
            pltpu.SemaphoreType.DMA,
        ],
        compiler_params=pltpu.CompilerParams(vmem_limit_bytes=GRANT),
        cost_estimate=pl.CostEstimate(
            flops=6 * tokens * width * deep, bytes_accessed=16 * width * deep, transcendentals=0
        ),
        name="scan",
    )(plan, gconv, gquery, keys, values, lam, rate, residues, filters, kv_halo, own, other, *arrived,
      weight)


def total_kernel(gconv, product, lam, entering, total):
    tokens = gconv.shape[0] // ROWS
    poles = lam.shape[0]

    def body(n, carry):
        state, sums = carry
        at = tile(tokens - 1 - n)
        conv, both = gconv[at, :], product[at, :]
        state = tuple(lam[m] * state[m] + conv for m in range(poles))
        return state, tuple(sums[m] + both * state[m] for m in range(poles))

    state = tuple(entering[m] for m in range(poles))
    zero = jnp.zeros((ROWS, LANES), jnp.float32)
    _, sums = lax.fori_loop(0, tokens, body, (state, (zero,) * poles), unroll=8)
    for m in range(poles):
        total[m] = sums[m]


def residue_total(gconv, product, lam, entering):
    return pl.pallas_call(
        total_kernel,
        in_specs=[VMEM] * 4,
        out_specs=VMEM,
        out_shape=jax.ShapeDtypeStruct(lam.shape, jnp.float32),
        compiler_params=pltpu.CompilerParams(vmem_limit_bytes=GRANT),
        cost_estimate=pl.CostEstimate(
            flops=4 * gconv.size * lam.shape[0], bytes_accessed=8 * gconv.size, transcendentals=0
        ),
        name="residue_total",
    )(gconv, product, lam, entering)


def project_kernel(at, count, plan, proj, weight, *refs):
    outs, buffer, sems = refs[:count], refs[count], refs[count + 1]
    deep = buffer.shape[2]
    copies = [
        pltpu.make_async_copy(
            weight.at[:, pl.ds(pl.multiple_of(plan[at + i] * deep, deep), deep), :],
            buffer.at[i], sems.at[i],
        )
        for i in range(count)
    ]
    for copy in copies:
        copy.start()
    for i in range(count):
        copies[i].wait()
        project_rows(buffer.at[i], proj, outs[i])


def project(plan, at, count, proj, weight, deep):
    _, tokens, width = proj.shape
    return pl.pallas_call(
        functools.partial(project_kernel, at, count),
        in_specs=[SMEM, VMEM, HBM],
        out_specs=[VMEM] * count,
        out_shape=[jax.ShapeDtypeStruct((deep, tokens), jnp.bfloat16)] * count,
        scratch_shapes=[
            pltpu.VMEM((count, 3, deep, width), jnp.bfloat16),
            pltpu.SemaphoreType.DMA((count,)),
        ],
        compiler_params=pltpu.CompilerParams(vmem_limit_bytes=GRANT),
        cost_estimate=pl.CostEstimate(
            flops=6 * tokens * width * deep * count,
            bytes_accessed=6 * width * deep * count,
            transcendentals=0,
        ),
        name="project",
    )(plan, proj, weight)


def scalars(*values):
    return jnp.stack([jnp.asarray(value, jnp.int32) for value in values])


def tiles(array):
    lead = array.shape[:-1]
    groups = array.shape[-1] // LANES
    array = array.reshape(lead + (groups, LANES))
    if groups < ROWS:
        array = jnp.pad(array, [(0, 0)] * len(lead) + [(0, ROWS - groups), (0, 0)])
    return array


def swap_even(value, count):
    return lax.ppermute(value, "chan", [(i, i ^ 1) for i in range(count)])


def swap_odd(value, count, blocks):
    pairs = []
    for block in range(blocks):
        for i in range(count):
            other = i + 1 if i % 2 else i - 1
            if 0 <= other < count:
                pairs.append((block * count + i, block * count + other))
            else:
                pairs.append((block * count + i, (block ^ 1) * count + i))
    return lax.ppermute(value, ("ctx", "chan"), pairs)


def swap_ctx(value, mask, blocks):
    return lax.ppermute(value, "ctx", [(i, i ^ mask) for i in range(blocks)])


def tie(*values):
    return lax.optimization_barrier(values)


def local(features, saved_conv, grad_out, out_weight, in_weight, short_taps, residues, decay_time):
    f32, bf16 = jnp.float32, jnp.bfloat16
    tokens, width = saved_conv.shape
    taps = short_taps.shape[1]
    extra = taps - 1
    poles = residues.shape[0]
    count = lax.axis_size("chan")
    me = lax.axis_index("chan")
    even = me % 2 == 0
    deep = in_weight.shape[1] // count
    blocks = lax.axis_size("ctx")
    block = lax.axis_index("ctx")

    rate = tiles(1.0 / decay_time)
    lam = jnp.exp(-rate)
    span = jnp.exp(-rate * tokens)
    res = tiles(residues)
    filters = tiles(short_taps)

    def shared(phase):
        far = count - phase
        as_even = jnp.where(me < phase, me + far, jnp.maximum(me - far + 1, 0))
        as_odd = jnp.where(me >= far, me - far, jnp.minimum(me + far - 1, count - 1))
        return jnp.where(even, as_even, as_odd)

    def reached(phase, along):
        right = jnp.minimum(me + count - phase, count - 1)
        left = jnp.maximum(me - (count - phase), 0)
        return jnp.where(along, right, left)

    def shards(phase):
        above, below = me + phase, me - phase
        high, low = jnp.minimum(above, count - 1), jnp.maximum(below, 0)
        at_even, at_odd = jnp.where(even, high, low), jnp.where(even, low, high)
        even_ok = jnp.where(even, above < count, below >= 0)
        odd_ok = jnp.where(even, below >= 0, above < count)
        if 2 * phase == count:
            return [jnp.where(even_ok, at_even, at_odd), even_ok]
        return [at_even, at_odd, even_ok, odd_ok]

    edge = (me == 0) | (me == count - 1)
    plan, places = [block, edge], {}

    def planned(name, values):
        places[name] = len(plan)
        plan.extend(values)

    planned("own", [me, 1])
    for phase in range(1, count - 1):
        planned(("gate", phase), shards(phase))
    planned("first", [shared(1)])
    chunks = []
    for phase in range(2, count):
        if 2 * phase <= count:
            chunks.append(shared(phase))
        else:
            chunks.append(reached(phase, even))
            if phase + 1 < count:
                chunks.append(reached(phase + 1, ~even))
    chunks.append(me)
    planned("chunks", chunks)
    plan = scalars(*plan)

    evens = swap_even(grad_out, count)
    odds = swap_odd(grad_out, count, blocks)
    query, keys, values, saved, product = spread_acts(features, saved_conv)
    acc = gate_step(plan, places["own"], None, [grad_out], out_weight, 1)
    kv_halo = tiles(features[1:3, :extra].astype(f32))
    kv_halo = lax.ppermute(kv_halo, "ctx", [(i, (i - 1) % blocks) for i in range(blocks)])
    last = jnp.where(even, jnp.minimum(count - 1, me + count - 1), jnp.maximum(me - count + 1, 0))
    last_weight = lax.dynamic_slice(out_weight, (0, last * width), (width, width))
    (
        evens, odds, acc, plan, query, keys, values, saved, product, rate, lam, span, res, filters
    ) = tie(evens, odds, acc, plan, query, keys, values, saved, product, rate, lam, span, res, filters)
    for phase in range(1, count - 1):
        next_evens = swap_even(odds, count)
        next_odds = swap_odd(evens, count, blocks)
        acc = gate_step(
            plan, places["gate", phase], acc, [evens, odds], out_weight,
            1 if 2 * phase == count else 2,
        )
        evens, odds = next_evens, next_odds
        if phase == 1:
            evens, odds, acc, kv_halo, last_weight = tie(evens, odds, acc, kv_halo, last_weight)
        elif phase < count - 2:
            evens, odds, acc = tie(evens, odds, acc)
    gconv, gquery, packet = close_gate(plan, 1, acc, evens, last_weight, query, saved, lam, extra)

    other = swap_ctx(packet, 1, blocks)
    chip = fold(plan, packet, other, span)
    arrived = [swap_ctx(chip, 2 * mask, blocks) for mask in range(1, blocks // 2)]

    def added(*parts):
        return sum(value.astype(f32) for value in parts if value is not None).astype(bf16)

    proj, part, entering, gconv = scan_block(
        plan, places["first"], gconv, gquery, keys, values, lam, rate, res, filters, kv_halo,
        packet, other, arrived, in_weight, deep, width,
    )
    for_even, for_odd = {1: part}, {2: part}
    parts = list(project(plan, places["chunks"], len(chunks), proj, in_weight, deep))
    evens, odds = swap_even(part, count), None
    evens, gconv, *parts = tie(evens, gconv, *parts)
    for phase in range(2, count):
        for_even[phase] = parts.pop(0)
        if 2 * phase <= count:
            for_odd[phase + 1] = for_even[phase]
        elif phase + 1 < count:
            for_odd[phase + 1] = parts.pop(0)
    total = residue_total(gconv, product, lam, entering)
    for phase in range(2, count):
        if odds is not None:
            odds = jnp.where(edge, jnp.zeros_like(odds), odds)
        next_evens = swap_even(added(for_even[phase], odds), count)
        odds = swap_odd(added(for_odd[phase], evens), count, blocks)
        evens = next_evens
    odds = jnp.where(edge, jnp.zeros_like(odds), odds)
    grad_input = added(parts.pop(0), evens, odds)

    mask = 1
    while mask < blocks:
        total = total + swap_ctx(total, mask, blocks)
        mask *= 2
    grad_residue = total[:, :width // LANES].reshape(poles, width) / (tokens * blocks)
    return grad_input, grad_residue


def solution(mesh):
    return jax.shard_map(
        local,
        mesh=mesh,
        in_specs=(
            P(None, "ctx", "chan"),
            P("ctx", "chan"),
            P("ctx", "chan"),
            P("chan", None),
            P(None, None, "chan"),
            P(None, None, "chan"),
            P(None, "chan"),
            P(None, "chan"),
        ),
        out_specs=(P("chan", "ctx"), P(None, "chan")),
        check_vma=False,
    )
```

time: 300 us -> 108 us (0.36)
  waiting for transfers between devices: 142 us -> 26.2 us
  other arithmetic: 68.2 us -> 3.17 us
  matrix products: 35.2 us -> 0 us
  Pallas kernels: 0 us -> 33.2 us
  starting transfers between devices: 10.5 us -> 32.8 us
  local copies, waits for them, and re-layouts: 29.4 us -> 10.6 us
  between operations: 14 us -> 0.9 us
    psum x1 -> x0, waiting for transfers between devices: 47.6 us -> none  [local(): lax.psum(partial_res, 'ctx') / (length * lax.axis_size('ctx'))]
    reduce_scatter x1 -> x0, waiting for transfers between devices: 44.2 us -> none  [local(): lax.psum_scatter(jnp.einsum('jdc,jtc->dt', in_weight, grad_proj, preferre...]
    dot_general x3 -> x0, matrix products: 35.2 us -> none  [the longest x1 14.7 us: local(): jnp.einsum('st,btx->bsx', upper, weighted.reshape(blocks, span_rows, pole...]
    pallas_call x0 -> x9, Pallas kernels: none -> 33.2 us  [the longest x3 10.7 us: gate_step(): pl.pallas_call(functools.partial(gate_kernel, at, has_acc, shards, len(pi...]
    reduce_sum x3 -> x0, other arithmetic: 26.2 us -> none  [the longest x1 14.7 us: local(): jnp.sum(product.reshape(blocks, span_rows, 1, width) * state, axis=(0, 1))]
    exp x3 -> x1, other arithmetic: 26 us -> 0.03 us  [local(): span = jnp.exp(-rate * tokens)]
    ppermute x8 -> x18, starting transfers between devices: 10.3 us -> 32.8 us  [the longest x6 23.3 us: swap_even(): return lax.ppermute(value, 'chan', [(i, i ^ 1) for i in range(count)])]
    all_gather x1 -> x0, waiting for transfers between devices: 22.3 us -> none  [local(): everything = lax.all_gather(grad_out, 'chan', axis=1, tiled=True)]
  transfers between devices with their start and end apart: 11 -> 18, of which waited for: 10 -> 11; matrix products, arithmetic and copies ran while one was open for 20% -> 6% of each run, Pallas kernels for 0% -> 22%
where the time goes in v2:
time: 108 us; the launch traced here: 107 us
  Pallas kernels  33.2 us (31%)
  starting transfers between devices  32.8 us (30%)
  waiting for transfers between devices  26.2 us (24%)
  local copies, waits for them, and re-layouts  10.6 us (10%)
  other arithmetic  3.17 us (3%)
    ppermute x6, starting transfers between devices, swap_even(): return lax.ppermute(value, 'chan', [(i, i ^ 1) for i in range(count)])  23.3 us
    ppermute x6, waiting for transfers between devices, swap_even(): return lax.ppermute(value, 'chan', [(i, i ^ 1) for i in range(count)])  14.2 us
    ppermute x7, waiting for transfers between devices, swap_ctx(): return lax.ppermute(value, 'ctx', [(i, i ^ mask) for i in range(blocks)])  11.9 us
    pallas_call x3, Pallas kernels, gate_step(): pl.pallas_call(functools.partial(gate_kernel, at, has_acc, shards, len(pi...  10.7 us
    pallas_call x1, Pallas kernels, project(): pl.pallas_call(functools.partial(project_kernel, at, count), in_specs=[SM...  8.84 us
    unnamed x21, local copies, waits for them, and re-layouts  7.94 us
    ppermute x7, starting transfers between devices, swap_ctx(): return lax.ppermute(value, 'ctx', [(i, i ^ mask) for i in range(blocks)])  6.59 us
    pallas_call x1, Pallas kernels, scan_block(): pl.pallas_call(functools.partial(scan_kernel, at, taps, len(arrived) + 1)...  6.54 us
  transfers between devices with their start and end apart: 18, of which 11 were waited for; matrix products, arithmetic and copies ran while one was open for 6% of the time, Pallas kernels for 22%

profile of v2, /device:TPU:0, one launch (start us, length us, event | category | flops | bytes accessed | tf_op | source)
XLA Modules:
  0.0 106.9 jit_solution(18199797082637289276)
XLA Ops:
  0.6 3.1 %collective-permute-start = (bf16[256,1024]{1,0:T(8,128)(2,1)}, bf16[256,1024]{1,0:T(8,128)(2,1)}, u32[]{:S(2)}, u32[]{:S(2)}) collective-permute-start(bf16[256,1024]{1,0:T(8,128)(2,1)} %refs_0_.1), channel_id=1, source_target_pairs={{0,1},{1,0},{2,3},{3,2},{4,5},{5,4},{6,7},{7,6},{8,9},{9,8},{10,11... | collective-permute-start | bytes 1572872 | tf_op jit(solution)/shard_map/ppermute | solution.py:400
  14.4 2.9 %gate_step.3.refs_0_ = f32[256,1024]{1,0:T(8,128)S(1)} custom-call(s32[14]{0:T(128)S(1)} %stack.65.plan, bf16[256,1024]{1,0:T(8,128)(2,1)S(1)} %copy-done.7, bf16[1024,4096]{1,0:T(8,128)(2,1)} %refs_3_.4), custom_call_target="tpu_custom_call" | custom-call | flops 536870912 | bytes 2097152 | tf_op jit(solution)/shard_map/gate_step/pallas_call | solution.py:98
  17.3 3.2 %collective-permute-start.2 = (bf16[256,1024]{1,0:T(8,128)(2,1)}, bf16[256,1024]{1,0:T(8,128)(2,1)}, u32[]{:S(2)}, u32[]{:S(2)}) collective-permute-start(bf16[256,1024]{1,0:T(8,128)(2,1)} %collective-permute-done.1.refs_2_), channel_id=1, source_target_pairs={{0,1},{1,0},{2,3},{3,2},{4,5},{5,4},{6,7},{7,6},{8,9},{9,8},{10,11... | collective-permute-start | bytes 1572872 | tf_op jit(solution)/shard_map/ppermute | solution.py:400
  21.3 2.8 %collective-permute-start.4 = (f32[2,2,8,128]{3,2,1,0:T(8,128)S(1)}, f32[2,2,8,128]{3,2,1,0:T(8,128)S(1)}, u32[]{:S(2)}, u32[]{:S(2)}) collective-permute-start(f32[2,2,8,128]{3,2,1,0:T(8,128)S(1)} %reshape.32), channel_id=1, source_target_pairs={{0,28},{4,0},{8,4},{12,8},{16,12},{20,16},{24,20},{28,24},{1,29},{... | collective-permute-start | bytes 49160 | tf_op jit(solution)/shard_map/ppermute | solution.py:491
  24.1 1.8 %constant_dynamic-slice_fusion.weight = bf16[1024,1024]{1,0:T(8,128)(2,1)S(1)} fusion(bf16[1024,4096]{1,0:T(8,128)(2,1)} %refs_3_.4, s32[]{:T(128)S(6)} %select_n.85), kind=kLoop, calls=%fused_computation.10 | loop fusion | bytes 4194308 | tf_op jit(solution)/shard_map/dynamic_slice | solution.py:493
  25.9 4.3 %gate_step.4.refs_0_ = f32[256,1024]{1,0:T(8,128)S(1)} custom-call(s32[14]{0:T(128)S(1)} %stack.65.plan, f32[256,1024]{1,0:T(8,128)S(1)} %gate_step.3.refs_0_, bf16[256,1024]{1,0:T(8,128)(2,1)} %collective-permute-done.refs_1_, bf16[256,1024]{1,0:T(8,128)(2,1)} %collective-permute-done.1.refs_2_, bf16[1024,4096]{1,0:T(8,128)(2,1)} %refs_3_.4), custom_call_target="tpu_custom_call" | custom-call | flops 1073741824 | bytes 4194304 | tf_op jit(solution)/shard_map/gate_step/pallas_call | solution.py:98
  30.2 2.0 %collective-permute-done.2.refs_1_ = bf16[256,1024]{1,0:T(8,128)(2,1)} collective-permute-done((bf16[256,1024]{1,0:T(8,128)(2,1)}, bf16[256,1024]{1,0:T(8,128)(2,1)}, u32[]{:S(2)}, u32[]{:S(2)}) %collective-permute-start.2) | collective-permute-done | bytes 524320 | tf_op jit(solution)/shard_map/ppermute | solution.py:400
  32.2 1.8 %collective-permute-start.5 = (bf16[256,1024]{1,0:T(8,128)(2,1)}, bf16[256,1024]{1,0:T(8,128)(2,1)S(1)}, u32[]{:S(2)}, u32[]{:S(2)}) collective-permute-start(bf16[256,1024]{1,0:T(8,128)(2,1)} %collective-permute-done.3.refs_2_), channel_id=1, source_target_pairs={{0,1},{1,0},{2,3},{3,2},{4,5},{5,4},{6,7},{7,6},{8,9},{9,8},{10,11... | collective-permute-start | bytes 1572872 | tf_op jit(solution)/shard_map/ppermute | solution.py:400
  34.0 3.6 %gate_step.5.acc = f32[256,1024]{1,0:T(8,128)S(1)} custom-call(s32[14]{0:T(128)S(1)} %stack.65.plan, f32[256,1024]{1,0:T(8,128)S(1)} %gate_step.4.refs_0_, bf16[256,1024]{1,0:T(8,128)(2,1)} %collective-permute-done.2.refs_1_, bf16[256,1024]{1,0:T(8,128)(2,1)} %collective-permute-done.3.refs_2_, bf16[1024,4096]{1,0:T(8,128)(2,1)} %refs_3_.4), custom_call_target="tpu_custom_call" | custom-call | flops 536870912 | bytes 2097152 | tf_op jit(solution)/shard_map/gate_step/pallas_call | solution.py:98
  37.6 7.3 %collective-permute-done.5.piece = bf16[256,1024]{1,0:T(8,128)(2,1)S(1)} collective-permute-done((bf16[256,1024]{1,0:T(8,128)(2,1)}, bf16[256,1024]{1,0:T(8,128)(2,1)S(1)}, u32[]{:S(2)}, u32[]{:S(2)}) %collective-permute-start.5) | collective-permute-done | bytes 524320 | tf_op jit(solution)/shard_map/ppermute | solution.py:400
  44.9 2.7 %close_gate.1 = (f32[2048,128]{1,0:T(8,128)S(1)}, f32[2048,128]{1,0:T(8,128)S(1)}, f32[19,8,128]{2,1,0:T(8,128)S(1)}) custom-call(s32[14]{0:T(128)S(1)} %stack.65.plan, f32[256,1024]{1,0:T(8,128)S(1)} %gate_step.5.acc, bf16[256,1024]{1,0:T(8,128)(2,1)S(1)} %collective-permute-done.5.piece, bf16[1024,1024]{1,0:T(8,128)(2,1)S(1)} %constant_dynamic-slice_fusion.weight, ...), custom_call_target="tpu_custom_call" | custom-call | flops 536870912 | bytes 8388608 | tf_op jit(solution)/shard_map/close_gate/pallas_call | solution.py:157
  49.5 2.5 %collective-permute-start.9 = (bf16[19,8,128]{2,1,0:T(8,128)(2,1)S(1)}, bf16[19,8,128]{2,1,0:T(8,128)(2,1)S(1)}, u32[]{:S(2)}, u32[]{:S(2)}) collective-permute-start(bf16[19,8,128]{2,1,0:T(8,128)(2,1)S(1)} %fold.1), channel_id=1, source_target_pairs={{0,24},{4,28},{8,16},{12,20},{16,8},{20,12},{24,0},{28,4},{1,25},{... | collective-permute-start | bytes 116744 | tf_op jit(solution)/shard_map/ppermute | solution.py:416
  54.5 1.5 %collective-permute-done.8.refs_1_ = bf16[19,8,128]{2,1,0:T(8,128)(2,1)S(1)} collective-permute-done((bf16[19,8,128]{2,1,0:T(8,128)(2,1)S(1)}, bf16[19,8,128]{2,1,0:T(8,128)(2,1)S(1)}, u32[]{:S(2)}, u32[]{:S(2)}) %collective-permute-start.8) | collective-permute-done | bytes 38944 | tf_op jit(solution)/shard_map/ppermute | solution.py:416
  56.5 6.5 %scan.1 = (bf16[3,256,1024]{2,1,0:T(8,128)(2,1)S(1)}, bf16[1024,256]{1,0:T(8,128)(2,1)S(1)}, f32[16,8,128]{2,1,0:T(8,128)S(1)}, f32[2048,128]{1,0:T(8,128)S(1)}) custom-call(s32[14]{0:T(128)S(1)} %stack.65.plan, f32[2048,128]{1,0:T(8,128)S(1)} %get-tuple-element.57.gconv, f32[2048,128]{1,0:T(8,128)S(1)} %get-tuple-element.58.gquery, ...), custom_call_target="tpu_custom_call" | custom-call | flops 1610612736 | bytes 16777216 | tf_op jit(solution)/shard_map/scan/pallas_call | solution.py:291
  63.1 1.6 %collective-permute-start.10 = (bf16[1024,256]{1,0:T(8,128)(2,1)S(1)}, bf16[1024,256]{1,0:T(8,128)(2,1)S(1)}, u32[]{:S(2)}, u32[]{:S(2)}) collective-permute-start(bf16[1024,256]{1,0:T(8,128)(2,1)S(1)} %get-tuple-element.67), channel_id=1, source_target_pairs={{0,1},{1,0},{2,3},{3,2},{4,5},{5,4},{6,7},{7,6},{8,9},{9,8},{10,11... | collective-permute-start | bytes 1572872 | tf_op jit(solution)/shard_map/ppermute | solution.py:400
  64.6 8.8 %project.1 = (bf16[1024,256]{1,0:T(8,128)(2,1)S(1)}, bf16[1024,256]{1,0:T(8,128)(2,1)S(1)}, bf16[1024,256]{1,0:T(8,128)(2,1)S(1)}) custom-call(s32[14]{0:T(128)S(1)} %stack.65.plan, bf16[3,256,1024]{2,1,0:T(8,128)(2,1)S(1)} %get-tuple-element.69.proj, bf16[3,4096,1024]{2,1,0:T(8,128)(2,1)} %weight.1), custom_call_target="tpu_custom_call" | custom-call | flops 4831838208 | bytes 18874368 | tf_op jit(solution)/shard_map/project/pallas_call | solution.py:367
  73.5 1.9 %collective-permute-done.10 = bf16[1024,256]{1,0:T(8,128)(2,1)S(1)} collective-permute-done((bf16[1024,256]{1,0:T(8,128)(2,1)S(1)}, bf16[1024,256]{1,0:T(8,128)(2,1)S(1)}, u32[]{:S(2)}, u32[]{:S(2)}) %collective-permute-start.10) | collective-permute-done | bytes 524320 | tf_op jit(solution)/shard_map/ppermute | solution.py:400
  75.6 3.9 %collective-permute-start.13 = (bf16[1024,256]{1,0:T(8,128)(2,1)S(1)}, bf16[1024,256]{1,0:T(8,128)(2,1)S(1)}, u32[]{:S(2)}, u32[]{:S(2)}) collective-permute-start(bf16[1024,256]{1,0:T(8,128)(2,1)S(1)} %get-tuple-element.76), channel_id=1, source_target_pairs={{0,1},{1,0},{2,3},{3,2},{4,5},{5,4},{6,7},{7,6},{8,9},{9,8},{10,11... | collective-permute-start | bytes 1572872 | tf_op jit(solution)/shard_map/ppermute | solution.py:400
  79.7 9.7 %collective-permute-start.12 = (bf16[1024,256]{1,0:T(8,128)(2,1)S(1)}, bf16[1024,256]{1,0:T(8,128)(2,1)S(1)}, u32[]{:S(2)}, u32[]{:S(2)}) collective-permute-start(bf16[1024,256]{1,0:T(8,128)(2,1)S(1)} %add_convert_fusion.2), channel_id=1, source_target_pairs={{0,1},{1,0},{2,3},{3,2},{4,5},{5,4},{6,7},{7,6},{8,9},{9,8},{10,11... | collective-permute-start | bytes 1572872 | tf_op jit(solution)/shard_map/ppermute | solution.py:400
  89.4 3.0 %collective-permute-done.13 = bf16[1024,256]{1,0:T(8,128)(2,1)S(1)} collective-permute-done((bf16[1024,256]{1,0:T(8,128)(2,1)S(1)}, bf16[1024,256]{1,0:T(8,128)(2,1)S(1)}, u32[]{:S(2)}, u32[]{:S(2)}) %collective-permute-start.13) | collective-permute-done | bytes 524320 | tf_op jit(solution)/shard_map/ppermute | solution.py:400
  92.6 2.4 %residue_total.1 = f32[16,8,128]{2,1,0:T(8,128)S(1)} custom-call(f32[2048,128]{1,0:T(8,128)S(1)} %get-tuple-element.77.gconv, f32[2048,128]{1,0:T(8,128)S(1)} %copy-done.2, f32[16,8,128]{2,1,0:T(8,128)S(1)} %get-tuple-element.56.lam, f32[16,8,128]{2,1,0:T(8,128)S(1)} %get-tuple-element.79.entering), custom_call_target="tpu_custom_call" | custom-call | flops 16777216 | bytes 2097152 | tf_op jit(solution)/shard_map/residue_total/pallas_call | solution.py:335
  97.1 3.7 %collective-permute-done.16 = f32[16,8,128]{2,1,0:T(8,128)S(1)} collective-permute-done((f32[16,8,128]{2,1,0:T(8,128)S(1)}, f32[16,8,128]{2,1,0:T(8,128)S(1)}, u32[]{:S(2)}, u32[]{:S(2)}) %collective-permute-start.16) | collective-permute-done | bytes 65568 | tf_op jit(solution)/shard_map/ppermute | solution.py:416
  100.9 1.7 %collective-permute-start.17 = (f32[16,8,128]{2,1,0:T(8,128)S(1)}, f32[16,8,128]{2,1,0:T(8,128)S(1)}, u32[]{:S(2)}, u32[]{:S(2)}) collective-permute-start(f32[16,8,128]{2,1,0:T(8,128)S(1)} %add.81), channel_id=1, source_target_pairs={{0,16},{4,20},{8,24},{12,28},{16,0},{20,4},{24,8},{28,12},{1,17},{... | collective-permute-start | bytes 196616 | tf_op jit(solution)/shard_map/ppermute | solution.py:416
  102.6 2.6 %collective-permute-done.17 = f32[16,8,128]{2,1,0:T(8,128)S(1)} collective-permute-done((f32[16,8,128]{2,1,0:T(8,128)S(1)}, f32[16,8,128]{2,1,0:T(8,128)S(1)}, u32[]{:S(2)}, u32[]{:S(2)}) %collective-permute-start.17) | collective-permute-done | bytes 65568 | tf_op jit(solution)/shard_map/ppermute | solution.py:416
  (56 shorter events, 20.7 us)
Async XLA Ops:
  0.6 16.7 %collective-permute-start = (bf16[256,1024]{1,0:T(8,128)(2,1)}, bf16[256,1024]{1,0:T(8,128)(2,1)}, u32[]{:S(2)}, u32[]{:S(2)}) collective-permute-start(bf16[256,1024]{1,0:T(8,128)(2,1)} %refs_0_.1), channel_id=1, source_target_pairs={{0,1},{1,0},{2,3},{3,2},{4,5},{5,4},{6,7},{7,6},{8,9},{9,8},{10,11... | collective-permute-start | bytes 1572872 | tf_op jit(solution)/shard_map/ppermute | solution.py:400
  3.7 13.6 %collective-permute-start.1 = (bf16[256,1024]{1,0:T(8,128)(2,1)}, bf16[256,1024]{1,0:T(8,128)(2,1)}, u32[]{:S(2)}, u32[]{:S(2)}) collective-permute-start(bf16[256,1024]{1,0:T(8,128)(2,1)} %refs_0_.1), channel_id=1, source_target_pairs={{0,4},{1,2},{2,1},{3,7},{4,0},{5,6},{6,5},{7,3},{8,12},{9,10},{10,... | collective-permute-start | bytes 1572872 | tf_op jit(solution)/shard_map/ppermute | solution.py:412
  6.3 1.4 %copy-start = (bf16[3,256,1024]{2,1,0:T(8,128)(2,1)S(1)}, bf16[3,256,1024]{2,1,0:T(8,128)(2,1)}, u32[]{:S(2)}) copy-start(bf16[3,256,1024]{2,1,0:T(8,128)(2,1)} %features.1) | copy-start | bytes 4718596
  7.7 1.0 copy-start.8
  13.3 1.0 copy-start.7
  17.3 14.9 %collective-permute-start.2 = (bf16[256,1024]{1,0:T(8,128)(2,1)}, bf16[256,1024]{1,0:T(8,128)(2,1)}, u32[]{:S(2)}, u32[]{:S(2)}) collective-permute-start(bf16[256,1024]{1,0:T(8,128)(2,1)} %collective-permute-done.1.refs_2_), channel_id=1, source_target_pairs={{0,1},{1,0},{2,3},{3,2},{4,5},{5,4},{6,7},{7,6},{8,9},{9,8},{10,11... | collective-permute-start | bytes 1572872 | tf_op jit(solution)/shard_map/ppermute | solution.py:400
  20.5 11.7 %collective-permute-start.3 = (bf16[256,1024]{1,0:T(8,128)(2,1)}, bf16[256,1024]{1,0:T(8,128)(2,1)}, u32[]{:S(2)}, u32[]{:S(2)}) collective-permute-start(bf16[256,1024]{1,0:T(8,128)(2,1)} %collective-permute-done.refs_1_), channel_id=1, source_target_pairs={{0,4},{1,2},{2,1},{3,7},{4,0},{5,6},{6,5},{7,3},{8,12},{9,10},{10,... | collective-permute-start | bytes 1572872 | tf_op jit(solution)/shard_map/ppermute | solution.py:412
  21.3 8.9 %collective-permute-start.4 = (f32[2,2,8,128]{3,2,1,0:T(8,128)S(1)}, f32[2,2,8,128]{3,2,1,0:T(8,128)S(1)}, u32[]{:S(2)}, u32[]{:S(2)}) collective-permute-start(f32[2,2,8,128]{3,2,1,0:T(8,128)S(1)} %reshape.32), channel_id=1, source_target_pairs={{0,28},{4,0},{8,4},{12,8},{16,12},{20,16},{24,20},{28,24},{1,29},{... | collective-permute-start | bytes 49160 | tf_op jit(solution)/shard_map/ppermute | solution.py:491
  30.2 14.8 %copy-start.4 = (f32[2048,128]{1,0:T(8,128)S(1)}, f32[2048,128]{1,0:T(8,128)}, u32[]{:S(2)}) copy-start(f32[2048,128]{1,0:T(8,128)} %copy-done.3) | copy-start | bytes 3145732
  30.2 14.7 %copy-start.6 = (f32[2048,128]{1,0:T(8,128)S(1)}, f32[2048,128]{1,0:T(8,128)}, u32[]{:S(2)}) copy-start(f32[2048,128]{1,0:T(8,128)} %copy-done.5) | copy-start | bytes 3145732
  32.2 12.7 %collective-permute-start.5 = (bf16[256,1024]{1,0:T(8,128)(2,1)}, bf16[256,1024]{1,0:T(8,128)(2,1)S(1)}, u32[]{:S(2)}, u32[]{:S(2)}) collective-permute-start(bf16[256,1024]{1,0:T(8,128)(2,1)} %collective-permute-done.3.refs_2_), channel_id=1, source_target_pairs={{0,1},{1,0},{2,3},{3,2},{4,5},{5,4},{6,7},{7,6},{8,9},{9,8},{10,11... | collective-permute-start | bytes 1572872 | tf_op jit(solution)/shard_map/ppermute | solution.py:400
  47.6 1.3 %collective-permute-start.6 = (f32[19,8,128]{2,1,0:T(8,128)S(1)}, f32[19,8,128]{2,1,0:T(8,128)S(1)}, u32[]{:S(2)}, u32[]{:S(2)}) collective-permute-start(f32[19,8,128]{2,1,0:T(8,128)S(1)} %get-tuple-element.65.own), channel_id=1, source_target_pairs={{0,4},{4,0},{8,12},{12,8},{16,20},{20,16},{24,28},{28,24},{1,5},{5... | collective-permute-start | bytes 233480 | tf_op jit(solution)/shard_map/ppermute | solution.py:416
  49.5 4.9 %collective-permute-start.9 = (bf16[19,8,128]{2,1,0:T(8,128)(2,1)S(1)}, bf16[19,8,128]{2,1,0:T(8,128)(2,1)S(1)}, u32[]{:S(2)}, u32[]{:S(2)}) collective-permute-start(bf16[19,8,128]{2,1,0:T(8,128)(2,1)S(1)} %fold.1), channel_id=1, source_target_pairs={{0,24},{4,28},{8,16},{12,20},{16,8},{20,12},{24,0},{28,4},{1,25},{... | collective-permute-start | bytes 116744 | tf_op jit(solution)/shard_map/ppermute | solution.py:416
  52.0 4.0 %collective-permute-start.8 = (bf16[19,8,128]{2,1,0:T(8,128)(2,1)S(1)}, bf16[19,8,128]{2,1,0:T(8,128)(2,1)S(1)}, u32[]{:S(2)}, u32[]{:S(2)}) collective-permute-start(bf16[19,8,128]{2,1,0:T(8,128)(2,1)S(1)} %fold.1), channel_id=1, source_target_pairs={{0,16},{4,20},{8,24},{12,28},{16,0},{20,4},{24,8},{28,12},{1,17},{... | collective-permute-start | bytes 116744 | tf_op jit(solution)/shard_map/ppermute | solution.py:416
  52.5 4.0 %collective-permute-start.7 = (bf16[19,8,128]{2,1,0:T(8,128)(2,1)S(1)}, bf16[19,8,128]{2,1,0:T(8,128)(2,1)S(1)}, u32[]{:S(2)}, u32[]{:S(2)}) collective-permute-start(bf16[19,8,128]{2,1,0:T(8,128)(2,1)S(1)} %fold.1), channel_id=1, source_target_pairs={{0,8},{4,12},{8,0},{12,4},{16,24},{20,28},{24,16},{28,20},{1,9},{5... | collective-permute-start | bytes 116744 | tf_op jit(solution)/shard_map/ppermute | solution.py:416
  63.1 12.3 %collective-permute-start.10 = (bf16[1024,256]{1,0:T(8,128)(2,1)S(1)}, bf16[1024,256]{1,0:T(8,128)(2,1)S(1)}, u32[]{:S(2)}, u32[]{:S(2)}) collective-permute-start(bf16[1024,256]{1,0:T(8,128)(2,1)S(1)} %get-tuple-element.67), channel_id=1, source_target_pairs={{0,1},{1,0},{2,3},{3,2},{4,5},{5,4},{6,7},{7,6},{8,9},{9,8},{10,11... | collective-permute-start | bytes 1572872 | tf_op jit(solution)/shard_map/ppermute | solution.py:400
  75.4 17.2 %copy-start.2 = (f32[2048,128]{1,0:T(8,128)S(1)}, f32[2048,128]{1,0:T(8,128)}, u32[]{:S(2)}) copy-start(f32[2048,128]{1,0:T(8,128)} %copy-done.1) | copy-start | bytes 3145732
  75.5 4.0 %collective-permute-start.11 = (bf16[1024,256]{1,0:T(8,128)(2,1)S(1)}, bf16[1024,256]{1,0:T(8,128)(2,1)S(1)}, u32[]{:S(2)}, u32[]{:S(2)}) collective-permute-start(bf16[1024,256]{1,0:T(8,128)(2,1)S(1)} %add_convert_fusion.3), channel_id=1, source_target_pairs={{0,4},{1,2},{2,1},{3,7},{4,0},{5,6},{6,5},{7,3},{8,12},{9,10},{10,... | collective-permute-start | bytes 1572872 | tf_op jit(solution)/shard_map/ppermute | solution.py:412
  75.6 16.7 %collective-permute-start.13 = (bf16[1024,256]{1,0:T(8,128)(2,1)S(1)}, bf16[1024,256]{1,0:T(8,128)(2,1)S(1)}, u32[]{:S(2)}, u32[]{:S(2)}) collective-permute-start(bf16[1024,256]{1,0:T(8,128)(2,1)S(1)} %get-tuple-element.76), channel_id=1, source_target_pairs={{0,1},{1,0},{2,3},{3,2},{4,5},{5,4},{6,7},{7,6},{8,9},{9,8},{10,11... | collective-permute-start | bytes 1572872 | tf_op jit(solution)/shard_map/ppermute | solution.py:400
  79.7 26.2 %collective-permute-start.12 = (bf16[1024,256]{1,0:T(8,128)(2,1)S(1)}, bf16[1024,256]{1,0:T(8,128)(2,1)S(1)}, u32[]{:S(2)}, u32[]{:S(2)}) collective-permute-start(bf16[1024,256]{1,0:T(8,128)(2,1)S(1)} %add_convert_fusion.2), channel_id=1, source_target_pairs={{0,1},{1,0},{2,3},{3,2},{4,5},{5,4},{6,7},{7,6},{8,9},{9,8},{10,11... | collective-permute-start | bytes 1572872 | tf_op jit(solution)/shard_map/ppermute | solution.py:400
  92.5 13.3 %collective-permute-start.14 = (bf16[1024,256]{1,0:T(8,128)(2,1)S(1)}, bf16[1024,256]{1,0:T(8,128)(2,1)S(1)}, u32[]{:S(2)}, u32[]{:S(2)}) collective-permute-start(bf16[1024,256]{1,0:T(8,128)(2,1)S(1)} %add_convert_fusion.1), channel_id=1, source_target_pairs={{0,4},{1,2},{2,1},{3,7},{4,0},{5,6},{6,5},{7,3},{8,12},{9,10},{10,... | collective-permute-start | bytes 1572872 | tf_op jit(solution)/shard_map/ppermute | solution.py:412
  95.0 1.5 %collective-permute-start.15 = (f32[16,8,128]{2,1,0:T(8,128)S(1)}, f32[16,8,128]{2,1,0:T(8,128)S(1)}, u32[]{:S(2)}, u32[]{:S(2)}) collective-permute-start(f32[16,8,128]{2,1,0:T(8,128)S(1)} %residue_total.1), channel_id=1, source_target_pairs={{0,4},{4,0},{8,12},{12,8},{16,20},{20,16},{24,28},{28,24},{1,5},{5... | collective-permute-start | bytes 196616 | tf_op jit(solution)/shard_map/ppermute | solution.py:416
  96.4 4.4 %collective-permute-start.16 = (f32[16,8,128]{2,1,0:T(8,128)S(1)}, f32[16,8,128]{2,1,0:T(8,128)S(1)}, u32[]{:S(2)}, u32[]{:S(2)}) collective-permute-start(f32[16,8,128]{2,1,0:T(8,128)S(1)} %add.80), channel_id=1, source_target_pairs={{0,8},{4,12},{8,0},{12,4},{16,24},{20,28},{24,16},{28,20},{1,9},{5... | collective-permute-start | bytes 196616 | tf_op jit(solution)/shard_map/ppermute | solution.py:416
  100.9 4.3 %collective-permute-start.17 = (f32[16,8,128]{2,1,0:T(8,128)S(1)}, f32[16,8,128]{2,1,0:T(8,128)S(1)}, u32[]{:S(2)}, u32[]{:S(2)}) collective-permute-start(f32[16,8,128]{2,1,0:T(8,128)S(1)} %add.81), channel_id=1, source_target_pairs={{0,16},{4,20},{8,24},{12,28},{16,0},{20,4},{24,8},{28,12},{1,17},{... | collective-permute-start | bytes 196616 | tf_op jit(solution)/shard_map/ppermute | solution.py:416
  (3 other events, 2.9 us)

commit v3 on v2

--- a/solution.py
+++ b/solution.py
@@ -14,6 +14,7 @@
 HBM = pl.BlockSpec(memory_space=pltpu.HBM)
 SMEM = pl.BlockSpec(memory_space=pltpu.SMEM)
 GRANT = 46 * 2**20
+SMALL = pl.CostEstimate(flops=1, bytes_accessed=1, transcendentals=0)
 
 
 def tile(token):
@@ -52,29 +53,32 @@
         out_specs=[VMEM] * 5,
         out_shape=[flat] * 5,
         compiler_params=pltpu.CompilerParams(vmem_limit_bytes=GRANT),
+        cost_estimate=SMALL,
         name="spread",
     )(features, saved)
 
 
-def gate_kernel(at, has_acc, shards, count, plan, *refs):
-    scal = [plan[at + i] for i in range(2 * shards)]
+def gate_kernel(at, has_acc, shards, count, halves, plan, *refs):
     acc = refs[0] if has_acc else None
-    pieces = [piece[...] for piece in refs[has_acc:has_acc + count]]
-    weight, out, buffer, sems = refs[has_acc + count:]
-    width, deep = buffer.shape[2:]
+    pieces = [
+        jnp.concatenate([refs[has_acc + halves * i + part][...] for part in range(halves)])
+        for i in range(count)
+    ]
+    weight, out, buffer, sems = refs[has_acc + halves * count:]
+    width, deep = buffer.shape[1:]
     block = min(256, width)
     copies = []
     for shard in range(shards):
-        columns = pl.ds(pl.multiple_of(scal[shard] * deep, deep), deep)
+        columns = pl.ds(pl.multiple_of(plan[at + shard] * deep, deep), deep)
         copies.append(
-            pltpu.make_async_copy(weight.at[:, columns], buffer.at[shard, 0], sems.at[shard])
+            pltpu.make_async_copy(weight.at[:, columns], buffer.at[shard], sems.at[shard])
         )
         copies[-1].start()
     if shards < count:
-        pieces = [jnp.where(scal[1] > 0, *pieces)]
+        pieces = [jnp.where(plan[at + 1] > 0, *pieces)]
     elif shards > 1:
         pieces = [
-            jnp.where(scal[shards + i] > 0, piece, jnp.zeros_like(piece))
+            jnp.where(plan[at + shards + i] > 0, piece, jnp.zeros_like(piece))
             for i, piece in enumerate(pieces)
         ]
     for shard in range(shards):
@@ -82,7 +86,7 @@
         for start in range(0, width, block):
             rows = pl.ds(start, block)
             value = lax.dot_general(
-                pieces[shard], buffer[shard, 0, rows, :], NT, preferred_element_type=jnp.float32
+                pieces[shard], buffer[shard, rows, :], NT, preferred_element_type=jnp.float32
             )
             if shard:
                 value = value + out[:, rows]
@@ -92,39 +96,42 @@
 
 
 def gate_step(plan, at, acc, pieces, weight, shards):
-    tokens, deep = pieces[0].shape
+    halves = len(pieces[0])
+    tokens, deep = halves * pieces[0][0].shape[0], pieces[0][0].shape[1]
     width = weight.shape[0]
     has_acc = acc is not None
+    flat = [piece for shard in pieces for piece in shard]
     return pl.pallas_call(
-        functools.partial(gate_kernel, at, has_acc, shards, len(pieces)),
-        in_specs=[SMEM] + [VMEM] * (has_acc + len(pieces))
-        + [HBM],
+        functools.partial(gate_kernel, at, has_acc, shards, len(pieces), halves),
+        in_specs=[SMEM] + [VMEM] * (has_acc + len(flat)) + [HBM],
         out_specs=VMEM,
         out_shape=jax.ShapeDtypeStruct((tokens, width), jnp.float32),
         scratch_shapes=[
-            pltpu.VMEM((shards, 1, width, deep), jnp.bfloat16),
+            pltpu.VMEM((shards, width, deep), jnp.bfloat16),
             pltpu.SemaphoreType.DMA((shards,)),
         ],
         compiler_params=pltpu.CompilerParams(vmem_limit_bytes=GRANT),
-        cost_estimate=pl.CostEstimate(
-            flops=2 * tokens * width * deep * shards,
-            bytes_accessed=2 * shards * width * deep,
-            transcendentals=0,
-        ),
+        cost_estimate=SMALL,
         name="gate_step",
-    )(plan, *([acc] if has_acc else []), *pieces, weight)
-
-
-def close_kernel(at_plan, extra, plan, acc, piece, weight, query, saved, lam, gconv, gquery, packet, gate):
-    tokens, width = acc.shape
+    )(plan, *([acc] if has_acc else []), *flat, weight)
+
+
+def close_kernel(at, extra, late, plan, acc, piece, weight, query, saved, lam, *refs):
+    if late:
+        gconv, gquery, packet, gate = refs
+    else:
+        later, gconv, gquery, packet, gate = refs
+    tokens = piece.shape[0]
+    first = tokens if late else 0
+    width = weight.shape[0]
     poles = lam.shape[0]
     block = min(256, width)
     if width < ROWS * LANES:
         gate[...] = jnp.zeros(gate.shape, gate.dtype)
-    arrived = jnp.where(plan[at_plan] > 0, piece[...], jnp.zeros(piece.shape, piece.dtype))
+    arrived = jnp.where(plan[at] > 0, piece[...], jnp.zeros(piece.shape, piece.dtype))
     for start in range(0, width, block):
         columns = pl.ds(start, block)
-        value = acc[:, columns] + lax.dot_general(
+        value = acc[pl.ds(first, tokens), columns] + lax.dot_general(
             arrived, weight[columns, :], NT, preferred_element_type=jnp.float32
         )
         for group in range(block // LANES):
@@ -132,44 +139,50 @@
             gate[rows, :] = value[:, group * LANES:(group + 1) * LANES]
 
     def body(n, state):
-        at = tile(tokens - 1 - n)
-        grad = gate[at, :]
-        conv = grad * query[at, :]
-        gconv[at, :] = conv
-        gquery[at, :] = grad * saved[at, :]
+        token = tokens - 1 - n
+        here = tile(token)
+        there = tile(first + token)
+        grad = gate[here, :]
+        conv = grad * query[there, :]
+        gconv[here, :] = conv
+        gquery[here, :] = grad * saved[there, :]
         return tuple(lam[m] * state[m] + conv for m in range(poles))
 
-    zero = jnp.zeros((ROWS, LANES), jnp.float32)
-    state = lax.fori_loop(0, tokens, body, (zero,) * poles, unroll=8)
+    if late:
+        state = (jnp.zeros((ROWS, LANES), jnp.float32),) * poles
+    else:
+        state = tuple(later[m] for m in range(poles))
+    state = lax.fori_loop(0, tokens, body, state, unroll=8)
     for m in range(poles):
         packet[m] = state[m]
-    for row in range(extra - 1):
-        packet[poles + row] = gconv[tile(row), :]
-    for row in range(extra):
-        packet[poles + extra - 1 + row] = gquery[tile(row), :]
-
-
-def close_gate(plan, at, acc, piece, weight, query, saved, lam, extra):
+    if not late:
+        for row in range(extra - 1):
+            packet[poles + row] = gconv[tile(row), :]
+        for row in range(extra):
+            packet[poles + extra - 1 + row] = gquery[tile(row), :]
+
+
+def close_gate(plan, at, acc, piece, weight, query, saved, lam, extra, later=None):
     tokens, deep = piece.shape
     width = weight.shape[0]
     poles = lam.shape[0]
+    late = later is None
     flat = (tokens * ROWS, LANES)
+    packed = (poles if late else poles + 2 * extra - 1, ROWS, LANES)
     return pl.pallas_call(
-        functools.partial(close_kernel, at, extra),
-        in_specs=[SMEM] + [VMEM] * 6,
+        functools.partial(close_kernel, at, extra, late),
+        in_specs=[SMEM] + [VMEM] * (6 if late else 7),
         out_specs=[VMEM] * 3,
         out_shape=[
             jax.ShapeDtypeStruct(flat, jnp.float32),
             jax.ShapeDtypeStruct(flat, jnp.float32),
-            jax.ShapeDtypeStruct((poles + 2 * extra - 1, ROWS, LANES), jnp.float32),
+            jax.ShapeDtypeStruct(packed, jnp.float32),
         ],
         scratch_shapes=[pltpu.VMEM(flat, jnp.float32)],
         compiler_params=pltpu.CompilerParams(vmem_limit_bytes=GRANT),
-        cost_estimate=pl.CostEstimate(
-            flops=2 * tokens * width * deep, bytes_accessed=8 * width * deep, transcendentals=0
-        ),
+        cost_estimate=SMALL,
         name="close_gate",
-    )(plan, acc, piece, weight, query, saved, lam)
+    )(plan, acc, piece, weight, query, saved, lam, *([] if late else [later]))
 
 
 def fold_kernel(plan, own, other, span, chip):
@@ -189,16 +202,17 @@
         out_specs=VMEM,
         out_shape=jax.ShapeDtypeStruct(own.shape, jnp.bfloat16),
         compiler_params=pltpu.CompilerParams(vmem_limit_bytes=GRANT),
+        cost_estimate=SMALL,
         name="fold",
     )(plan, own, other, span)
 
 
 def scan_kernel(
-    at_plan, taps, chips, plan, gconv, gquery, key_acts, value_acts, lam, rate, residues, filters, kv_halo,
-    own, other, *refs,
+    at_plan, taps, chips, plan, late_conv, late_query, early_conv, early_query, key_acts, value_acts,
+    lam, rate, residues, filters, kv_halo, own, other, *refs,
 ):
     arrived = refs[:chips - 1]
-    weight, proj, chunk, entering, passed, spread, buffer, sem = refs[chips - 1:]
+    weight, proj, chunk, chunk_rest, entering, passed, spread, buffer, sem = refs[chips - 1:]
     extra = taps - 1
     tokens, width = proj.shape[1:]
     poles = lam.shape[0]
@@ -241,14 +255,17 @@
         values.append(product * kv_halo[0, row])
         queries.append(halo[extra - 1 + row])
 
-    def body(n, carry):
+    half = tokens // 2
+
+    def body(first, gconv, gquery, n, carry):
         state, later = carry
-        at = tile(tokens - 1 - n)
-        conv = gconv[at, :]
+        here = tile(half - 1 - n)
+        at = tile(first + half - 1 - n)
+        conv = gconv[here, :]
         passed[at, :] = conv
         state = tuple(lam[m] * state[m] + conv for m in range(poles))
         product = tree_sum([residues[m] * state[m] for m in range(poles)])
-        now = (gquery[at, :], product * value_acts[at, :], product * key_acts[at, :])
+        now = (gquery[here, :], product * value_acts[at, :], product * key_acts[at, :])
         for which in range(3):
             spread[which, at, :] = tree_sum(
                 [filters[which, 0] * now[which]]
@@ -260,44 +277,49 @@
         tuple(entering[m] for m in range(poles)),
         (tuple(queries), tuple(keys), tuple(values)),
     )
-    lax.fori_loop(0, tokens, body, carry, unroll=8)
+    for first, gconv, gquery in ((half, late_conv, late_query), (0, early_conv, early_query)):
+        carry = lax.fori_loop(
+            0, half, functools.partial(body, first, gconv, gquery), carry, unroll=8
+        )
     for which in range(3):
         for group in range(width // LANES):
             proj[which, :, pl.ds(group * LANES, LANES)] = spread[
                 which, pl.ds(group, tokens, stride=ROWS), :
             ].astype(jnp.bfloat16)
     copy.wait()
-    project_rows(buffer, proj, chunk)
-
-
-def project_rows(weight, proj, out):
-    rows = out.shape[0]
+    project_rows(buffer, proj, (chunk, chunk_rest))
+
+
+def project_rows(weight, proj, outs):
+    rows = outs[0].shape[0]
     block = min(256, rows)
-    for start in range(0, rows, block):
-        value = tree_sum([
-            lax.dot_general(
-                weight[which, pl.ds(start, block), :], proj[which],
-                NT, preferred_element_type=jnp.float32,
-            )
-            for which in range(3)
-        ])
-        out[pl.ds(start, block), :] = value.astype(out.dtype)
-
-
-def scan_block(plan, at, gconv, gquery, keys, values, lam, rate, residues, filters, kv_halo, own, other,
+    for part, out in enumerate(outs):
+        for start in range(0, rows, block):
+            value = tree_sum([
+                lax.dot_general(
+                    weight[which, pl.ds(part * rows + start, block), :], proj[which],
+                    NT, preferred_element_type=jnp.float32,
+                )
+                for which in range(3)
+            ])
+            out[pl.ds(start, block), :] = value.astype(out.dtype)
+
+
+def scan_block(plan, at, gated, keys, values, lam, rate, residues, filters, kv_halo, own, other,
                arrived, weight, deep, width):
-    tokens = gconv.shape[0] // ROWS
+    tokens = keys.shape[0] // ROWS
     taps = filters.shape[1]
     return pl.pallas_call(
         functools.partial(scan_kernel, at, taps, len(arrived) + 1),
-        in_specs=[SMEM] + [VMEM] * (11 + len(arrived))
+        in_specs=[SMEM] + [VMEM] * (13 + len(arrived))
         + [HBM],
-        out_specs=[VMEM] * 4,
+        out_specs=[VMEM] * 5,
         out_shape=[
             jax.ShapeDtypeStruct((3, tokens, width), jnp.bfloat16),
-            jax.ShapeDtypeStruct((deep, tokens), jnp.bfloat16),
+            jax.ShapeDtypeStruct((deep // 2, tokens), jnp.bfloat16),
+            jax.ShapeDtypeStruct((deep // 2, tokens), jnp.bfloat16),
             jax.ShapeDtypeStruct(lam.shape, jnp.float32),
-            jax.ShapeDtypeStruct(gconv.shape, jnp.float32),
+            jax.ShapeDtypeStruct(keys.shape, jnp.float32),
         ],
         scratch_shapes=[
             pltpu.VMEM((3, tokens * ROWS, LANES), jnp.float32),
@@ -305,15 +327,12 @@
             pltpu.SemaphoreType.DMA,
         ],
         compiler_params=pltpu.CompilerParams(vmem_limit_bytes=GRANT),
-        cost_estimate=pl.CostEstimate(
-            flops=6 * tokens * width * deep, bytes_accessed=16 * width * deep, transcendentals=0
-        ),
+        cost_estimate=SMALL,
         name="scan",
-    )(plan, gconv, gquery, keys, values, lam, rate, residues, filters, kv_halo, own, other, *arrived,
-      weight)
-
-
-def total_kernel(gconv, product, lam, entering, total):
+    )(plan, *gated, keys, values, lam, rate, residues, filters, kv_halo, own, other, *arrived, weight)
+
+
+def add_up_residues(gconv, product, lam, entering, total):
     tokens = gconv.shape[0] // ROWS
     poles = lam.shape[0]
 
@@ -331,22 +350,13 @@
         total[m] = sums[m]
 
 
-def residue_total(gconv, product, lam, entering):
-    return pl.pallas_call(
-        total_kernel,
-        in_specs=[VMEM] * 4,
-        out_specs=VMEM,
-        out_shape=jax.ShapeDtypeStruct(lam.shape, jnp.float32),
-        compiler_params=pltpu.CompilerParams(vmem_limit_bytes=GRANT),
-        cost_estimate=pl.CostEstimate(
-            flops=4 * gconv.size * lam.shape[0], bytes_accessed=8 * gconv.size, transcendentals=0
-        ),
-        name="residue_total",
-    )(gconv, product, lam, entering)
-
-
-def project_kernel(at, count, plan, proj, weight, *refs):
-    outs, buffer, sems = refs[:count], refs[count], refs[count + 1]
+def project_kernel(at, count, with_total, plan, proj, weight, *refs):
+    if with_total:
+        sources, refs = refs[:4], refs[4:]
+    outs, refs = refs[:2 * count], refs[2 * count:]
+    if with_total:
+        total, refs = refs[0], refs[1:]
+    buffer, sems = refs
     deep = buffer.shape[2]
     copies = [
         pltpu.make_async_copy(
@@ -357,18 +367,23 @@
     ]
     for copy in copies:
         copy.start()
+    if with_total:
+        add_up_residues(*sources, total)
     for i in range(count):
         copies[i].wait()
-        project_rows(buffer.at[i], proj, outs[i])
-
-
-def project(plan, at, count, proj, weight, deep):
+        project_rows(buffer.at[i], proj, outs[2 * i:2 * i + 2])
+
+
+def project(plan, at, count, proj, weight, deep, sources=()):
     _, tokens, width = proj.shape
+    outs = [jax.ShapeDtypeStruct((deep // 2, tokens), jnp.bfloat16)] * (2 * count)
+    if sources:
+        outs.append(jax.ShapeDtypeStruct(sources[-1].shape, jnp.float32))
     return pl.pallas_call(
-        functools.partial(project_kernel, at, count),
-        in_specs=[SMEM, VMEM, HBM],
-        out_specs=[VMEM] * count,
-        out_shape=[jax.ShapeDtypeStruct((deep, tokens), jnp.bfloat16)] * count,
+        functools.partial(project_kernel, at, count, bool(sources)),
+        in_specs=[SMEM, VMEM, HBM] + [VMEM] * len(sources),
+        out_specs=[VMEM] * len(outs),
+        out_shape=outs,
         scratch_shapes=[
             pltpu.VMEM((count, 3, deep, width), jnp.bfloat16),
             pltpu.SemaphoreType.DMA((count,)),
@@ -380,7 +395,7 @@
             transcendentals=0,
         ),
         name="project",
-    )(plan, proj, weight)
+    )(plan, proj, weight, *sources)
 
 
 def scalars(*values):
@@ -483,30 +498,47 @@
     planned("chunks", chunks)
     plan = scalars(*plan)
 
-    evens = swap_even(grad_out, count)
-    odds = swap_odd(grad_out, count, blocks)
-    query, keys, values, saved, product = spread_acts(features, saved_conv)
-    acc = gate_step(plan, places["own"], None, [grad_out], out_weight, 1)
-    kv_halo = tiles(features[1:3, :extra].astype(f32))
-    kv_halo = lax.ppermute(kv_halo, "ctx", [(i, (i - 1) % blocks) for i in range(blocks)])
-    last = jnp.where(even, jnp.minimum(count - 1, me + count - 1), jnp.maximum(me - count + 1, 0))
-    last_weight = lax.dynamic_slice(out_weight, (0, last * width), (width, width))
-    (
-        evens, odds, acc, plan, query, keys, values, saved, product, rate, lam, span, res, filters
-    ) = tie(evens, odds, acc, plan, query, keys, values, saved, product, rate, lam, span, res, filters)
+    half = tokens // 2
+    evens = [swap_even(grad_out[half:], count)]
+    odds = [swap_odd(grad_out[half:], count, blocks)]
+    rest, plan, rate, lam, span, res, filters = tie(grad_out, plan, rate, lam, span, res, filters)
+    evens.append(swap_even(rest[:half], count))
+    odds.append(swap_odd(rest[:half], count, blocks))
+    evens[0], odds[0] = tie(evens[0], odds[0])
+    acc = None
     for phase in range(1, count - 1):
-        next_evens = swap_even(odds, count)
-        next_odds = swap_odd(evens, count, blocks)
+        ahead = [[swap_even(odds[0], count)], [swap_odd(evens[0], count, blocks)]]
+        if phase == 1:
+            acc = gate_step(plan, places["own"], None, [[grad_out]], out_weight, 1)
+            evens[1], odds[1], acc = tie(evens[1], odds[1], acc)
+        ahead[0].append(swap_even(odds[1], count))
+        ahead[1].append(swap_odd(evens[1], count, blocks))
         acc = gate_step(
-            plan, places["gate", phase], acc, [evens, odds], out_weight,
+            plan, places["gate", phase], acc, [evens[::-1], odds[::-1]], out_weight,
             1 if 2 * phase == count else 2,
         )
-        evens, odds = next_evens, next_odds
+        evens, odds = ahead
+        if phase < count - 2:
+            evens[0], odds[0], acc = tie(evens[0], odds[0], acc)
+            evens[1], odds[1] = tie(evens[1], odds[1])
         if phase == 1:
-            evens, odds, acc, kv_halo, last_weight = tie(evens, odds, acc, kv_halo, last_weight)
-        elif phase < count - 2:
-            evens, odds, acc = tie(evens, odds, acc)
-    gconv, gquery, packet = close_gate(plan, 1, acc, evens, last_weight, query, saved, lam, extra)
+            odds[0], features, saved_conv = tie(odds[0], features, saved_conv)
+            kv_halo = tiles(features[1:3, :extra].astype(f32))
+            kv_halo = lax.ppermute(kv_halo, "ctx", [(i, (i - 1) % blocks) for i in range(blocks)])
+            last = jnp.where(
+                even, jnp.minimum(count - 1, me + count - 1), jnp.maximum(me - count + 1, 0)
+            )
+            last_weight = lax.dynamic_slice(out_weight, (0, last * width), (width, width))
+            query, keys, values, saved, product = spread_acts(features, saved_conv)
+            odds[1], kv_halo, last_weight, query, keys, values, saved, product = tie(
+                odds[1], kv_halo, last_weight, query, keys, values, saved, product
+            )
+    late_conv, late_query, later = close_gate(
+        plan, 1, acc, evens[0], last_weight, query, saved, lam, extra
+    )
+    early_conv, early_query, packet = close_gate(
+        plan, 1, acc, evens[1], last_weight, query, saved, lam, extra, later
+    )
 
     other = swap_ctx(packet, 1, blocks)
     chip = fold(plan, packet, other, span)
@@ -515,29 +547,41 @@
     def added(*parts):
         return sum(value.astype(f32) for value in parts if value is not None).astype(bf16)
 
-    proj, part, entering, gconv = scan_block(
-        plan, places["first"], gconv, gquery, keys, values, lam, rate, res, filters, kv_halo,
-        packet, other, arrived, in_weight, deep, width,
+    def masked(value):
+        return None if value is None else jnp.where(edge, jnp.zeros_like(value), value)
+
+    proj, *part, entering, gconv = scan_block(
+        plan, places["first"], [late_conv, late_query, early_conv, early_query], keys, values, lam,
+        rate, res, filters, kv_halo, packet, other, arrived, in_weight, deep, width,
     )
     for_even, for_odd = {1: part}, {2: part}
-    parts = list(project(plan, places["chunks"], len(chunks), proj, in_weight, deep))
-    evens, odds = swap_even(part, count), None
-    evens, gconv, *parts = tie(evens, gconv, *parts)
+    evens, odds = [swap_even(piece, count) for piece in part], [None, None]
+    *parts, total = project(
+        plan, places["chunks"], 1, proj, in_weight, deep, [gconv, product, lam, entering]
+    )
+    evens[0], proj, total, *parts = tie(
+        evens[0], proj, total, *parts
+    )
+    parts += project(plan, places["chunks"] + 1, len(chunks) - 1, proj, in_weight, deep)
     for phase in range(2, count):
-        for_even[phase] = parts.pop(0)
+        for_even[phase], parts = parts[:2], parts[2:]
         if 2 * phase <= count:
             for_odd[phase + 1] = for_even[phase]
         elif phase + 1 < count:
-            for_odd[phase + 1] = parts.pop(0)
-    total = residue_total(gconv, product, lam, entering)
+            for_odd[phase + 1], parts = parts[:2], parts[2:]
     for phase in range(2, count):
-        if odds is not None:
-            odds = jnp.where(edge, jnp.zeros_like(odds), odds)
-        next_evens = swap_even(added(for_even[phase], odds), count)
-        odds = swap_odd(added(for_odd[phase], evens), count, blocks)
-        evens = next_evens
-    odds = jnp.where(edge, jnp.zeros_like(odds), odds)
-    grad_input = added(parts.pop(0), evens, odds)
+        if phase > 2:
+            for piece in range(2):
+                evens[piece], odds[piece] = tie(evens[piece], odds[piece])
+        if phase == count - 1:
+            odds[0], total = tie(odds[0], total)
+        for piece in range(2):
+            next_even = swap_even(added(for_even[phase][piece], masked(odds[piece])), count)
+            odds[piece] = swap_odd(added(for_odd[phase][piece], evens[piece]), count, blocks)
+            evens[piece] = next_even
+    grad_input = jnp.concatenate(
+        [added(parts[piece], evens[piece], masked(odds[piece])) for piece in range(2)]
+    )
 
     mask = 1
     while mask < blocks:

time: 108 us -> 98.5 us (0.912)
  starting transfers between devices: 32.8 us -> 26.8 us
  local copies, waits for them, and re-layouts: 10.6 us -> 6.23 us
  Pallas kernels: 33.2 us -> 35.4 us
    unnamed x21 -> x9, local copies, waits for them, and re-layouts: 7.94 us -> 1.53 us
    ppermute x6 -> x12, starting transfers between devices: 23.3 us -> 18.5 us  [swap_even(): return lax.ppermute(value, 'chan', [(i, i ^ 1) for i in range(count)])]
    pallas_call x3 -> x4, Pallas kernels: 13.9 us -> 16.5 us  [the longest x2 12.2 us: project(): pl.pallas_call(functools.partial(project_kernel, at, count, bool(sources)...]
    ppermute x1, starting transfers between devices: 2.79 us -> 0.75 us  [local(): lax.ppermute(kv_halo, 'ctx', [(i, (i - 1) % blocks) for i in range(blocks)])]
    slice x0 -> x2, local copies, waits for them, and re-layouts: none -> 2 us  [the longest x1 1.03 us: local(): evens = [swap_even(grad_out[half:], count)]]
    ppermute x7, waiting for transfers between devices: 11.9 us -> 10 us  [swap_ctx(): return lax.ppermute(value, 'ctx', [(i, i ^ mask) for i in range(blocks)])]
    ppermute x6 -> x12, waiting for transfers between devices: 14.2 us -> 15.1 us  [swap_even(): return lax.ppermute(value, 'chan', [(i, i ^ 1) for i in range(count)])]
  transfers between devices with their start and end apart: 18 -> 28, of which waited for: 11 -> 14; matrix products, arithmetic and copies ran while one was open for 6% -> 8% of each run, Pallas kernels for 22% -> 27%
where the time goes in v3:
time: 98.5 us; the launch traced here: 97.9 us
  Pallas kernels  35.4 us (36%)
  starting transfers between devices  26.8 us (27%)
  waiting for transfers between devices  25.2 us (26%)
  local copies, waits for them, and re-layouts  6.23 us (6%)
  other arithmetic  3.18 us (3%)
  between operations  1.07 us (1%)
    ppermute x12, starting transfers between devices, swap_even(): return lax.ppermute(value, 'chan', [(i, i ^ 1) for i in range(count)])  18.5 us
    ppermute x12, waiting for transfers between devices, swap_even(): return lax.ppermute(value, 'chan', [(i, i ^ 1) for i in range(count)])  15.1 us
    pallas_call x2, Pallas kernels, project(): pl.pallas_call(functools.partial(project_kernel, at, count, bool(sources)...  12.2 us
    pallas_call x3, Pallas kernels, gate_step(): pl.pallas_call(functools.partial(gate_kernel, at, has_acc, shards, len(pi...  10.4 us
    ppermute x7, waiting for transfers between devices, swap_ctx(): return lax.ppermute(value, 'ctx', [(i, i ^ mask) for i in range(blocks)])  10 us
    pallas_call x1, Pallas kernels, scan_block(): pl.pallas_call(functools.partial(scan_kernel, at, taps, len(arrived) + 1)...  6.53 us
    ppermute x7, starting transfers between devices, swap_ctx(): return lax.ppermute(value, 'ctx', [(i, i ^ mask) for i in range(blocks)])  6.5 us
    pallas_call x2, Pallas kernels, close_gate(): pl.pallas_call(functools.partial(close_kernel, at, extra, late), in_specs...  4.27 us
  transfers between devices with their start and end apart: 28, of which 14 were waited for; matrix products, arithmetic and copies ran while one was open for 8% of the time, Pallas kernels for 27%

profile of v3, /device:TPU:0, one launch (start us, length us, event | category | flops | bytes accessed | tf_op | source)
XLA Modules:
  0.0 97.9 jit_solution(12172765171799434059)
XLA Ops:
  2.2 4.1 %collective-permute-start = (bf16[128,1024]{1,0:T(8,128)(2,1)S(1)}, bf16[128,1024]{1,0:T(8,128)(2,1)S(1)}, u32[]{:S(2)}, u32[]{:S(2)}) collective-permute-start(bf16[128,1024]{1,0:T(8,128)(2,1)S(1)} %slice.11), channel_id=1, source_target_pairs={{0,1},{1,0},{2,3},{3,2},{4,5},{5,4},{6,7},{7,6},{8,9},{9,8},{10,11... | collective-permute-start | bytes 786440 | tf_op jit(solution)/shard_map/ppermute | solution.py:415
  12.4 1.7 %collective-permute-start.2 = (bf16[128,1024]{1,0:T(8,128)(2,1)S(1)}, bf16[128,1024]{1,0:T(8,128)(2,1)S(1)}, u32[]{:S(2)}, u32[]{:S(2)}) collective-permute-start(bf16[128,1024]{1,0:T(8,128)(2,1)S(1)} %collective-permute-done.1.refs_4_), channel_id=1, source_target_pairs={{0,1},{1,0},{2,3},{3,2},{4,5},{5,4},{6,7},{7,6},{8,9},{9,8},{10,11... | collective-permute-start | bytes 786440 | tf_op jit(solution)/shard_map/ppermute | solution.py:415
  14.1 2.9 %gate_step.3.refs_0_ = f32[256,1024]{1,0:T(8,128)S(1)} custom-call(s32[14]{0:T(128)S(1)} %stack.65.plan, bf16[256,1024]{1,0:T(8,128)(2,1)S(1)} %copy-done, bf16[1024,4096]{1,0:T(8,128)(2,1)} %refs_5_.3), custom_call_target="tpu_custom_call" | custom-call | flops 1 | bytes 1 | tf_op jit(solution)/shard_map/gate_step/pallas_call | solution.py:104
  17.1 2.4 %collective-permute-done.4.refs_1_ = bf16[128,1024]{1,0:T(8,128)(2,1)} collective-permute-done((bf16[128,1024]{1,0:T(8,128)(2,1)S(1)}, bf16[128,1024]{1,0:T(8,128)(2,1)}, u32[]{:S(2)}, u32[]{:S(2)}) %collective-permute-start.4) | collective-permute-done | bytes 262176 | tf_op jit(solution)/shard_map/ppermute | solution.py:415
  19.5 2.0 %collective-permute-start.6 = (bf16[128,1024]{1,0:T(8,128)(2,1)S(1)}, bf16[128,1024]{1,0:T(8,128)(2,1)}, u32[]{:S(2)}, u32[]{:S(2)}) collective-permute-start(bf16[128,1024]{1,0:T(8,128)(2,1)S(1)} %collective-permute-done.5.refs_3_), channel_id=1, source_target_pairs={{0,1},{1,0},{2,3},{3,2},{4,5},{5,4},{6,7},{7,6},{8,9},{9,8},{10,11... | collective-permute-start | bytes 786440 | tf_op jit(solution)/shard_map/ppermute | solution.py:415
  21.5 4.0 %gate_step.4.refs_0_ = f32[256,1024]{1,0:T(8,128)S(1)} custom-call(s32[14]{0:T(128)S(1)} %stack.65.plan, f32[256,1024]{1,0:T(8,128)S(1)} %gate_step.3.refs_0_, bf16[128,1024]{1,0:T(8,128)(2,1)} %collective-permute-done.4.refs_1_, bf16[128,1024]{1,0:T(8,128)(2,1)S(1)} %collective-permute-done.refs_2_, bf16[128,1024]{1,0:T(8,128)(2,1)S(1)} %collective-permute-done.5.refs_3_, ...), custom_call_target="tpu_custom_call" | custom-call | flops 1 | bytes 1 | tf_op jit(solution)/shard_map/gate_step/pallas_call | solution.py:104
  27.1 1.8 %constant_dynamic-slice_fusion.weight = bf16[1024,1024]{1,0:T(8,128)(2,1)S(1)} fusion(bf16[1024,4096]{1,0:T(8,128)(2,1)} %refs_5_.3, s32[]{:T(128)S(6)} %select_n.93), kind=kLoop, calls=%fused_computation.15 | loop fusion | bytes 4194308 | tf_op jit(solution)/shard_map/dynamic_slice | solution.py:531
  28.9 1.6 %collective-permute-start.9 = (bf16[128,1024]{1,0:T(8,128)(2,1)}, bf16[128,1024]{1,0:T(8,128)(2,1)S(1)}, u32[]{:S(2)}, u32[]{:S(2)}) collective-permute-start(bf16[128,1024]{1,0:T(8,128)(2,1)} %collective-permute-done.3.refs_4_), channel_id=1, source_target_pairs={{0,1},{1,0},{2,3},{3,2},{4,5},{5,4},{6,7},{7,6},{8,9},{9,8},{10,11... | collective-permute-start | bytes 786440 | tf_op jit(solution)/shard_map/ppermute | solution.py:415
  32.6 3.5 %gate_step.5.acc = f32[256,1024]{1,0:T(8,128)S(1)} custom-call(s32[14]{0:T(128)S(1)} %stack.65.plan, f32[256,1024]{1,0:T(8,128)S(1)} %gate_step.4.refs_0_, bf16[128,1024]{1,0:T(8,128)(2,1)} %collective-permute-done.6.refs_1_, bf16[128,1024]{1,0:T(8,128)(2,1)S(1)} %collective-permute-done.2.refs_2_, bf16[128,1024]{1,0:T(8,128)(2,1)} %collective-permute-done.7.refs_3_, ...), custom_call_target="tpu_custom_call" | custom-call | flops 1 | bytes 1 | tf_op jit(solution)/shard_map/gate_step/pallas_call | solution.py:104
  36.0 2.3 %collective-permute-done.9.piece = bf16[128,1024]{1,0:T(8,128)(2,1)S(1)} collective-permute-done((bf16[128,1024]{1,0:T(8,128)(2,1)}, bf16[128,1024]{1,0:T(8,128)(2,1)S(1)}, u32[]{:S(2)}, u32[]{:S(2)}) %collective-permute-start.9) | collective-permute-done | bytes 262176 | tf_op jit(solution)/shard_map/ppermute | solution.py:415
  38.4 2.2 %close_gate.2 = (f32[1024,128]{1,0:T(8,128)S(1)}, f32[1024,128]{1,0:T(8,128)S(1)}, f32[16,8,128]{2,1,0:T(8,128)S(1)}) custom-call(s32[14]{0:T(128)S(1)} %stack.65.plan, f32[256,1024]{1,0:T(8,128)S(1)} %gate_step.5.acc, bf16[128,1024]{1,0:T(8,128)(2,1)S(1)} %collective-permute-done.9.piece, bf16[1024,1024]{1,0:T(8,128)(2,1)S(1)} %constant_dynamic-slice_fusion.weight, ...), custom_call_target="tpu_custom_call" | custom-call | flops 1 | bytes 1 | tf_op jit(solution)/shard_map/close_gate/pallas_call | solution.py:172
  40.6 2.2 %collective-permute-done.10.piece = bf16[128,1024]{1,0:T(8,128)(2,1)S(1)} collective-permute-done((bf16[128,1024]{1,0:T(8,128)(2,1)}, bf16[128,1024]{1,0:T(8,128)(2,1)S(1)}, u32[]{:S(2)}, u32[]{:S(2)}) %collective-permute-start.10) | collective-permute-done | bytes 262176 | tf_op jit(solution)/shard_map/ppermute | solution.py:415
  42.8 2.0 %close_gate.3 = (f32[1024,128]{1,0:T(8,128)S(1)}, f32[1024,128]{1,0:T(8,128)S(1)}, f32[19,8,128]{2,1,0:T(8,128)S(1)}) custom-call(s32[14]{0:T(128)S(1)} %stack.65.plan, f32[256,1024]{1,0:T(8,128)S(1)} %gate_step.5.acc, bf16[128,1024]{1,0:T(8,128)(2,1)S(1)} %collective-permute-done.10.piece, bf16[1024,1024]{1,0:T(8,128)(2,1)S(1)} %constant_dynamic-slice_fusion.weight, ...), custom_call_target="tpu_custom_call" | custom-call | flops 1 | bytes 1 | tf_op jit(solution)/shard_map/close_gate/pallas_call | solution.py:172
  46.8 2.5 %collective-permute-start.14 = (bf16[19,8,128]{2,1,0:T(8,128)(2,1)S(1)}, bf16[19,8,128]{2,1,0:T(8,128)(2,1)S(1)}, u32[]{:S(2)}, u32[]{:S(2)}) collective-permute-start(bf16[19,8,128]{2,1,0:T(8,128)(2,1)S(1)} %fold.1), channel_id=1, source_target_pairs={{0,24},{4,28},{8,16},{12,20},{16,8},{20,12},{24,0},{28,4},{1,25},{... | collective-permute-start | bytes 116744 | tf_op jit(solution)/shard_map/ppermute | solution.py:431
  53.8 6.5 %scan.1 = (bf16[3,256,1024]{2,1,0:T(8,128)(2,1)S(1)}, bf16[512,256]{1,0:T(8,128)(2,1)S(1)}, bf16[512,256]{1,0:T(8,128)(2,1)S(1)}, f32[16,8,128]{2,1,0:T(8,128)S(1)}, f32[2048,128]{1,0:T(8,128)S(1)}) custom-call(s32[14]{0:T(128)S(1)} %stack.65.plan, f32[1024,128]{1,0:T(8,128)S(1)} %get-tuple-element.89.late_conv, ...), custom_call_target="tpu_custom_call" | custom-call | flops 1 | bytes 1 | tf_op jit(solution)/shard_map/scan/pallas_call | solution.py:312
  62.4 5.2 %project.2 = (bf16[512,256]{1,0:T(8,128)(2,1)S(1)}, bf16[512,256]{1,0:T(8,128)(2,1)S(1)}, f32[16,8,128]{2,1,0:T(8,128)S(1)}) custom-call(s32[14]{0:T(128)S(1)} %stack.65.plan, bf16[3,256,1024]{2,1,0:T(8,128)(2,1)S(1)} %get-tuple-element.110.proj, bf16[3,4096,1024]{2,1,0:T(8,128)(2,1)} %weight.3, f32[2048,128]{1,0:T(8,128)S(1)} %get-tuple-element.104.refs_0_, ...), custom_call_target="tpu_custom_call" | custom-call | flops 1610612736 | bytes 6291456 | tf_op jit(solution)/shard_map/project/pallas_call | solution.py:382
  67.6 2.0 %collective-permute-done.15 = bf16[512,256]{1,0:T(8,128)(2,1)S(1)} collective-permute-done((bf16[512,256]{1,0:T(8,128)(2,1)S(1)}, bf16[512,256]{1,0:T(8,128)(2,1)S(1)}, u32[]{:S(2)}, u32[]{:S(2)}) %collective-permute-start.15) | collective-permute-done | bytes 262176 | tf_op jit(solution)/shard_map/ppermute | solution.py:415
  69.8 1.9 %collective-permute-start.16 = (bf16[512,256]{1,0:T(8,128)(2,1)S(1)}, bf16[512,256]{1,0:T(8,128)(2,1)S(1)}, u32[]{:S(2)}, u32[]{:S(2)}) collective-permute-start(bf16[512,256]{1,0:T(8,128)(2,1)S(1)} %get-tuple-element.113), channel_id=1, source_target_pairs={{0,1},{1,0},{2,3},{3,2},{4,5},{5,4},{6,7},{7,6},{8,9},{9,8},{10,11... | collective-permute-start | bytes 786440 | tf_op jit(solution)/shard_map/ppermute | solution.py:415
  72.8 7.0 %project.3 = (bf16[512,256]{1,0:T(8,128)(2,1)S(1)}, bf16[512,256]{1,0:T(8,128)(2,1)S(1)}, bf16[512,256]{1,0:T(8,128)(2,1)S(1)}, bf16[512,256]{1,0:T(8,128)(2,1)S(1)}) custom-call(s32[14]{0:T(128)S(1)} %stack.65.plan, bf16[3,256,1024]{2,1,0:T(8,128)(2,1)S(1)} %get-tuple-element.110.proj, bf16[3,4096,1024]{2,1,0:T(8,128)(2,1)} %weight.3), custom_call_target="tpu_custom_call" | custom-call | flops 3221225472 | bytes 12582912 | tf_op jit(solution)/shard_map/project/pallas_call | solution.py:382
  80.6 1.8 %collective-permute-start.18 = (bf16[512,256]{1,0:T(8,128)(2,1)S(1)}, bf16[512,256]{1,0:T(8,128)(2,1)S(1)}, u32[]{:S(2)}, u32[]{:S(2)}) collective-permute-start(bf16[512,256]{1,0:T(8,128)(2,1)S(1)} %add_convert_fusion.6), channel_id=1, source_target_pairs={{0,1},{1,0},{2,3},{3,2},{4,5},{5,4},{6,7},{7,6},{8,9},{9,8},{10,11... | collective-permute-start | bytes 786440 | tf_op jit(solution)/shard_map/ppermute | solution.py:415
  82.6 1.8 %collective-permute-done.20 = bf16[512,256]{1,0:T(8,128)(2,1)S(1)} collective-permute-done((bf16[512,256]{1,0:T(8,128)(2,1)S(1)}, bf16[512,256]{1,0:T(8,128)(2,1)S(1)}, u32[]{:S(2)}, u32[]{:S(2)}) %collective-permute-start.20) | collective-permute-done | bytes 262176 | tf_op jit(solution)/shard_map/ppermute | solution.py:415
  85.3 3.4 %collective-permute-done.26 = f32[16,8,128]{2,1,0:T(8,128)S(1)} collective-permute-done((f32[16,8,128]{2,1,0:T(8,128)S(1)}, f32[16,8,128]{2,1,0:T(8,128)S(1)}, u32[]{:S(2)}, u32[]{:S(2)}) %collective-permute-start.26) | collective-permute-done | bytes 65568 | tf_op jit(solution)/shard_map/ppermute | solution.py:431
  91.2 1.9 %collective-permute-done.27 = f32[16,8,128]{2,1,0:T(8,128)S(1)} collective-permute-done((f32[16,8,128]{2,1,0:T(8,128)S(1)}, f32[16,8,128]{2,1,0:T(8,128)S(1)}, u32[]{:S(2)}, u32[]{:S(2)}) %collective-permute-start.27) | collective-permute-done | bytes 65568 | tf_op jit(solution)/shard_map/ppermute | solution.py:431
  93.9 3.0 %collective-permute-done.23 = bf16[512,256]{1,0:T(8,128)(2,1)S(1)} collective-permute-done((bf16[512,256]{1,0:T(8,128)(2,1)S(1)}, bf16[512,256]{1,0:T(8,128)(2,1)S(1)}, u32[]{:S(2)}, u32[]{:S(2)}) %collective-permute-start.23) | collective-permute-done | bytes 262176 | tf_op jit(solution)/shard_map/ppermute | solution.py:415
  (72 shorter events, 26.7 us)
Async XLA Ops:
  1.7 10.2 %collective-permute-start.1 = (bf16[128,1024]{1,0:T(8,128)(2,1)S(1)}, bf16[128,1024]{1,0:T(8,128)(2,1)S(1)}, u32[]{:S(2)}, u32[]{:S(2)}) collective-permute-start(bf16[128,1024]{1,0:T(8,128)(2,1)S(1)} %slice.11), channel_id=1, source_target_pairs={{0,4},{1,2},{2,1},{3,7},{4,0},{5,6},{6,5},{7,3},{8,12},{9,10},{10,... | collective-permute-start | bytes 786440 | tf_op jit(solution)/shard_map/ppermute | solution.py:427
  2.2 10.2 %collective-permute-start = (bf16[128,1024]{1,0:T(8,128)(2,1)S(1)}, bf16[128,1024]{1,0:T(8,128)(2,1)S(1)}, u32[]{:S(2)}, u32[]{:S(2)}) collective-permute-start(bf16[128,1024]{1,0:T(8,128)(2,1)S(1)} %slice.11), channel_id=1, source_target_pairs={{0,1},{1,0},{2,3},{3,2},{4,5},{5,4},{6,7},{7,6},{8,9},{9,8},{10,11... | collective-permute-start | bytes 786440 | tf_op jit(solution)/shard_map/ppermute | solution.py:415
  10.1 6.9 %collective-permute-start.5 = (bf16[128,1024]{1,0:T(8,128)(2,1)S(1)}, bf16[128,1024]{1,0:T(8,128)(2,1)S(1)}, u32[]{:S(2)}, u32[]{:S(2)}) collective-permute-start(bf16[128,1024]{1,0:T(8,128)(2,1)S(1)} %slice.12), channel_id=1, source_target_pairs={{0,4},{1,2},{2,1},{3,7},{4,0},{5,6},{6,5},{7,3},{8,12},{9,10},{10,... | collective-permute-start | bytes 786440 | tf_op jit(solution)/shard_map/ppermute | solution.py:427
  10.2 9.3 %collective-permute-start.4 = (bf16[128,1024]{1,0:T(8,128)(2,1)S(1)}, bf16[128,1024]{1,0:T(8,128)(2,1)}, u32[]{:S(2)}, u32[]{:S(2)}) collective-permute-start(bf16[128,1024]{1,0:T(8,128)(2,1)S(1)} %slice.12), channel_id=1, source_target_pairs={{0,1},{1,0},{2,3},{3,2},{4,5},{5,4},{6,7},{7,6},{8,9},{9,8},{10,11... | collective-permute-start | bytes 786440 | tf_op jit(solution)/shard_map/ppermute | solution.py:415
  12.4 13.2 %collective-permute-start.2 = (bf16[128,1024]{1,0:T(8,128)(2,1)S(1)}, bf16[128,1024]{1,0:T(8,128)(2,1)S(1)}, u32[]{:S(2)}, u32[]{:S(2)}) collective-permute-start(bf16[128,1024]{1,0:T(8,128)(2,1)S(1)} %collective-permute-done.1.refs_4_), channel_id=1, source_target_pairs={{0,1},{1,0},{2,3},{3,2},{4,5},{5,4},{6,7},{7,6},{8,9},{9,8},{10,11... | collective-permute-start | bytes 786440 | tf_op jit(solution)/shard_map/ppermute | solution.py:415
  14.1 11.4 %collective-permute-start.3 = (bf16[128,1024]{1,0:T(8,128)(2,1)S(1)}, bf16[128,1024]{1,0:T(8,128)(2,1)}, u32[]{:S(2)}, u32[]{:S(2)}) collective-permute-start(bf16[128,1024]{1,0:T(8,128)(2,1)S(1)} %collective-permute-done.refs_2_), channel_id=1, source_target_pairs={{0,4},{1,2},{2,1},{3,7},{4,0},{5,6},{6,5},{7,3},{8,12},{9,10},{10,... | collective-permute-start | bytes 786440 | tf_op jit(solution)/shard_map/ppermute | solution.py:427
  19.5 12.6 %collective-permute-start.7 = (bf16[128,1024]{1,0:T(8,128)(2,1)}, bf16[128,1024]{1,0:T(8,128)(2,1)}, u32[]{:S(2)}, u32[]{:S(2)}) collective-permute-start(bf16[128,1024]{1,0:T(8,128)(2,1)} %collective-permute-done.4.refs_1_), channel_id=1, source_target_pairs={{0,4},{1,2},{2,1},{3,7},{4,0},{5,6},{6,5},{7,3},{8,12},{9,10},{10,... | collective-permute-start | bytes 786440 | tf_op jit(solution)/shard_map/ppermute | solution.py:427
  19.5 12.6 %collective-permute-start.6 = (bf16[128,1024]{1,0:T(8,128)(2,1)S(1)}, bf16[128,1024]{1,0:T(8,128)(2,1)}, u32[]{:S(2)}, u32[]{:S(2)}) collective-permute-start(bf16[128,1024]{1,0:T(8,128)(2,1)S(1)} %collective-permute-done.5.refs_3_), channel_id=1, source_target_pairs={{0,1},{1,0},{2,3},{3,2},{4,5},{5,4},{6,7},{7,6},{8,9},{9,8},{10,11... | collective-permute-start | bytes 786440 | tf_op jit(solution)/shard_map/ppermute | solution.py:415
  26.4 5.7 %collective-permute-start.8 = (f32[2,2,8,128]{3,2,1,0:T(8,128)S(1)}, f32[2,2,8,128]{3,2,1,0:T(8,128)S(1)}, u32[]{:S(2)}, u32[]{:S(2)}) collective-permute-start(f32[2,2,8,128]{3,2,1,0:T(8,128)S(1)} %reshape.32), channel_id=1, source_target_pairs={{0,28},{4,0},{8,4},{12,8},{16,12},{20,16},{24,20},{28,24},{1,29},{... | collective-permute-start | bytes 49160 | tf_op jit(solution)/shard_map/ppermute | solution.py:527
  28.9 9.5 %collective-permute-start.9 = (bf16[128,1024]{1,0:T(8,128)(2,1)}, bf16[128,1024]{1,0:T(8,128)(2,1)S(1)}, u32[]{:S(2)}, u32[]{:S(2)}) collective-permute-start(bf16[128,1024]{1,0:T(8,128)(2,1)} %collective-permute-done.3.refs_4_), channel_id=1, source_target_pairs={{0,1},{1,0},{2,3},{3,2},{4,5},{5,4},{6,7},{7,6},{8,9},{9,8},{10,11... | collective-permute-start | bytes 786440 | tf_op jit(solution)/shard_map/ppermute | solution.py:415
  32.1 10.7 %collective-permute-start.10 = (bf16[128,1024]{1,0:T(8,128)(2,1)}, bf16[128,1024]{1,0:T(8,128)(2,1)S(1)}, u32[]{:S(2)}, u32[]{:S(2)}) collective-permute-start(bf16[128,1024]{1,0:T(8,128)(2,1)} %collective-permute-done.7.refs_3_), channel_id=1, source_target_pairs={{0,1},{1,0},{2,3},{3,2},{4,5},{5,4},{6,7},{7,6},{8,9},{9,8},{10,11... | collective-permute-start | bytes 786440 | tf_op jit(solution)/shard_map/ppermute | solution.py:415
  46.8 4.9 %collective-permute-start.14 = (bf16[19,8,128]{2,1,0:T(8,128)(2,1)S(1)}, bf16[19,8,128]{2,1,0:T(8,128)(2,1)S(1)}, u32[]{:S(2)}, u32[]{:S(2)}) collective-permute-start(bf16[19,8,128]{2,1,0:T(8,128)(2,1)S(1)} %fold.1), channel_id=1, source_target_pairs={{0,24},{4,28},{8,16},{12,20},{16,8},{20,12},{24,0},{28,4},{1,25},{... | collective-permute-start | bytes 116744 | tf_op jit(solution)/shard_map/ppermute | solution.py:431
  60.3 9.3 %collective-permute-start.15 = (bf16[512,256]{1,0:T(8,128)(2,1)S(1)}, bf16[512,256]{1,0:T(8,128)(2,1)S(1)}, u32[]{:S(2)}, u32[]{:S(2)}) collective-permute-start(bf16[512,256]{1,0:T(8,128)(2,1)S(1)} %get-tuple-element.102), channel_id=1, source_target_pairs={{0,1},{1,0},{2,3},{3,2},{4,5},{5,4},{6,7},{7,6},{8,9},{9,8},{10,11... | collective-permute-start | bytes 786440 | tf_op jit(solution)/shard_map/ppermute | solution.py:415
  61.5 11.2 %collective-permute-start.21 = (bf16[512,256]{1,0:T(8,128)(2,1)S(1)}, bf16[512,256]{1,0:T(8,128)(2,1)S(1)}, u32[]{:S(2)}, u32[]{:S(2)}) collective-permute-start(bf16[512,256]{1,0:T(8,128)(2,1)S(1)} %get-tuple-element.122), channel_id=1, source_target_pairs={{0,1},{1,0},{2,3},{3,2},{4,5},{5,4},{6,7},{7,6},{8,9},{9,8},{10,11... | collective-permute-start | bytes 786440 | tf_op jit(solution)/shard_map/ppermute | solution.py:415
  69.7 10.1 %collective-permute-start.17 = (bf16[512,256]{1,0:T(8,128)(2,1)S(1)}, bf16[512,256]{1,0:T(8,128)(2,1)S(1)}, u32[]{:S(2)}, u32[]{:S(2)}) collective-permute-start(bf16[512,256]{1,0:T(8,128)(2,1)S(1)} %add_convert_fusion.7), channel_id=1, source_target_pairs={{0,4},{1,2},{2,1},{3,7},{4,0},{5,6},{6,5},{7,3},{8,12},{9,10},{10,... | collective-permute-start | bytes 786440 | tf_op jit(solution)/shard_map/ppermute | solution.py:427
  69.8 10.1 %collective-permute-start.16 = (bf16[512,256]{1,0:T(8,128)(2,1)S(1)}, bf16[512,256]{1,0:T(8,128)(2,1)S(1)}, u32[]{:S(2)}, u32[]{:S(2)}) collective-permute-start(bf16[512,256]{1,0:T(8,128)(2,1)S(1)} %get-tuple-element.113), channel_id=1, source_target_pairs={{0,1},{1,0},{2,3},{3,2},{4,5},{5,4},{6,7},{7,6},{8,9},{9,8},{10,11... | collective-permute-start | bytes 786440 | tf_op jit(solution)/shard_map/ppermute | solution.py:415
  71.7 12.7 %collective-permute-start.20 = (bf16[512,256]{1,0:T(8,128)(2,1)S(1)}, bf16[512,256]{1,0:T(8,128)(2,1)S(1)}, u32[]{:S(2)}, u32[]{:S(2)}) collective-permute-start(bf16[512,256]{1,0:T(8,128)(2,1)S(1)} %get-tuple-element.121), channel_id=1, source_target_pairs={{0,1},{1,0},{2,3},{3,2},{4,5},{5,4},{6,7},{7,6},{8,9},{9,8},{10,11... | collective-permute-start | bytes 786440 | tf_op jit(solution)/shard_map/ppermute | solution.py:415
  72.7 11.7 %collective-permute-start.22 = (bf16[512,256]{1,0:T(8,128)(2,1)S(1)}, bf16[512,256]{1,0:T(8,128)(2,1)S(1)}, u32[]{:S(2)}, u32[]{:S(2)}) collective-permute-start(bf16[512,256]{1,0:T(8,128)(2,1)S(1)} %add_convert_fusion.3), channel_id=1, source_target_pairs={{0,4},{1,2},{2,1},{3,7},{4,0},{5,6},{6,5},{7,3},{8,12},{9,10},{10,... | collective-permute-start | bytes 786440 | tf_op jit(solution)/shard_map/ppermute | solution.py:427
  79.9 4.5 %collective-permute-start.25 = (f32[16,8,128]{2,1,0:T(8,128)S(1)}, f32[16,8,128]{2,1,0:T(8,128)S(1)}, u32[]{:S(2)}, u32[]{:S(2)}) collective-permute-start(f32[16,8,128]{2,1,0:T(8,128)S(1)} %get-tuple-element.125), channel_id=1, source_target_pairs={{0,4},{4,0},{8,12},{12,8},{16,20},{20,16},{24,28},{28,24},{1,5},{5... | collective-permute-start | bytes 196616 | tf_op jit(solution)/shard_map/ppermute | solution.py:431
  80.6 13.2 %collective-permute-start.18 = (bf16[512,256]{1,0:T(8,128)(2,1)S(1)}, bf16[512,256]{1,0:T(8,128)(2,1)S(1)}, u32[]{:S(2)}, u32[]{:S(2)}) collective-permute-start(bf16[512,256]{1,0:T(8,128)(2,1)S(1)} %add_convert_fusion.6), channel_id=1, source_target_pairs={{0,1},{1,0},{2,3},{3,2},{4,5},{5,4},{6,7},{7,6},{8,9},{9,8},{10,11... | collective-permute-start | bytes 786440 | tf_op jit(solution)/shard_map/ppermute | solution.py:415
  82.4 11.4 %collective-permute-start.19 = (bf16[512,256]{1,0:T(8,128)(2,1)S(1)}, bf16[512,256]{1,0:T(8,128)(2,1)S(1)}, u32[]{:S(2)}, u32[]{:S(2)}) collective-permute-start(bf16[512,256]{1,0:T(8,128)(2,1)S(1)} %add_convert_fusion.5), channel_id=1, source_target_pairs={{0,4},{1,2},{2,1},{3,7},{4,0},{5,6},{6,5},{7,3},{8,12},{9,10},{10,... | collective-permute-start | bytes 786440 | tf_op jit(solution)/shard_map/ppermute | solution.py:427
  84.4 4.3 %collective-permute-start.26 = (f32[16,8,128]{2,1,0:T(8,128)S(1)}, f32[16,8,128]{2,1,0:T(8,128)S(1)}, u32[]{:S(2)}, u32[]{:S(2)}) collective-permute-start(f32[16,8,128]{2,1,0:T(8,128)S(1)} %add.100), channel_id=1, source_target_pairs={{0,8},{4,12},{8,0},{12,4},{16,24},{20,28},{24,16},{28,20},{1,9},{5... | collective-permute-start | bytes 196616 | tf_op jit(solution)/shard_map/ppermute | solution.py:431
  85.2 8.7 %collective-permute-start.24 = (bf16[512,256]{1,0:T(8,128)(2,1)S(1)}, bf16[512,256]{1,0:T(8,128)(2,1)S(1)}, u32[]{:S(2)}, u32[]{:S(2)}) collective-permute-start(bf16[512,256]{1,0:T(8,128)(2,1)S(1)} %add_convert_fusion.1), channel_id=1, source_target_pairs={{0,4},{1,2},{2,1},{3,7},{4,0},{5,6},{6,5},{7,3},{8,12},{9,10},{10,... | collective-permute-start | bytes 786440 | tf_op jit(solution)/shard_map/ppermute | solution.py:427
  90.4 6.5 %collective-permute-start.23 = (bf16[512,256]{1,0:T(8,128)(2,1)S(1)}, bf16[512,256]{1,0:T(8,128)(2,1)S(1)}, u32[]{:S(2)}, u32[]{:S(2)}) collective-permute-start(bf16[512,256]{1,0:T(8,128)(2,1)S(1)} %add_convert_fusion.2), channel_id=1, source_target_pairs={{0,1},{1,0},{2,3},{3,2},{4,5},{5,4},{6,7},{7,6},{8,9},{9,8},{10,11... | collective-permute-start | bytes 786440 | tf_op jit(solution)/shard_map/ppermute | solution.py:415
  (7 other events, 35.5 us)

commit v4 on v3

--- a/solution.py
+++ b/solution.py
@@ -14,6 +14,7 @@
 HBM = pl.BlockSpec(memory_space=pltpu.HBM)
 SMEM = pl.BlockSpec(memory_space=pltpu.SMEM)
 GRANT = 46 * 2**20
+TAIL = 16
 SMALL = pl.CostEstimate(flops=1, bytes_accessed=1, transcendentals=0)
 
 
@@ -116,11 +117,11 @@
     )(plan, *([acc] if has_acc else []), *flat, weight)
 
 
-def close_kernel(at, extra, late, plan, acc, piece, weight, query, saved, lam, *refs):
+def close_kernel(at, extra, late, plan, acc, piece, weight, query, saved, lam, other, *refs):
     if late:
-        gconv, gquery, packet, gate = refs
+        residues, (gconv, gquery, packet, products, gate) = other, refs
     else:
-        later, gconv, gquery, packet, gate = refs
+        later, (gconv, gquery, packet, gate) = other, refs
     tokens = piece.shape[0]
     first = tokens if late else 0
     width = weight.shape[0]
@@ -146,7 +147,10 @@
         conv = grad * query[there, :]
         gconv[here, :] = conv
         gquery[here, :] = grad * saved[there, :]
-        return tuple(lam[m] * state[m] + conv for m in range(poles))
+        state = tuple(lam[m] * state[m] + conv for m in range(poles))
+        if late:
+            products[here, :] = tree_sum([residues[m] * state[m] for m in range(poles)])
+        return state
 
     if late:
         state = (jnp.zeros((ROWS, LANES), jnp.float32),) * poles
@@ -162,27 +166,24 @@
             packet[poles + extra - 1 + row] = gquery[tile(row), :]
 
 
-def close_gate(plan, at, acc, piece, weight, query, saved, lam, extra, later=None):
+def close_gate(plan, at, acc, piece, weight, query, saved, lam, extra, residues=None, later=None):
     tokens, deep = piece.shape
     width = weight.shape[0]
     poles = lam.shape[0]
     late = later is None
-    flat = (tokens * ROWS, LANES)
+    flat = jax.ShapeDtypeStruct((tokens * ROWS, LANES), jnp.float32)
     packed = (poles if late else poles + 2 * extra - 1, ROWS, LANES)
+    outs = [flat, flat, jax.ShapeDtypeStruct(packed, jnp.float32)] + [flat] * late
     return pl.pallas_call(
         functools.partial(close_kernel, at, extra, late),
-        in_specs=[SMEM] + [VMEM] * (6 if late else 7),
-        out_specs=[VMEM] * 3,
-        out_shape=[
-            jax.ShapeDtypeStruct(flat, jnp.float32),
-            jax.ShapeDtypeStruct(flat, jnp.float32),
-            jax.ShapeDtypeStruct(packed, jnp.float32),
-        ],
-        scratch_shapes=[pltpu.VMEM(flat, jnp.float32)],
+        in_specs=[SMEM] + [VMEM] * 7,
+        out_specs=[VMEM] * len(outs),
+        out_shape=outs,
+        scratch_shapes=[pltpu.VMEM(flat.shape, jnp.float32)],
         compiler_params=pltpu.CompilerParams(vmem_limit_bytes=GRANT),
         cost_estimate=SMALL,
         name="close_gate",
-    )(plan, acc, piece, weight, query, saved, lam, *([] if late else [later]))
+    )(plan, acc, piece, weight, query, saved, lam, residues if late else later)
 
 
 def fold_kernel(plan, own, other, span, chip):
@@ -207,18 +208,86 @@
     )(plan, own, other, span)
 
 
+def filtered(filters, which, now, later):
+    return tree_sum(
+        [filters[which, 0] * now]
+        + [filters[which, lag + 1] * value for lag, value in enumerate(later)]
+    )
+
+
+def gather_rows(spread, out, first, tokens):
+    for group in range(out.shape[-1] // LANES):
+        out[pl.ds(first, tokens), pl.ds(group * LANES, LANES)] = spread[
+            pl.ds(first * ROWS + group, tokens, stride=ROWS), :
+        ].astype(out.dtype)
+
+
+def settle_kernel(
+    taps, later, late_conv, late_query, early_conv, early_query, lam, residues, filters,
+    products, passed, queries, spread,
+):
+    extra = taps - 1
+    half = late_conv.shape[0] // ROWS
+    poles = lam.shape[0]
+
+    def late_body(n, after):
+        token = half - TAIL - 1 - n
+        now = late_query[tile(token), :]
+        spread[tile(half + token), :] = filtered(filters, 0, now, after)
+        return (now,) + after[:-1]
+
+    after = tuple(late_query[tile(half - TAIL + row), :] for row in range(extra))
+    after = lax.fori_loop(0, half - TAIL, late_body, after, unroll=8)
+
+    def body(n, carry):
+        state, after = carry
+        here = tile(half - 1 - n)
+        conv = early_conv[here, :]
+        passed[here, :] = conv
+        passed[tile(2 * half - 1 - n), :] = late_conv[here, :]
+        state = tuple(lam[m] * state[m] + conv for m in range(poles))
+        products[here, :] = tree_sum([residues[m] * state[m] for m in range(poles)])
+        now = early_query[here, :]
+        spread[here, :] = filtered(filters, 0, now, after)
+        return state, (now,) + after[:-1]
+
+    state = tuple(later[m] for m in range(poles))
+    lax.fori_loop(0, half, body, (state, after), unroll=8)
+    gather_rows(spread, queries, 0, 2 * half - TAIL)
+
+
+def settle(later, late_conv, late_query, early_conv, early_query, lam, residues, filters, width):
+    taps = filters.shape[1]
+    half = late_conv.shape[0] // ROWS
+    return pl.pallas_call(
+        functools.partial(settle_kernel, taps),
+        in_specs=[VMEM] * 8,
+        out_specs=[VMEM] * 3,
+        out_shape=[
+            jax.ShapeDtypeStruct(early_conv.shape, jnp.float32),
+            jax.ShapeDtypeStruct((2 * half * ROWS, LANES), jnp.float32),
+            jax.ShapeDtypeStruct((2 * half, width), jnp.bfloat16),
+        ],
+        scratch_shapes=[pltpu.VMEM((2 * half * ROWS, LANES), jnp.float32)],
+        compiler_params=pltpu.CompilerParams(vmem_limit_bytes=GRANT),
+        cost_estimate=SMALL,
+        name="settle",
+    )(later, late_conv, late_query, early_conv, early_query, lam, residues, filters)
+
+
 def scan_kernel(
-    at_plan, taps, chips, plan, late_conv, late_query, early_conv, early_query, key_acts, value_acts,
-    lam, rate, residues, filters, kv_halo, own, other, *refs,
+    at_plan, taps, chips, plan, late_products, early_products, queries, late_query, key_acts,
+    value_acts, lam, rate, residues, filters, kv_halo, own, other, *refs,
 ):
     arrived = refs[:chips - 1]
-    weight, proj, chunk, chunk_rest, entering, passed, spread, buffer, sem = refs[chips - 1:]
+    weight, proj, chunk, chunk_rest, entering, spread, buffer, sem = refs[chips - 1:]
     extra = taps - 1
     tokens, width = proj.shape[1:]
+    half = tokens // 2
     poles = lam.shape[0]
-    deep = buffer.shape[1]
+    rows = 2 * chunk.shape[0]
     copy = pltpu.make_async_copy(
-        weight.at[:, pl.ds(pl.multiple_of(plan[at_plan] * deep, deep), deep), :], buffer, sem
+        weight.at[:, pl.ds(pl.multiple_of(plan[at_plan] * rows, rows), rows), :], buffer, sem
     )
     copy.start()
 
@@ -246,48 +315,66 @@
         halo.append(value)
 
     state = [entering[m] for m in range(poles)]
-    keys, values, queries = [], [], []
+    parts = tuple(residues[m] * state[m] for m in range(poles))
+    keys, values, after = [], [], []
     for row in range(extra):
         if row:
             state = [(state[m] - halo[row - 1]) * jnp.exp(rate[m]) for m in range(poles)]
         product = tree_sum([residues[m] * state[m] for m in range(poles)])
         keys.append(product * kv_halo[1, row])
         values.append(product * kv_halo[0, row])
-        queries.append(halo[extra - 1 + row])
-
-    half = tokens // 2
-
-    def body(first, gconv, gquery, n, carry):
-        state, later = carry
-        here = tile(half - 1 - n)
-        at = tile(first + half - 1 - n)
-        conv = gconv[here, :]
-        passed[at, :] = conv
-        state = tuple(lam[m] * state[m] + conv for m in range(poles))
-        product = tree_sum([residues[m] * state[m] for m in range(poles)])
-        now = (gquery[here, :], product * value_acts[at, :], product * key_acts[at, :])
-        for which in range(3):
-            spread[which, at, :] = tree_sum(
-                [filters[which, 0] * now[which]]
-                + [filters[which, lag] * later[which][lag - 1] for lag in range(1, taps)]
-            )
-        return state, tuple((now[which],) + later[which][:-1] for which in range(3))
-
-    carry = (
-        tuple(entering[m] for m in range(poles)),
-        (tuple(queries), tuple(keys), tuple(values)),
-    )
-    for first, gconv, gquery in ((half, late_conv, late_query), (0, early_conv, early_query)):
-        carry = lax.fori_loop(
-            0, half, functools.partial(body, first, gconv, gquery), carry, unroll=8
-        )
-    for which in range(3):
-        for group in range(width // LANES):
-            proj[which, :, pl.ds(group * LANES, LANES)] = spread[
-                which, pl.ds(group, tokens, stride=ROWS), :
-            ].astype(jnp.bfloat16)
+        after.append(halo[extra - 1 + row])
+
+    for token in range(tokens - 1, tokens - TAIL - 1, -1):
+        now = late_query[pl.ds((token - half) * ROWS, ROWS), :]
+        spread[0, pl.ds(token * ROWS, ROWS), :] = filtered(filters, 0, now, after)
+        after = [now] + after[:-1]
+    proj[0, pl.ds(0, tokens - TAIL), :] = queries[pl.ds(0, tokens - TAIL), :]
+    gather_rows(spread.at[0], proj.at[0], tokens - TAIL, TAIL)
+
+    def body(first, products, n, carry):
+        parts, later = carry
+        token = half - 1 - n
+        at = tile(first + token)
+        parts = tuple(lam[m] * parts[m] for m in range(poles))
+        product = products[tile(token), :] + tree_sum(parts)
+        now = (product * value_acts[at, :], product * key_acts[at, :])
+        for which in range(2):
+            spread[1 + which, at, :] = filtered(filters, 1 + which, now[which], later[which])
+        return parts, tuple((now[which],) + later[which][:-1] for which in range(2))
+
+    carry = (parts, (tuple(keys), tuple(values)))
+    for first, products in ((half, late_products), (0, early_products)):
+        carry = lax.fori_loop(0, half, functools.partial(body, first, products), carry, unroll=8)
+    for which in range(1, 3):
+        gather_rows(spread.at[which], proj.at[which], 0, tokens)
     copy.wait()
     project_rows(buffer, proj, (chunk, chunk_rest))
+
+
+def scan_block(plan, at, settled, keys, values, lam, rate, residues, filters, kv_halo, own, other,
+               arrived, weight, deep, width):
+    tokens = keys.shape[0] // ROWS
+    taps = filters.shape[1]
+    return pl.pallas_call(
+        functools.partial(scan_kernel, at, taps, len(arrived) + 1),
+        in_specs=[SMEM] + [VMEM] * (13 + len(arrived)) + [HBM],
+        out_specs=[VMEM] * 4,
+        out_shape=[
+            jax.ShapeDtypeStruct((3, tokens, width), jnp.bfloat16),
+            jax.ShapeDtypeStruct((deep // 2, tokens), jnp.bfloat16),
+            jax.ShapeDtypeStruct((deep // 2, tokens), jnp.bfloat16),
+            jax.ShapeDtypeStruct(lam.shape, jnp.float32),
+        ],
+        scratch_shapes=[
+            pltpu.VMEM((3, tokens * ROWS, LANES), jnp.float32),
+            pltpu.VMEM((3, deep, width), jnp.bfloat16),
+            pltpu.SemaphoreType.DMA,
+        ],
+        compiler_params=pltpu.CompilerParams(vmem_limit_bytes=GRANT),
+        cost_estimate=SMALL,
+        name="scan",
+    )(plan, *settled, keys, values, lam, rate, residues, filters, kv_halo, own, other, *arrived, weight)
 
 
 def project_rows(weight, proj, outs):
@@ -305,33 +392,6 @@
             out[pl.ds(start, block), :] = value.astype(out.dtype)
 
 
-def scan_block(plan, at, gated, keys, values, lam, rate, residues, filters, kv_halo, own, other,
-               arrived, weight, deep, width):
-    tokens = keys.shape[0] // ROWS
-    taps = filters.shape[1]
-    return pl.pallas_call(
-        functools.partial(scan_kernel, at, taps, len(arrived) + 1),
-        in_specs=[SMEM] + [VMEM] * (13 + len(arrived))
-        + [HBM],
-        out_specs=[VMEM] * 5,
-        out_shape=[
-            jax.ShapeDtypeStruct((3, tokens, width), jnp.bfloat16),
-            jax.ShapeDtypeStruct((deep // 2, tokens), jnp.bfloat16),
-            jax.ShapeDtypeStruct((deep // 2, tokens), jnp.bfloat16),
-            jax.ShapeDtypeStruct(lam.shape, jnp.float32),
-            jax.ShapeDtypeStruct(keys.shape, jnp.float32),
-        ],
-        scratch_shapes=[
-            pltpu.VMEM((3, tokens * ROWS, LANES), jnp.float32),
-            pltpu.VMEM((3, deep, width), jnp.bfloat16),
-            pltpu.SemaphoreType.DMA,
-        ],
-        compiler_params=pltpu.CompilerParams(vmem_limit_bytes=GRANT),
-        cost_estimate=SMALL,
-        name="scan",
-    )(plan, *gated, keys, values, lam, rate, residues, filters, kv_halo, own, other, *arrived, weight)
-
-
 def add_up_residues(gconv, product, lam, entering, total):
     tokens = gconv.shape[0] // ROWS
     poles = lam.shape[0]
@@ -350,25 +410,21 @@
         total[m] = sums[m]
 
 
-def project_kernel(at, count, with_total, plan, proj, weight, *refs):
-    if with_total:
-        sources, refs = refs[:4], refs[4:]
-    outs, refs = refs[:2 * count], refs[2 * count:]
-    if with_total:
-        total, refs = refs[0], refs[1:]
-    buffer, sems = refs
+def project_kernel(at, count, sources, plan, proj, weight, *refs):
+    if sources:
+        add_up = functools.partial(add_up_residues, *refs[:sources + 1])
+        refs = refs[sources + 1:]
+    outs, (buffer, sems) = refs[:2 * count], refs[2 * count:]
     deep = buffer.shape[2]
-    copies = [
-        pltpu.make_async_copy(
-            weight.at[:, pl.ds(pl.multiple_of(plan[at + i] * deep, deep), deep), :],
-            buffer.at[i], sems.at[i],
+    copies = []
+    for i in range(count):
+        start = pl.multiple_of(plan[at + i] * deep, deep)
+        copies.append(
+            pltpu.make_async_copy(weight.at[:, pl.ds(start, deep), :], buffer.at[i], sems.at[i])
         )
-        for i in range(count)
-    ]
-    for copy in copies:
-        copy.start()
-    if with_total:
-        add_up_residues(*sources, total)
+        copies[-1].start()
+    if sources:
+        add_up()
     for i in range(count):
         copies[i].wait()
         project_rows(buffer.at[i], proj, outs[2 * i:2 * i + 2])
@@ -378,9 +434,9 @@
     _, tokens, width = proj.shape
     outs = [jax.ShapeDtypeStruct((deep // 2, tokens), jnp.bfloat16)] * (2 * count)
     if sources:
-        outs.append(jax.ShapeDtypeStruct(sources[-1].shape, jnp.float32))
+        outs = [jax.ShapeDtypeStruct(sources[-1].shape, jnp.float32)] + outs
     return pl.pallas_call(
-        functools.partial(project_kernel, at, count, bool(sources)),
+        functools.partial(project_kernel, at, count, len(sources)),
         in_specs=[SMEM, VMEM, HBM] + [VMEM] * len(sources),
         out_specs=[VMEM] * len(outs),
         out_shape=outs,
@@ -533,16 +589,19 @@
             odds[1], kv_halo, last_weight, query, keys, values, saved, product = tie(
                 odds[1], kv_halo, last_weight, query, keys, values, saved, product
             )
-    late_conv, late_query, later = close_gate(
-        plan, 1, acc, evens[0], last_weight, query, saved, lam, extra
+    late_conv, late_query, later, late_products = close_gate(
+        plan, 1, acc, evens[0], last_weight, query, saved, lam, extra, residues=res
     )
     early_conv, early_query, packet = close_gate(
-        plan, 1, acc, evens[1], last_weight, query, saved, lam, extra, later
+        plan, 1, acc, evens[1], last_weight, query, saved, lam, extra, later=later
     )
 
     other = swap_ctx(packet, 1, blocks)
     chip = fold(plan, packet, other, span)
     arrived = [swap_ctx(chip, 2 * mask, blocks) for mask in range(1, blocks // 2)]
+    early_products, gconv, queries = settle(
+        later, late_conv, late_query, early_conv, early_query, lam, res, filters, width
+    )
 
     def added(*parts):
         return sum(value.astype(f32) for value in parts if value is not None).astype(bf16)
@@ -550,15 +609,15 @@
     def masked(value):
         return None if value is None else jnp.where(edge, jnp.zeros_like(value), value)
 
-    proj, *part, entering, gconv = scan_block(
-        plan, places["first"], [late_conv, late_query, early_conv, early_query], keys, values, lam,
-        rate, res, filters, kv_halo, packet, other, arrived, in_weight, deep, width,
+    proj, *part, entering = scan_block(
+        plan, places["first"], [late_products, early_products, queries, late_query], keys, values,
+        lam, rate, res, filters, kv_halo, packet, other, arrived, in_weight, deep, width,
+    )
+    total, *parts = project(
+        plan, places["chunks"], 1, proj, in_weight, deep, [gconv, product, lam, entering]
     )
     for_even, for_odd = {1: part}, {2: part}
     evens, odds = [swap_even(piece, count) for piece in part], [None, None]
-    *parts, total = project(
-        plan, places["chunks"], 1, proj, in_weight, deep, [gconv, product, lam, entering]
-    )
     evens[0], proj, total, *parts = tie(
         evens[0], proj, total, *parts
     )

time: 98.5 us -> 97.1 us (0.986)
  waiting for transfers between devices: 25.2 us -> 22.6 us
  Pallas kernels: 35.4 us -> 36.5 us
    ppermute x7, waiting for transfers between devices: 10 us -> 8.16 us  [swap_ctx(): return lax.ppermute(value, 'ctx', [(i, i ^ mask) for i in range(blocks)])]
    pallas_call x2 -> x3, Pallas kernels: 12.2 us -> 14 us  [the longest x2 12.2 us: project(): pl.pallas_call(functools.partial(project_kernel, at, count, len(sources))...]
    pallas_call x1, Pallas kernels: 6.53 us -> 5.17 us  [scan_block(): pl.pallas_call(functools.partial(scan_kernel, at, taps, len(arrived) + 1)...]
  transfers between devices with their start and end apart: 28 -> 28, of which waited for: 14 -> 13; matrix products, arithmetic and copies ran while one was open for 8% -> 8% of each run, Pallas kernels for 27% -> 30%
where the time goes in v4:
time: 97.1 us; the launch traced here: 96.5 us
  Pallas kernels  36.5 us (38%)
  starting transfers between devices  26.9 us (28%)
  waiting for transfers between devices  22.6 us (23%)
  local copies, waits for them, and re-layouts  6.23 us (6%)
  other arithmetic  3.18 us (3%)
  between operations  1.07 us (1%)
    ppermute x12, starting transfers between devices, swap_even(): return lax.ppermute(value, 'chan', [(i, i ^ 1) for i in range(count)])  18.5 us
    ppermute x12, waiting for transfers between devices, swap_even(): return lax.ppermute(value, 'chan', [(i, i ^ 1) for i in range(count)])  14.5 us
    pallas_call x2, Pallas kernels, project(): pl.pallas_call(functools.partial(project_kernel, at, count, len(sources))...  12.2 us
    pallas_call x3, Pallas kernels, gate_step(): pl.pallas_call(functools.partial(gate_kernel, at, has_acc, shards, len(pi...  10.4 us
    ppermute x7, waiting for transfers between devices, swap_ctx(): return lax.ppermute(value, 'ctx', [(i, i ^ mask) for i in range(blocks)])  8.16 us
    ppermute x7, starting transfers between devices, swap_ctx(): return lax.ppermute(value, 'ctx', [(i, i ^ mask) for i in range(blocks)])  6.55 us
    pallas_call x1, Pallas kernels, scan_block(): pl.pallas_call(functools.partial(scan_kernel, at, taps, len(arrived) + 1)...  5.17 us
    pallas_call x2, Pallas kernels, close_gate(): pl.pallas_call(functools.partial(close_kernel, at, extra, late), in_specs...  4.94 us
  transfers between devices with their start and end apart: 28, of which 13 were waited for; matrix products, arithmetic and copies ran while one was open for 8% of the time, Pallas kernels for 30%

profile of v4, /device:TPU:0, one launch (start us, length us, event | category | flops | bytes accessed | tf_op | source)
XLA Modules:
  0.0 96.5 jit_solution(293977648436746637)
XLA Ops:
  2.2 4.1 %collective-permute-start = (bf16[128,1024]{1,0:T(8,128)(2,1)S(1)}, bf16[128,1024]{1,0:T(8,128)(2,1)S(1)}, u32[]{:S(2)}, u32[]{:S(2)}) collective-permute-start(bf16[128,1024]{1,0:T(8,128)(2,1)S(1)} %slice.11), channel_id=1, source_target_pairs={{0,1},{1,0},{2,3},{3,2},{4,5},{5,4},{6,7},{7,6},{8,9},{9,8},{10,11... | collective-permute-start | bytes 786440 | tf_op jit(solution)/shard_map/ppermute | solution.py:471
  12.4 1.7 %collective-permute-start.2 = (bf16[128,1024]{1,0:T(8,128)(2,1)S(1)}, bf16[128,1024]{1,0:T(8,128)(2,1)S(1)}, u32[]{:S(2)}, u32[]{:S(2)}) collective-permute-start(bf16[128,1024]{1,0:T(8,128)(2,1)S(1)} %collective-permute-done.1.refs_4_), channel_id=1, source_target_pairs={{0,1},{1,0},{2,3},{3,2},{4,5},{5,4},{6,7},{7,6},{8,9},{9,8},{10,11... | collective-permute-start | bytes 786440 | tf_op jit(solution)/shard_map/ppermute | solution.py:471
  14.1 2.9 %gate_step.3.refs_0_ = f32[256,1024]{1,0:T(8,128)S(1)} custom-call(s32[14]{0:T(128)S(1)} %stack.65.plan, bf16[256,1024]{1,0:T(8,128)(2,1)S(1)} %copy-done, bf16[1024,4096]{1,0:T(8,128)(2,1)} %refs_5_.3), custom_call_target="tpu_custom_call" | custom-call | flops 1 | bytes 1 | tf_op jit(solution)/shard_map/gate_step/pallas_call | solution.py:105
  17.1 2.4 %collective-permute-done.4.refs_1_ = bf16[128,1024]{1,0:T(8,128)(2,1)} collective-permute-done((bf16[128,1024]{1,0:T(8,128)(2,1)S(1)}, bf16[128,1024]{1,0:T(8,128)(2,1)}, u32[]{:S(2)}, u32[]{:S(2)}) %collective-permute-start.4) | collective-permute-done | bytes 262176 | tf_op jit(solution)/shard_map/ppermute | solution.py:471
  19.5 2.0 %collective-permute-start.6 = (bf16[128,1024]{1,0:T(8,128)(2,1)S(1)}, bf16[128,1024]{1,0:T(8,128)(2,1)}, u32[]{:S(2)}, u32[]{:S(2)}) collective-permute-start(bf16[128,1024]{1,0:T(8,128)(2,1)S(1)} %collective-permute-done.5.refs_3_), channel_id=1, source_target_pairs={{0,1},{1,0},{2,3},{3,2},{4,5},{5,4},{6,7},{7,6},{8,9},{9,8},{10,11... | collective-permute-start | bytes 786440 | tf_op jit(solution)/shard_map/ppermute | solution.py:471
  21.5 4.0 %gate_step.4.refs_0_ = f32[256,1024]{1,0:T(8,128)S(1)} custom-call(s32[14]{0:T(128)S(1)} %stack.65.plan, f32[256,1024]{1,0:T(8,128)S(1)} %gate_step.3.refs_0_, bf16[128,1024]{1,0:T(8,128)(2,1)} %collective-permute-done.4.refs_1_, bf16[128,1024]{1,0:T(8,128)(2,1)S(1)} %collective-permute-done.refs_2_, bf16[128,1024]{1,0:T(8,128)(2,1)S(1)} %collective-permute-done.5.refs_3_, ...), custom_call_target="tpu_custom_call" | custom-call | flops 1 | bytes 1 | tf_op jit(solution)/shard_map/gate_step/pallas_call | solution.py:105
  27.1 1.8 %constant_dynamic-slice_fusion.weight = bf16[1024,1024]{1,0:T(8,128)(2,1)S(1)} fusion(bf16[1024,4096]{1,0:T(8,128)(2,1)} %refs_5_.3, s32[]{:T(128)S(6)} %select_n.93), kind=kLoop, calls=%fused_computation.15 | loop fusion | bytes 4194308 | tf_op jit(solution)/shard_map/dynamic_slice | solution.py:587
  28.9 1.6 %collective-permute-start.9 = (bf16[128,1024]{1,0:T(8,128)(2,1)}, bf16[128,1024]{1,0:T(8,128)(2,1)S(1)}, u32[]{:S(2)}, u32[]{:S(2)}) collective-permute-start(bf16[128,1024]{1,0:T(8,128)(2,1)} %collective-permute-done.3.refs_4_), channel_id=1, source_target_pairs={{0,1},{1,0},{2,3},{3,2},{4,5},{5,4},{6,7},{7,6},{8,9},{9,8},{10,11... | collective-permute-start | bytes 786440 | tf_op jit(solution)/shard_map/ppermute | solution.py:471
  32.6 3.5 %gate_step.5.acc = f32[256,1024]{1,0:T(8,128)S(1)} custom-call(s32[14]{0:T(128)S(1)} %stack.65.plan, f32[256,1024]{1,0:T(8,128)S(1)} %gate_step.4.refs_0_, bf16[128,1024]{1,0:T(8,128)(2,1)} %collective-permute-done.6.refs_1_, bf16[128,1024]{1,0:T(8,128)(2,1)S(1)} %collective-permute-done.2.refs_2_, bf16[128,1024]{1,0:T(8,128)(2,1)} %collective-permute-done.7.refs_3_, ...), custom_call_target="tpu_custom_call" | custom-call | flops 1 | bytes 1 | tf_op jit(solution)/shard_map/gate_step/pallas_call | solution.py:105
  36.0 2.3 %collective-permute-done.9.piece = bf16[128,1024]{1,0:T(8,128)(2,1)S(1)} collective-permute-done((bf16[128,1024]{1,0:T(8,128)(2,1)}, bf16[128,1024]{1,0:T(8,128)(2,1)S(1)}, u32[]{:S(2)}, u32[]{:S(2)}) %collective-permute-start.9) | collective-permute-done | bytes 262176 | tf_op jit(solution)/shard_map/ppermute | solution.py:471
  38.4 2.9 %close_gate.2 = (f32[1024,128]{1,0:T(8,128)S(1)}, f32[1024,128]{1,0:T(8,128)S(1)}, f32[16,8,128]{2,1,0:T(8,128)S(1)}, f32[1024,128]{1,0:T(8,128)S(1)}) custom-call(s32[14]{0:T(128)S(1)} %stack.65.plan, f32[256,1024]{1,0:T(8,128)S(1)} %gate_step.5.acc, bf16[128,1024]{1,0:T(8,128)(2,1)S(1)} %collective-permute-done.9.piece, ...), custom_call_target="tpu_custom_call" | custom-call | flops 1 | bytes 1 | tf_op jit(solution)/shard_map/close_gate/pallas_call | solution.py:177
  42.8 2.0 %close_gate.3 = (f32[1024,128]{1,0:T(8,128)S(1)}, f32[1024,128]{1,0:T(8,128)S(1)}, f32[19,8,128]{2,1,0:T(8,128)S(1)}) custom-call(s32[14]{0:T(128)S(1)} %stack.65.plan, f32[256,1024]{1,0:T(8,128)S(1)} %gate_step.5.acc, bf16[128,1024]{1,0:T(8,128)(2,1)S(1)} %collective-permute-done.10.piece, bf16[1024,1024]{1,0:T(8,128)(2,1)S(1)} %constant_dynamic-slice_fusion.weight, ...), custom_call_target="tpu_custom_call" | custom-call | flops 1 | bytes 1 | tf_op jit(solution)/shard_map/close_gate/pallas_call | solution.py:177
  46.8 2.5 %collective-permute-start.14 = (bf16[19,8,128]{2,1,0:T(8,128)(2,1)S(1)}, bf16[19,8,128]{2,1,0:T(8,128)(2,1)S(1)}, u32[]{:S(2)}, u32[]{:S(2)}) collective-permute-start(bf16[19,8,128]{2,1,0:T(8,128)(2,1)S(1)} %fold.1), channel_id=1, source_target_pairs={{0,24},{4,28},{8,16},{12,20},{16,8},{20,12},{24,0},{28,4},{1,25},{... | collective-permute-start | bytes 116744 | tf_op jit(solution)/shard_map/ppermute | solution.py:487
  50.3 1.8 %settle.1 = (f32[1024,128]{1,0:T(8,128)S(1)}, f32[2048,128]{1,0:T(8,128)S(1)}, bf16[256,1024]{1,0:T(8,128)(2,1)S(1)}) custom-call(f32[16,8,128]{2,1,0:T(8,128)S(1)} %get-tuple-element.94.other.later, f32[1024,128]{1,0:T(8,128)S(1)} %get-tuple-element.95.late_conv, f32[1024,128]{1,0:T(8,128)S(1)} %get-tuple-element.96.late_query, ...), custom_call_target="tpu_custom_call" | custom-call | flops 1 | bytes 1 | tf_op jit(solution)/shard_map/settle/pallas_call | solution.py:262
  53.8 5.2 %scan.1 = (bf16[3,256,1024]{2,1,0:T(8,128)(2,1)S(1)}, bf16[512,256]{1,0:T(8,128)(2,1)S(1)}, bf16[512,256]{1,0:T(8,128)(2,1)S(1)}, f32[16,8,128]{2,1,0:T(8,128)S(1)}) custom-call(s32[14]{0:T(128)S(1)} %stack.65.plan, f32[1024,128]{1,0:T(8,128)S(1)} %get-tuple-element.93.late_products, f32[1024,128]{1,0:T(8,128)S(1)} %get-tuple-element.100.early_products, ...), custom_call_target="tpu_custom_call" | custom-call | flops 1 | bytes 1 | tf_op jit(solution)/shard_map/scan/pallas_call | solution.py:359
  61.0 5.2 %project.2 = (f32[16,8,128]{2,1,0:T(8,128)S(1)}, bf16[512,256]{1,0:T(8,128)(2,1)S(1)}, bf16[512,256]{1,0:T(8,128)(2,1)S(1)}) custom-call(s32[14]{0:T(128)S(1)} %stack.65.plan, bf16[3,256,1024]{2,1,0:T(8,128)(2,1)S(1)} %get-tuple-element.116.proj, bf16[3,4096,1024]{2,1,0:T(8,128)(2,1)} %weight.3, f32[2048,128]{1,0:T(8,128)S(1)} %get-tuple-element.110.refs_0_, ...), custom_call_target="tpu_custom_call" | custom-call | flops 1610612736 | bytes 6291456 | tf_op jit(solution)/shard_map/project/pallas_call | solution.py:438
  66.2 2.0 %collective-permute-done.15 = bf16[512,256]{1,0:T(8,128)(2,1)S(1)} collective-permute-done((bf16[512,256]{1,0:T(8,128)(2,1)S(1)}, bf16[512,256]{1,0:T(8,128)(2,1)S(1)}, u32[]{:S(2)}, u32[]{:S(2)}) %collective-permute-start.15) | collective-permute-done | bytes 262176 | tf_op jit(solution)/shard_map/ppermute | solution.py:471
  68.4 1.9 %collective-permute-start.16 = (bf16[512,256]{1,0:T(8,128)(2,1)S(1)}, bf16[512,256]{1,0:T(8,128)(2,1)S(1)}, u32[]{:S(2)}, u32[]{:S(2)}) collective-permute-start(bf16[512,256]{1,0:T(8,128)(2,1)S(1)} %get-tuple-element.119), channel_id=1, source_target_pairs={{0,1},{1,0},{2,3},{3,2},{4,5},{5,4},{6,7},{7,6},{8,9},{9,8},{10,11... | collective-permute-start | bytes 786440 | tf_op jit(solution)/shard_map/ppermute | solution.py:471
  71.4 7.0 %project.3 = (bf16[512,256]{1,0:T(8,128)(2,1)S(1)}, bf16[512,256]{1,0:T(8,128)(2,1)S(1)}, bf16[512,256]{1,0:T(8,128)(2,1)S(1)}, bf16[512,256]{1,0:T(8,128)(2,1)S(1)}) custom-call(s32[14]{0:T(128)S(1)} %stack.65.plan, bf16[3,256,1024]{2,1,0:T(8,128)(2,1)S(1)} %get-tuple-element.116.proj, bf16[3,4096,1024]{2,1,0:T(8,128)(2,1)} %weight.3), custom_call_target="tpu_custom_call" | custom-call | flops 3221225472 | bytes 12582912 | tf_op jit(solution)/shard_map/project/pallas_call | solution.py:438
  79.2 1.9 %collective-permute-start.18 = (bf16[512,256]{1,0:T(8,128)(2,1)S(1)}, bf16[512,256]{1,0:T(8,128)(2,1)S(1)}, u32[]{:S(2)}, u32[]{:S(2)}) collective-permute-start(bf16[512,256]{1,0:T(8,128)(2,1)S(1)} %add_convert_fusion.6), channel_id=1, source_target_pairs={{0,1},{1,0},{2,3},{3,2},{4,5},{5,4},{6,7},{7,6},{8,9},{9,8},{10,11... | collective-permute-start | bytes 786440 | tf_op jit(solution)/shard_map/ppermute | solution.py:471
  81.3 1.8 %collective-permute-done.20 = bf16[512,256]{1,0:T(8,128)(2,1)S(1)} collective-permute-done((bf16[512,256]{1,0:T(8,128)(2,1)S(1)}, bf16[512,256]{1,0:T(8,128)(2,1)S(1)}, u32[]{:S(2)}, u32[]{:S(2)}) %collective-permute-start.20) | collective-permute-done | bytes 262176 | tf_op jit(solution)/shard_map/ppermute | solution.py:471
  84.0 3.4 %collective-permute-done.26 = f32[16,8,128]{2,1,0:T(8,128)S(1)} collective-permute-done((f32[16,8,128]{2,1,0:T(8,128)S(1)}, f32[16,8,128]{2,1,0:T(8,128)S(1)}, u32[]{:S(2)}, u32[]{:S(2)}) %collective-permute-start.26) | collective-permute-done | bytes 65568 | tf_op jit(solution)/shard_map/ppermute | solution.py:487
  89.9 1.8 %collective-permute-done.27 = f32[16,8,128]{2,1,0:T(8,128)S(1)} collective-permute-done((f32[16,8,128]{2,1,0:T(8,128)S(1)}, f32[16,8,128]{2,1,0:T(8,128)S(1)}, u32[]{:S(2)}, u32[]{:S(2)}) %collective-permute-start.27) | collective-permute-done | bytes 65568 | tf_op jit(solution)/shard_map/ppermute | solution.py:487
  92.5 3.1 %collective-permute-done.23 = bf16[512,256]{1,0:T(8,128)(2,1)S(1)} collective-permute-done((bf16[512,256]{1,0:T(8,128)(2,1)S(1)}, bf16[512,256]{1,0:T(8,128)(2,1)S(1)}, u32[]{:S(2)}, u32[]{:S(2)}) %collective-permute-start.23) | collective-permute-done | bytes 262176 | tf_op jit(solution)/shard_map/ppermute | solution.py:471
  (73 shorter events, 26.5 us)
Async XLA Ops:
  1.7 10.2 %collective-permute-start.1 = (bf16[128,1024]{1,0:T(8,128)(2,1)S(1)}, bf16[128,1024]{1,0:T(8,128)(2,1)S(1)}, u32[]{:S(2)}, u32[]{:S(2)}) collective-permute-start(bf16[128,1024]{1,0:T(8,128)(2,1)S(1)} %slice.11), channel_id=1, source_target_pairs={{0,4},{1,2},{2,1},{3,7},{4,0},{5,6},{6,5},{7,3},{8,12},{9,10},{10,... | collective-permute-start | bytes 786440 | tf_op jit(solution)/shard_map/ppermute | solution.py:483
  2.2 10.2 %collective-permute-start = (bf16[128,1024]{1,0:T(8,128)(2,1)S(1)}, bf16[128,1024]{1,0:T(8,128)(2,1)S(1)}, u32[]{:S(2)}, u32[]{:S(2)}) collective-permute-start(bf16[128,1024]{1,0:T(8,128)(2,1)S(1)} %slice.11), channel_id=1, source_target_pairs={{0,1},{1,0},{2,3},{3,2},{4,5},{5,4},{6,7},{7,6},{8,9},{9,8},{10,11... | collective-permute-start | bytes 786440 | tf_op jit(solution)/shard_map/ppermute | solution.py:471
  10.1 6.9 %collective-permute-start.5 = (bf16[128,1024]{1,0:T(8,128)(2,1)S(1)}, bf16[128,1024]{1,0:T(8,128)(2,1)S(1)}, u32[]{:S(2)}, u32[]{:S(2)}) collective-permute-start(bf16[128,1024]{1,0:T(8,128)(2,1)S(1)} %slice.12), channel_id=1, source_target_pairs={{0,4},{1,2},{2,1},{3,7},{4,0},{5,6},{6,5},{7,3},{8,12},{9,10},{10,... | collective-permute-start | bytes 786440 | tf_op jit(solution)/shard_map/ppermute | solution.py:483
  10.2 9.3 %collective-permute-start.4 = (bf16[128,1024]{1,0:T(8,128)(2,1)S(1)}, bf16[128,1024]{1,0:T(8,128)(2,1)}, u32[]{:S(2)}, u32[]{:S(2)}) collective-permute-start(bf16[128,1024]{1,0:T(8,128)(2,1)S(1)} %slice.12), channel_id=1, source_target_pairs={{0,1},{1,0},{2,3},{3,2},{4,5},{5,4},{6,7},{7,6},{8,9},{9,8},{10,11... | collective-permute-start | bytes 786440 | tf_op jit(solution)/shard_map/ppermute | solution.py:471
  12.4 13.2 %collective-permute-start.2 = (bf16[128,1024]{1,0:T(8,128)(2,1)S(1)}, bf16[128,1024]{1,0:T(8,128)(2,1)S(1)}, u32[]{:S(2)}, u32[]{:S(2)}) collective-permute-start(bf16[128,1024]{1,0:T(8,128)(2,1)S(1)} %collective-permute-done.1.refs_4_), channel_id=1, source_target_pairs={{0,1},{1,0},{2,3},{3,2},{4,5},{5,4},{6,7},{7,6},{8,9},{9,8},{10,11... | collective-permute-start | bytes 786440 | tf_op jit(solution)/shard_map/ppermute | solution.py:471
  14.1 11.4 %collective-permute-start.3 = (bf16[128,1024]{1,0:T(8,128)(2,1)S(1)}, bf16[128,1024]{1,0:T(8,128)(2,1)}, u32[]{:S(2)}, u32[]{:S(2)}) collective-permute-start(bf16[128,1024]{1,0:T(8,128)(2,1)S(1)} %collective-permute-done.refs_2_), channel_id=1, source_target_pairs={{0,4},{1,2},{2,1},{3,7},{4,0},{5,6},{6,5},{7,3},{8,12},{9,10},{10,... | collective-permute-start | bytes 786440 | tf_op jit(solution)/shard_map/ppermute | solution.py:483
  19.5 12.6 %collective-permute-start.7 = (bf16[128,1024]{1,0:T(8,128)(2,1)}, bf16[128,1024]{1,0:T(8,128)(2,1)}, u32[]{:S(2)}, u32[]{:S(2)}) collective-permute-start(bf16[128,1024]{1,0:T(8,128)(2,1)} %collective-permute-done.4.refs_1_), channel_id=1, source_target_pairs={{0,4},{1,2},{2,1},{3,7},{4,0},{5,6},{6,5},{7,3},{8,12},{9,10},{10,... | collective-permute-start | bytes 786440 | tf_op jit(solution)/shard_map/ppermute | solution.py:483
  19.5 12.6 %collective-permute-start.6 = (bf16[128,1024]{1,0:T(8,128)(2,1)S(1)}, bf16[128,1024]{1,0:T(8,128)(2,1)}, u32[]{:S(2)}, u32[]{:S(2)}) collective-permute-start(bf16[128,1024]{1,0:T(8,128)(2,1)S(1)} %collective-permute-done.5.refs_3_), channel_id=1, source_target_pairs={{0,1},{1,0},{2,3},{3,2},{4,5},{5,4},{6,7},{7,6},{8,9},{9,8},{10,11... | collective-permute-start | bytes 786440 | tf_op jit(solution)/shard_map/ppermute | solution.py:471
  26.4 5.7 %collective-permute-start.8 = (f32[2,2,8,128]{3,2,1,0:T(8,128)S(1)}, f32[2,2,8,128]{3,2,1,0:T(8,128)S(1)}, u32[]{:S(2)}, u32[]{:S(2)}) collective-permute-start(f32[2,2,8,128]{3,2,1,0:T(8,128)S(1)} %reshape.32), channel_id=1, source_target_pairs={{0,28},{4,0},{8,4},{12,8},{16,12},{20,16},{24,20},{28,24},{1,29},{... | collective-permute-start | bytes 49160 | tf_op jit(solution)/shard_map/ppermute | solution.py:583
  28.9 9.5 %collective-permute-start.9 = (bf16[128,1024]{1,0:T(8,128)(2,1)}, bf16[128,1024]{1,0:T(8,128)(2,1)S(1)}, u32[]{:S(2)}, u32[]{:S(2)}) collective-permute-start(bf16[128,1024]{1,0:T(8,128)(2,1)} %collective-permute-done.3.refs_4_), channel_id=1, source_target_pairs={{0,1},{1,0},{2,3},{3,2},{4,5},{5,4},{6,7},{7,6},{8,9},{9,8},{10,11... | collective-permute-start | bytes 786440 | tf_op jit(solution)/shard_map/ppermute | solution.py:471
  32.1 10.7 %collective-permute-start.10 = (bf16[128,1024]{1,0:T(8,128)(2,1)}, bf16[128,1024]{1,0:T(8,128)(2,1)S(1)}, u32[]{:S(2)}, u32[]{:S(2)}) collective-permute-start(bf16[128,1024]{1,0:T(8,128)(2,1)} %collective-permute-done.7.refs_3_), channel_id=1, source_target_pairs={{0,1},{1,0},{2,3},{3,2},{4,5},{5,4},{6,7},{7,6},{8,9},{9,8},{10,11... | collective-permute-start | bytes 786440 | tf_op jit(solution)/shard_map/ppermute | solution.py:471
  46.8 5.4 %collective-permute-start.14 = (bf16[19,8,128]{2,1,0:T(8,128)(2,1)S(1)}, bf16[19,8,128]{2,1,0:T(8,128)(2,1)S(1)}, u32[]{:S(2)}, u32[]{:S(2)}) collective-permute-start(bf16[19,8,128]{2,1,0:T(8,128)(2,1)S(1)} %fold.1), channel_id=1, source_target_pairs={{0,24},{4,28},{8,16},{12,20},{16,8},{20,12},{24,0},{28,4},{1,25},{... | collective-permute-start | bytes 116744 | tf_op jit(solution)/shard_map/ppermute | solution.py:487
  58.9 9.3 %collective-permute-start.15 = (bf16[512,256]{1,0:T(8,128)(2,1)S(1)}, bf16[512,256]{1,0:T(8,128)(2,1)S(1)}, u32[]{:S(2)}, u32[]{:S(2)}) collective-permute-start(bf16[512,256]{1,0:T(8,128)(2,1)S(1)} %get-tuple-element.108), channel_id=1, source_target_pairs={{0,1},{1,0},{2,3},{3,2},{4,5},{5,4},{6,7},{7,6},{8,9},{9,8},{10,11... | collective-permute-start | bytes 786440 | tf_op jit(solution)/shard_map/ppermute | solution.py:471
  60.1 11.2 %collective-permute-start.21 = (bf16[512,256]{1,0:T(8,128)(2,1)S(1)}, bf16[512,256]{1,0:T(8,128)(2,1)S(1)}, u32[]{:S(2)}, u32[]{:S(2)}) collective-permute-start(bf16[512,256]{1,0:T(8,128)(2,1)S(1)} %get-tuple-element.128), channel_id=1, source_target_pairs={{0,1},{1,0},{2,3},{3,2},{4,5},{5,4},{6,7},{7,6},{8,9},{9,8},{10,11... | collective-permute-start | bytes 786440 | tf_op jit(solution)/shard_map/ppermute | solution.py:471
  68.3 10.1 %collective-permute-start.17 = (bf16[512,256]{1,0:T(8,128)(2,1)S(1)}, bf16[512,256]{1,0:T(8,128)(2,1)S(1)}, u32[]{:S(2)}, u32[]{:S(2)}) collective-permute-start(bf16[512,256]{1,0:T(8,128)(2,1)S(1)} %add_convert_fusion.7), channel_id=1, source_target_pairs={{0,4},{1,2},{2,1},{3,7},{4,0},{5,6},{6,5},{7,3},{8,12},{9,10},{10,... | collective-permute-start | bytes 786440 | tf_op jit(solution)/shard_map/ppermute | solution.py:483
  68.4 10.1 %collective-permute-start.16 = (bf16[512,256]{1,0:T(8,128)(2,1)S(1)}, bf16[512,256]{1,0:T(8,128)(2,1)S(1)}, u32[]{:S(2)}, u32[]{:S(2)}) collective-permute-start(bf16[512,256]{1,0:T(8,128)(2,1)S(1)} %get-tuple-element.119), channel_id=1, source_target_pairs={{0,1},{1,0},{2,3},{3,2},{4,5},{5,4},{6,7},{7,6},{8,9},{9,8},{10,11... | collective-permute-start | bytes 786440 | tf_op jit(solution)/shard_map/ppermute | solution.py:471
  70.3 12.7 %collective-permute-start.20 = (bf16[512,256]{1,0:T(8,128)(2,1)S(1)}, bf16[512,256]{1,0:T(8,128)(2,1)S(1)}, u32[]{:S(2)}, u32[]{:S(2)}) collective-permute-start(bf16[512,256]{1,0:T(8,128)(2,1)S(1)} %get-tuple-element.127), channel_id=1, source_target_pairs={{0,1},{1,0},{2,3},{3,2},{4,5},{5,4},{6,7},{7,6},{8,9},{9,8},{10,11... | collective-permute-start | bytes 786440 | tf_op jit(solution)/shard_map/ppermute | solution.py:471
  71.4 11.7 %collective-permute-start.22 = (bf16[512,256]{1,0:T(8,128)(2,1)S(1)}, bf16[512,256]{1,0:T(8,128)(2,1)S(1)}, u32[]{:S(2)}, u32[]{:S(2)}) collective-permute-start(bf16[512,256]{1,0:T(8,128)(2,1)S(1)} %add_convert_fusion.3), channel_id=1, source_target_pairs={{0,4},{1,2},{2,1},{3,7},{4,0},{5,6},{6,5},{7,3},{8,12},{9,10},{10,... | collective-permute-start | bytes 786440 | tf_op jit(solution)/shard_map/ppermute | solution.py:483
  78.6 4.5 %collective-permute-start.25 = (f32[16,8,128]{2,1,0:T(8,128)S(1)}, f32[16,8,128]{2,1,0:T(8,128)S(1)}, u32[]{:S(2)}, u32[]{:S(2)}) collective-permute-start(f32[16,8,128]{2,1,0:T(8,128)S(1)} %get-tuple-element.131), channel_id=1, source_target_pairs={{0,4},{4,0},{8,12},{12,8},{16,20},{20,16},{24,28},{28,24},{1,5},{5... | collective-permute-start | bytes 196616 | tf_op jit(solution)/shard_map/ppermute | solution.py:487
  79.2 13.2 %collective-permute-start.18 = (bf16[512,256]{1,0:T(8,128)(2,1)S(1)}, bf16[512,256]{1,0:T(8,128)(2,1)S(1)}, u32[]{:S(2)}, u32[]{:S(2)}) collective-permute-start(bf16[512,256]{1,0:T(8,128)(2,1)S(1)} %add_convert_fusion.6), channel_id=1, source_target_pairs={{0,1},{1,0},{2,3},{3,2},{4,5},{5,4},{6,7},{7,6},{8,9},{9,8},{10,11... | collective-permute-start | bytes 786440 | tf_op jit(solution)/shard_map/ppermute | solution.py:471
  81.0 11.3 %collective-permute-start.19 = (bf16[512,256]{1,0:T(8,128)(2,1)S(1)}, bf16[512,256]{1,0:T(8,128)(2,1)S(1)}, u32[]{:S(2)}, u32[]{:S(2)}) collective-permute-start(bf16[512,256]{1,0:T(8,128)(2,1)S(1)} %add_convert_fusion.5), channel_id=1, source_target_pairs={{0,4},{1,2},{2,1},{3,7},{4,0},{5,6},{6,5},{7,3},{8,12},{9,10},{10,... | collective-permute-start | bytes 786440 | tf_op jit(solution)/shard_map/ppermute | solution.py:483
  83.1 4.3 %collective-permute-start.26 = (f32[16,8,128]{2,1,0:T(8,128)S(1)}, f32[16,8,128]{2,1,0:T(8,128)S(1)}, u32[]{:S(2)}, u32[]{:S(2)}) collective-permute-start(f32[16,8,128]{2,1,0:T(8,128)S(1)} %add.100), channel_id=1, source_target_pairs={{0,8},{4,12},{8,0},{12,4},{16,24},{20,28},{24,16},{28,20},{1,9},{5... | collective-permute-start | bytes 196616 | tf_op jit(solution)/shard_map/ppermute | solution.py:487
  83.9 8.6 %collective-permute-start.24 = (bf16[512,256]{1,0:T(8,128)(2,1)S(1)}, bf16[512,256]{1,0:T(8,128)(2,1)S(1)}, u32[]{:S(2)}, u32[]{:S(2)}) collective-permute-start(bf16[512,256]{1,0:T(8,128)(2,1)S(1)} %add_convert_fusion.1), channel_id=1, source_target_pairs={{0,4},{1,2},{2,1},{3,7},{4,0},{5,6},{6,5},{7,3},{8,12},{9,10},{10,... | collective-permute-start | bytes 786440 | tf_op jit(solution)/shard_map/ppermute | solution.py:483
  89.1 6.5 %collective-permute-start.23 = (bf16[512,256]{1,0:T(8,128)(2,1)S(1)}, bf16[512,256]{1,0:T(8,128)(2,1)S(1)}, u32[]{:S(2)}, u32[]{:S(2)}) collective-permute-start(bf16[512,256]{1,0:T(8,128)(2,1)S(1)} %add_convert_fusion.2), channel_id=1, source_target_pairs={{0,1},{1,0},{2,3},{3,2},{4,5},{5,4},{6,7},{7,6},{8,9},{9,8},{10,11... | collective-permute-start | bytes 786440 | tf_op jit(solution)/shard_map/ppermute | solution.py:471
  (7 other events, 35.5 us)

commit v5 on v4

--- a/solution.py
+++ b/solution.py
@@ -201,7 +201,7 @@
         fold_kernel,
         in_specs=[SMEM] + [VMEM] * 3,
         out_specs=VMEM,
-        out_shape=jax.ShapeDtypeStruct(own.shape, jnp.bfloat16),
+        out_shape=jax.ShapeDtypeStruct(own.shape, jnp.float32),
         compiler_params=pltpu.CompilerParams(vmem_limit_bytes=GRANT),
         cost_estimate=SMALL,
         name="fold",
@@ -392,7 +392,7 @@
             out[pl.ds(start, block), :] = value.astype(out.dtype)
 
 
-def add_up_residues(gconv, product, lam, entering, total):
+def add_up_residues(tiles_of, gconv, product, lam, entering, total):
     tokens = gconv.shape[0] // ROWS
     poles = lam.shape[0]
 
@@ -407,13 +407,14 @@
     zero = jnp.zeros((ROWS, LANES), jnp.float32)
     _, sums = lax.fori_loop(0, tokens, body, (state, (zero,) * poles), unroll=8)
     for m in range(poles):
-        total[m] = sums[m]
+        tiles_of[pl.ds(m * ROWS, ROWS), :] = sums[m]
+    gather_rows(tiles_of, total, 0, poles)
 
 
 def project_kernel(at, count, sources, plan, proj, weight, *refs):
     if sources:
-        add_up = functools.partial(add_up_residues, *refs[:sources + 1])
-        refs = refs[sources + 1:]
+        add_up = functools.partial(add_up_residues, refs[-1], *refs[:sources + 1])
+        refs = refs[sources + 1:-1]
     outs, (buffer, sems) = refs[:2 * count], refs[2 * count:]
     deep = buffer.shape[2]
     copies = []
@@ -434,7 +435,7 @@
     _, tokens, width = proj.shape
     outs = [jax.ShapeDtypeStruct((deep // 2, tokens), jnp.bfloat16)] * (2 * count)
     if sources:
-        outs = [jax.ShapeDtypeStruct(sources[-1].shape, jnp.float32)] + outs
+        outs = [jax.ShapeDtypeStruct((sources[-1].shape[0], width), jnp.float32)] + outs
     return pl.pallas_call(
         functools.partial(project_kernel, at, count, len(sources)),
         in_specs=[SMEM, VMEM, HBM] + [VMEM] * len(sources),
@@ -443,7 +444,7 @@
         scratch_shapes=[
             pltpu.VMEM((count, 3, deep, width), jnp.bfloat16),
             pltpu.SemaphoreType.DMA((count,)),
-        ],
+        ] + [pltpu.VMEM((array.shape[0] * ROWS, LANES), jnp.float32) for array in sources[-1:]],
         compiler_params=pltpu.CompilerParams(vmem_limit_bytes=GRANT),
         cost_estimate=pl.CostEstimate(
             flops=6 * tokens * width * deep * count,
@@ -638,15 +639,16 @@
             next_even = swap_even(added(for_even[phase][piece], masked(odds[piece])), count)
             odds[piece] = swap_odd(added(for_odd[phase][piece], evens[piece]), count, blocks)
             evens[piece] = next_even
+    mask = 1
+    while 2 * mask < blocks:
+        total = total + swap_ctx(total, mask, blocks)
+        mask *= 2
+    other = swap_ctx(total, mask, blocks)
+    evens[0], odds[0], evens[1], other = tie(evens[0], odds[0], evens[1], other)
+    grad_residue = (total + other) / (tokens * blocks)
     grad_input = jnp.concatenate(
         [added(parts[piece], evens[piece], masked(odds[piece])) for piece in range(2)]
     )
-
-    mask = 1
-    while mask < blocks:
-        total = total + swap_ctx(total, mask, blocks)
-        mask *= 2
-    grad_residue = total[:, :width // LANES].reshape(poles, width) / (tokens * blocks)
     return grad_input, grad_residue
 
 

time: 97.1 us -> 97.1 us (level)
  waiting for transfers between devices: 22.6 us -> 20.3 us
  starting transfers between devices: 26.9 us -> 29.1 us
    ppermute x7, waiting for transfers between devices: 8.16 us -> 6.1 us  [swap_ctx(): return lax.ppermute(value, 'ctx', [(i, i ^ mask) for i in range(blocks)])]
    ppermute x7, starting transfers between devices: 6.55 us -> 8.41 us  [swap_ctx(): return lax.ppermute(value, 'ctx', [(i, i ^ mask) for i in range(blocks)])]
  transfers between devices with their start and end apart: 28 -> 28, of which waited for: 13 -> 14; matrix products, arithmetic and copies ran while one was open for 8% -> 8% of each run, Pallas kernels for 30% -> 30%
where the time goes in v5:
time: 97.1 us; the launch traced here: 96.5 us
  Pallas kernels  36.5 us (38%)
  starting transfers between devices  29.1 us (30%)
  waiting for transfers between devices  20.3 us (21%)
  local copies, waits for them, and re-layouts  5.59 us (6%)
  other arithmetic  3.82 us (4%)
  between operations  1.06 us (1%)
    ppermute x12, starting transfers between devices, swap_even(): return lax.ppermute(value, 'chan', [(i, i ^ 1) for i in range(count)])  19 us
    ppermute x12, waiting for transfers between devices, swap_even(): return lax.ppermute(value, 'chan', [(i, i ^ 1) for i in range(count)])  14.2 us
    pallas_call x2, Pallas kernels, project(): pl.pallas_call(functools.partial(project_kernel, at, count, len(sources))...  12.2 us
    pallas_call x3, Pallas kernels, gate_step(): pl.pallas_call(functools.partial(gate_kernel, at, has_acc, shards, len(pi...  10.4 us
    ppermute x7, starting transfers between devices, swap_ctx(): return lax.ppermute(value, 'ctx', [(i, i ^ mask) for i in range(blocks)])  8.41 us
    ppermute x7, waiting for transfers between devices, swap_ctx(): return lax.ppermute(value, 'ctx', [(i, i ^ mask) for i in range(blocks)])  6.1 us
    pallas_call x1, Pallas kernels, scan_block(): pl.pallas_call(functools.partial(scan_kernel, at, taps, len(arrived) + 1)...  5.16 us
    pallas_call x2, Pallas kernels, close_gate(): pl.pallas_call(functools.partial(close_kernel, at, extra, late), in_specs...  4.94 us
  transfers between devices with their start and end apart: 28, of which 14 were waited for; matrix products, arithmetic and copies ran while one was open for 8% of the time, Pallas kernels for 30%

profile of v5, /device:TPU:0, one launch (start us, length us, event | category | flops | bytes accessed | tf_op | source)
XLA Modules:
  0.0 96.5 jit_solution(18160272099511484678)
XLA Ops:
  2.2 4.1 %collective-permute-start = (bf16[128,1024]{1,0:T(8,128)(2,1)S(1)}, bf16[128,1024]{1,0:T(8,128)(2,1)S(1)}, u32[]{:S(2)}, u32[]{:S(2)}) collective-permute-start(bf16[128,1024]{1,0:T(8,128)(2,1)S(1)} %slice.11), channel_id=1, source_target_pairs={{0,1},{1,0},{2,3},{3,2},{4,5},{5,4},{6,7},{7,6},{8,9},{9,8},{10,11... | collective-permute-start | bytes 786440 | tf_op jit(solution)/shard_map/ppermute | solution.py:472
  10.2 1.6 %collective-permute-start.4 = (bf16[128,1024]{1,0:T(8,128)(2,1)S(1)}, bf16[128,1024]{1,0:T(8,128)(2,1)}, u32[]{:S(2)}, u32[]{:S(2)}) collective-permute-start(bf16[128,1024]{1,0:T(8,128)(2,1)S(1)} %slice.12), channel_id=1, source_target_pairs={{0,1},{1,0},{2,3},{3,2},{4,5},{5,4},{6,7},{7,6},{8,9},{9,8},{10,11... | collective-permute-start | bytes 786440 | tf_op jit(solution)/shard_map/ppermute | solution.py:472
  12.4 1.7 %collective-permute-start.2 = (bf16[128,1024]{1,0:T(8,128)(2,1)S(1)}, bf16[128,1024]{1,0:T(8,128)(2,1)S(1)}, u32[]{:S(2)}, u32[]{:S(2)}) collective-permute-start(bf16[128,1024]{1,0:T(8,128)(2,1)S(1)} %collective-permute-done.1.refs_4_), channel_id=1, source_target_pairs={{0,1},{1,0},{2,3},{3,2},{4,5},{5,4},{6,7},{7,6},{8,9},{9,8},{10,11... | collective-permute-start | bytes 786440 | tf_op jit(solution)/shard_map/ppermute | solution.py:472
  14.1 2.9 %gate_step.3.refs_0_ = f32[256,1024]{1,0:T(8,128)S(1)} custom-call(s32[14]{0:T(128)S(1)} %stack.65.plan, bf16[256,1024]{1,0:T(8,128)(2,1)S(1)} %copy-done, bf16[1024,4096]{1,0:T(8,128)(2,1)} %refs_5_.3), custom_call_target="tpu_custom_call" | custom-call | flops 1 | bytes 1 | tf_op jit(solution)/shard_map/gate_step/pallas_call | solution.py:105
  17.1 2.4 %collective-permute-done.4.refs_1_ = bf16[128,1024]{1,0:T(8,128)(2,1)} collective-permute-done((bf16[128,1024]{1,0:T(8,128)(2,1)S(1)}, bf16[128,1024]{1,0:T(8,128)(2,1)}, u32[]{:S(2)}, u32[]{:S(2)}) %collective-permute-start.4) | collective-permute-done | bytes 262176 | tf_op jit(solution)/shard_map/ppermute | solution.py:472
  19.5 2.0 %collective-permute-start.6 = (bf16[128,1024]{1,0:T(8,128)(2,1)S(1)}, bf16[128,1024]{1,0:T(8,128)(2,1)}, u32[]{:S(2)}, u32[]{:S(2)}) collective-permute-start(bf16[128,1024]{1,0:T(8,128)(2,1)S(1)} %collective-permute-done.5.refs_3_), channel_id=1, source_target_pairs={{0,1},{1,0},{2,3},{3,2},{4,5},{5,4},{6,7},{7,6},{8,9},{9,8},{10,11... | collective-permute-start | bytes 786440 | tf_op jit(solution)/shard_map/ppermute | solution.py:472
  21.5 4.0 %gate_step.4.refs_0_ = f32[256,1024]{1,0:T(8,128)S(1)} custom-call(s32[14]{0:T(128)S(1)} %stack.65.plan, f32[256,1024]{1,0:T(8,128)S(1)} %gate_step.3.refs_0_, bf16[128,1024]{1,0:T(8,128)(2,1)} %collective-permute-done.4.refs_1_, bf16[128,1024]{1,0:T(8,128)(2,1)S(1)} %collective-permute-done.refs_2_, bf16[128,1024]{1,0:T(8,128)(2,1)S(1)} %collective-permute-done.5.refs_3_, ...), custom_call_target="tpu_custom_call" | custom-call | flops 1 | bytes 1 | tf_op jit(solution)/shard_map/gate_step/pallas_call | solution.py:105
  27.1 1.8 %constant_dynamic-slice_fusion.weight = bf16[1024,1024]{1,0:T(8,128)(2,1)S(1)} fusion(bf16[1024,4096]{1,0:T(8,128)(2,1)} %refs_5_.3, s32[]{:T(128)S(6)} %select_n.93), kind=kLoop, calls=%fused_computation.14 | loop fusion | bytes 4194308 | tf_op jit(solution)/shard_map/dynamic_slice | solution.py:588
  32.6 3.5 %gate_step.5.acc = f32[256,1024]{1,0:T(8,128)S(1)} custom-call(s32[14]{0:T(128)S(1)} %stack.65.plan, f32[256,1024]{1,0:T(8,128)S(1)} %gate_step.4.refs_0_, bf16[128,1024]{1,0:T(8,128)(2,1)} %collective-permute-done.6.refs_1_, bf16[128,1024]{1,0:T(8,128)(2,1)S(1)} %collective-permute-done.2.refs_2_, bf16[128,1024]{1,0:T(8,128)(2,1)} %collective-permute-done.7.refs_3_, ...), custom_call_target="tpu_custom_call" | custom-call | flops 1 | bytes 1 | tf_op jit(solution)/shard_map/gate_step/pallas_call | solution.py:105
  36.0 2.3 %collective-permute-done.9.piece = bf16[128,1024]{1,0:T(8,128)(2,1)S(1)} collective-permute-done((bf16[128,1024]{1,0:T(8,128)(2,1)}, bf16[128,1024]{1,0:T(8,128)(2,1)S(1)}, u32[]{:S(2)}, u32[]{:S(2)}) %collective-permute-start.9) | collective-permute-done | bytes 262176 | tf_op jit(solution)/shard_map/ppermute | solution.py:472
  38.4 2.9 %close_gate.2 = (f32[1024,128]{1,0:T(8,128)S(1)}, f32[1024,128]{1,0:T(8,128)S(1)}, f32[16,8,128]{2,1,0:T(8,128)S(1)}, f32[1024,128]{1,0:T(8,128)S(1)}) custom-call(s32[14]{0:T(128)S(1)} %stack.65.plan, f32[256,1024]{1,0:T(8,128)S(1)} %gate_step.5.acc, bf16[128,1024]{1,0:T(8,128)(2,1)S(1)} %collective-permute-done.9.piece, ...), custom_call_target="tpu_custom_call" | custom-call | flops 1 | bytes 1 | tf_op jit(solution)/shard_map/close_gate/pallas_call | solution.py:177
  42.8 2.0 %close_gate.3 = (f32[1024,128]{1,0:T(8,128)S(1)}, f32[1024,128]{1,0:T(8,128)S(1)}, f32[19,8,128]{2,1,0:T(8,128)S(1)}) custom-call(s32[14]{0:T(128)S(1)} %stack.65.plan, f32[256,1024]{1,0:T(8,128)S(1)} %gate_step.5.acc, bf16[128,1024]{1,0:T(8,128)(2,1)S(1)} %collective-permute-done.10.piece, bf16[1024,1024]{1,0:T(8,128)(2,1)S(1)} %constant_dynamic-slice_fusion.weight, ...), custom_call_target="tpu_custom_call" | custom-call | flops 1 | bytes 1 | tf_op jit(solution)/shard_map/close_gate/pallas_call | solution.py:177
  46.8 2.5 %collective-permute-start.14 = (f32[19,8,128]{2,1,0:T(8,128)S(1)}, f32[19,8,128]{2,1,0:T(8,128)S(1)}, u32[]{:S(2)}, u32[]{:S(2)}) collective-permute-start(f32[19,8,128]{2,1,0:T(8,128)S(1)} %fold.1), channel_id=1, source_target_pairs={{0,24},{4,28},{8,16},{12,20},{16,8},{20,12},{24,0},{28,4},{1,25},{... | collective-permute-start | bytes 233480 | tf_op jit(solution)/shard_map/ppermute | solution.py:488
  50.3 1.8 %settle.1 = (f32[1024,128]{1,0:T(8,128)S(1)}, f32[2048,128]{1,0:T(8,128)S(1)}, bf16[256,1024]{1,0:T(8,128)(2,1)S(1)}) custom-call(f32[16,8,128]{2,1,0:T(8,128)S(1)} %get-tuple-element.98.other.later, f32[1024,128]{1,0:T(8,128)S(1)} %get-tuple-element.99.late_conv, f32[1024,128]{1,0:T(8,128)S(1)} %get-tuple-element.100.late_query, ...), custom_call_target="tpu_custom_call" | custom-call | flops 1 | bytes 1 | tf_op jit(solution)/shard_map/settle/pallas_call | solution.py:262
  54.2 5.2 %scan.1 = (bf16[3,256,1024]{2,1,0:T(8,128)(2,1)S(1)}, bf16[512,256]{1,0:T(8,128)(2,1)S(1)}, bf16[512,256]{1,0:T(8,128)(2,1)S(1)}, f32[16,8,128]{2,1,0:T(8,128)S(1)}) custom-call(s32[14]{0:T(128)S(1)} %stack.65.plan, f32[1024,128]{1,0:T(8,128)S(1)} %get-tuple-element.97.late_products, f32[1024,128]{1,0:T(8,128)S(1)} %get-tuple-element.104.early_products, ...), custom_call_target="tpu_custom_call" | custom-call | flops 1 | bytes 1 | tf_op jit(solution)/shard_map/scan/pallas_call | solution.py:359
  61.5 5.2 %project.2 = (f32[16,1024]{1,0:T(8,128)S(1)}, bf16[512,256]{1,0:T(8,128)(2,1)S(1)}, bf16[512,256]{1,0:T(8,128)(2,1)S(1)}) custom-call(s32[14]{0:T(128)S(1)} %stack.65.plan, bf16[3,256,1024]{2,1,0:T(8,128)(2,1)S(1)} %get-tuple-element.120.proj, bf16[3,4096,1024]{2,1,0:T(8,128)(2,1)} %weight.3, f32[2048,128]{1,0:T(8,128)S(1)} %get-tuple-element.114.refs_0_, ...), custom_call_target="tpu_custom_call" | custom-call | flops 1610612736 | bytes 6291456 | tf_op jit(solution)/shard_map/project/pallas_call | solution.py:439
  66.6 2.0 %collective-permute-done.15 = bf16[512,256]{1,0:T(8,128)(2,1)S(1)} collective-permute-done((bf16[512,256]{1,0:T(8,128)(2,1)S(1)}, bf16[512,256]{1,0:T(8,128)(2,1)S(1)}, u32[]{:S(2)}, u32[]{:S(2)}) %collective-permute-start.15) | collective-permute-done | bytes 262176 | tf_op jit(solution)/shard_map/ppermute | solution.py:472
  68.8 1.9 %collective-permute-start.16 = (bf16[512,256]{1,0:T(8,128)(2,1)S(1)}, bf16[512,256]{1,0:T(8,128)(2,1)S(1)}, u32[]{:S(2)}, u32[]{:S(2)}) collective-permute-start(bf16[512,256]{1,0:T(8,128)(2,1)S(1)} %get-tuple-element.123), channel_id=1, source_target_pairs={{0,1},{1,0},{2,3},{3,2},{4,5},{5,4},{6,7},{7,6},{8,9},{9,8},{10,11... | collective-permute-start | bytes 786440 | tf_op jit(solution)/shard_map/ppermute | solution.py:472
  70.9 1.6 %collective-permute-done.21 = bf16[512,256]{1,0:T(8,128)(2,1)S(1)} collective-permute-done((bf16[512,256]{1,0:T(8,128)(2,1)S(1)}, bf16[512,256]{1,0:T(8,128)(2,1)S(1)}, u32[]{:S(2)}, u32[]{:S(2)}) %collective-permute-start.21) | collective-permute-done | bytes 262176 | tf_op jit(solution)/shard_map/ppermute | solution.py:472
  72.7 7.0 %project.3 = (bf16[512,256]{1,0:T(8,128)(2,1)S(1)}, bf16[512,256]{1,0:T(8,128)(2,1)S(1)}, bf16[512,256]{1,0:T(8,128)(2,1)S(1)}, bf16[512,256]{1,0:T(8,128)(2,1)S(1)}) custom-call(s32[14]{0:T(128)S(1)} %stack.65.plan, bf16[3,256,1024]{2,1,0:T(8,128)(2,1)S(1)} %get-tuple-element.120.proj, bf16[3,4096,1024]{2,1,0:T(8,128)(2,1)} %weight.3), custom_call_target="tpu_custom_call" | custom-call | flops 3221225472 | bytes 12582912 | tf_op jit(solution)/shard_map/project/pallas_call | solution.py:439
  83.6 2.1 %collective-permute-start.25 = (f32[16,1024]{1,0:T(8,128)S(1)}, f32[16,1024]{1,0:T(8,128)S(1)}, u32[]{:S(2)}, u32[]{:S(2)}) collective-permute-start(f32[16,1024]{1,0:T(8,128)S(1)} %add.95), channel_id=1, source_target_pairs={{0,8},{4,12},{8,0},{12,4},{16,24},{20,28},{24,16},{28,20},{1,9},{5... | collective-permute-start | bytes 196616 | tf_op jit(solution)/shard_map/ppermute | solution.py:488
  88.0 2.1 %collective-permute-start.26 = (f32[16,1024]{1,0:T(8,128)S(1)}, f32[16,1024]{1,0:T(8,128)S(1)}, u32[]{:S(2)}, u32[]{:S(2)}) collective-permute-start(f32[16,1024]{1,0:T(8,128)S(1)} %add.96), channel_id=1, source_target_pairs={{0,16},{4,20},{8,24},{12,28},{16,0},{20,4},{24,8},{28,12},{1,17},{... | collective-permute-start | bytes 196616 | tf_op jit(solution)/shard_map/ppermute | solution.py:488
  90.2 2.1 %collective-permute-done.26 = f32[16,1024]{1,0:T(8,128)S(1)} collective-permute-done((f32[16,1024]{1,0:T(8,128)S(1)}, f32[16,1024]{1,0:T(8,128)S(1)}, u32[]{:S(2)}, u32[]{:S(2)}) %collective-permute-start.26) | collective-permute-done | bytes 65568 | tf_op jit(solution)/shard_map/ppermute | solution.py:488
  92.3 2.4 %collective-permute-done.23 = bf16[512,256]{1,0:T(8,128)(2,1)S(1)} collective-permute-done((bf16[512,256]{1,0:T(8,128)(2,1)S(1)}, bf16[512,256]{1,0:T(8,128)(2,1)S(1)}, u32[]{:S(2)}, u32[]{:S(2)}) %collective-permute-start.23) | collective-permute-done | bytes 262176 | tf_op jit(solution)/shard_map/ppermute | solution.py:472
  (72 shorter events, 28.0 us)
Async XLA Ops:
  1.7 10.2 %collective-permute-start.1 = (bf16[128,1024]{1,0:T(8,128)(2,1)S(1)}, bf16[128,1024]{1,0:T(8,128)(2,1)S(1)}, u32[]{:S(2)}, u32[]{:S(2)}) collective-permute-start(bf16[128,1024]{1,0:T(8,128)(2,1)S(1)} %slice.11), channel_id=1, source_target_pairs={{0,4},{1,2},{2,1},{3,7},{4,0},{5,6},{6,5},{7,3},{8,12},{9,10},{10,... | collective-permute-start | bytes 786440 | tf_op jit(solution)/shard_map/ppermute | solution.py:484
  2.2 10.2 %collective-permute-start = (bf16[128,1024]{1,0:T(8,128)(2,1)S(1)}, bf16[128,1024]{1,0:T(8,128)(2,1)S(1)}, u32[]{:S(2)}, u32[]{:S(2)}) collective-permute-start(bf16[128,1024]{1,0:T(8,128)(2,1)S(1)} %slice.11), channel_id=1, source_target_pairs={{0,1},{1,0},{2,3},{3,2},{4,5},{5,4},{6,7},{7,6},{8,9},{9,8},{10,11... | collective-permute-start | bytes 786440 | tf_op jit(solution)/shard_map/ppermute | solution.py:472
  10.1 6.9 %collective-permute-start.5 = (bf16[128,1024]{1,0:T(8,128)(2,1)S(1)}, bf16[128,1024]{1,0:T(8,128)(2,1)S(1)}, u32[]{:S(2)}, u32[]{:S(2)}) collective-permute-start(bf16[128,1024]{1,0:T(8,128)(2,1)S(1)} %slice.12), channel_id=1, source_target_pairs={{0,4},{1,2},{2,1},{3,7},{4,0},{5,6},{6,5},{7,3},{8,12},{9,10},{10,... | collective-permute-start | bytes 786440 | tf_op jit(solution)/shard_map/ppermute | solution.py:484
  10.2 9.3 %collective-permute-start.4 = (bf16[128,1024]{1,0:T(8,128)(2,1)S(1)}, bf16[128,1024]{1,0:T(8,128)(2,1)}, u32[]{:S(2)}, u32[]{:S(2)}) collective-permute-start(bf16[128,1024]{1,0:T(8,128)(2,1)S(1)} %slice.12), channel_id=1, source_target_pairs={{0,1},{1,0},{2,3},{3,2},{4,5},{5,4},{6,7},{7,6},{8,9},{9,8},{10,11... | collective-permute-start | bytes 786440 | tf_op jit(solution)/shard_map/ppermute | solution.py:472
  12.4 13.2 %collective-permute-start.2 = (bf16[128,1024]{1,0:T(8,128)(2,1)S(1)}, bf16[128,1024]{1,0:T(8,128)(2,1)S(1)}, u32[]{:S(2)}, u32[]{:S(2)}) collective-permute-start(bf16[128,1024]{1,0:T(8,128)(2,1)S(1)} %collective-permute-done.1.refs_4_), channel_id=1, source_target_pairs={{0,1},{1,0},{2,3},{3,2},{4,5},{5,4},{6,7},{7,6},{8,9},{9,8},{10,11... | collective-permute-start | bytes 786440 | tf_op jit(solution)/shard_map/ppermute | solution.py:472
  14.1 11.4 %collective-permute-start.3 = (bf16[128,1024]{1,0:T(8,128)(2,1)S(1)}, bf16[128,1024]{1,0:T(8,128)(2,1)}, u32[]{:S(2)}, u32[]{:S(2)}) collective-permute-start(bf16[128,1024]{1,0:T(8,128)(2,1)S(1)} %collective-permute-done.refs_2_), channel_id=1, source_target_pairs={{0,4},{1,2},{2,1},{3,7},{4,0},{5,6},{6,5},{7,3},{8,12},{9,10},{10,... | collective-permute-start | bytes 786440 | tf_op jit(solution)/shard_map/ppermute | solution.py:484
  19.5 12.6 %collective-permute-start.7 = (bf16[128,1024]{1,0:T(8,128)(2,1)}, bf16[128,1024]{1,0:T(8,128)(2,1)}, u32[]{:S(2)}, u32[]{:S(2)}) collective-permute-start(bf16[128,1024]{1,0:T(8,128)(2,1)} %collective-permute-done.4.refs_1_), channel_id=1, source_target_pairs={{0,4},{1,2},{2,1},{3,7},{4,0},{5,6},{6,5},{7,3},{8,12},{9,10},{10,... | collective-permute-start | bytes 786440 | tf_op jit(solution)/shard_map/ppermute | solution.py:484
  19.5 12.6 %collective-permute-start.6 = (bf16[128,1024]{1,0:T(8,128)(2,1)S(1)}, bf16[128,1024]{1,0:T(8,128)(2,1)}, u32[]{:S(2)}, u32[]{:S(2)}) collective-permute-start(bf16[128,1024]{1,0:T(8,128)(2,1)S(1)} %collective-permute-done.5.refs_3_), channel_id=1, source_target_pairs={{0,1},{1,0},{2,3},{3,2},{4,5},{5,4},{6,7},{7,6},{8,9},{9,8},{10,11... | collective-permute-start | bytes 786440 | tf_op jit(solution)/shard_map/ppermute | solution.py:472
  26.4 5.7 %collective-permute-start.8 = (f32[2,2,8,128]{3,2,1,0:T(8,128)S(1)}, f32[2,2,8,128]{3,2,1,0:T(8,128)S(1)}, u32[]{:S(2)}, u32[]{:S(2)}) collective-permute-start(f32[2,2,8,128]{3,2,1,0:T(8,128)S(1)} %reshape.29), channel_id=1, source_target_pairs={{0,28},{4,0},{8,4},{12,8},{16,12},{20,16},{24,20},{28,24},{1,29},{... | collective-permute-start | bytes 49160 | tf_op jit(solution)/shard_map/ppermute | solution.py:584
  28.9 9.5 %collective-permute-start.9 = (bf16[128,1024]{1,0:T(8,128)(2,1)}, bf16[128,1024]{1,0:T(8,128)(2,1)S(1)}, u32[]{:S(2)}, u32[]{:S(2)}) collective-permute-start(bf16[128,1024]{1,0:T(8,128)(2,1)} %collective-permute-done.3.refs_4_), channel_id=1, source_target_pairs={{0,1},{1,0},{2,3},{3,2},{4,5},{5,4},{6,7},{7,6},{8,9},{9,8},{10,11... | collective-permute-start | bytes 786440 | tf_op jit(solution)/shard_map/ppermute | solution.py:472
  32.1 10.7 %collective-permute-start.10 = (bf16[128,1024]{1,0:T(8,128)(2,1)}, bf16[128,1024]{1,0:T(8,128)(2,1)S(1)}, u32[]{:S(2)}, u32[]{:S(2)}) collective-permute-start(bf16[128,1024]{1,0:T(8,128)(2,1)} %collective-permute-done.7.refs_3_), channel_id=1, source_target_pairs={{0,1},{1,0},{2,3},{3,2},{4,5},{5,4},{6,7},{7,6},{8,9},{9,8},{10,11... | collective-permute-start | bytes 786440 | tf_op jit(solution)/shard_map/ppermute | solution.py:472
  46.8 5.4 %collective-permute-start.14 = (f32[19,8,128]{2,1,0:T(8,128)S(1)}, f32[19,8,128]{2,1,0:T(8,128)S(1)}, u32[]{:S(2)}, u32[]{:S(2)}) collective-permute-start(f32[19,8,128]{2,1,0:T(8,128)S(1)} %fold.1), channel_id=1, source_target_pairs={{0,24},{4,28},{8,16},{12,20},{16,8},{20,12},{24,0},{28,4},{1,25},{... | collective-permute-start | bytes 233480 | tf_op jit(solution)/shard_map/ppermute | solution.py:488
  49.3 4.5 %collective-permute-start.13 = (f32[19,8,128]{2,1,0:T(8,128)S(1)}, f32[19,8,128]{2,1,0:T(8,128)S(1)}, u32[]{:S(2)}, u32[]{:S(2)}) collective-permute-start(f32[19,8,128]{2,1,0:T(8,128)S(1)} %fold.1), channel_id=1, source_target_pairs={{0,16},{4,20},{8,24},{12,28},{16,0},{20,4},{24,8},{28,12},{1,17},{... | collective-permute-start | bytes 233480 | tf_op jit(solution)/shard_map/ppermute | solution.py:488
  49.8 4.4 %collective-permute-start.12 = (f32[19,8,128]{2,1,0:T(8,128)S(1)}, f32[19,8,128]{2,1,0:T(8,128)S(1)}, u32[]{:S(2)}, u32[]{:S(2)}) collective-permute-start(f32[19,8,128]{2,1,0:T(8,128)S(1)} %fold.1), channel_id=1, source_target_pairs={{0,8},{4,12},{8,0},{12,4},{16,24},{20,28},{24,16},{28,20},{1,9},{5... | collective-permute-start | bytes 233480 | tf_op jit(solution)/shard_map/ppermute | solution.py:488
  59.4 9.3 %collective-permute-start.15 = (bf16[512,256]{1,0:T(8,128)(2,1)S(1)}, bf16[512,256]{1,0:T(8,128)(2,1)S(1)}, u32[]{:S(2)}, u32[]{:S(2)}) collective-permute-start(bf16[512,256]{1,0:T(8,128)(2,1)S(1)} %get-tuple-element.112), channel_id=1, source_target_pairs={{0,1},{1,0},{2,3},{3,2},{4,5},{5,4},{6,7},{7,6},{8,9},{9,8},{10,11... | collective-permute-start | bytes 786440 | tf_op jit(solution)/shard_map/ppermute | solution.py:472
  60.5 12.0 %collective-permute-start.21 = (bf16[512,256]{1,0:T(8,128)(2,1)S(1)}, bf16[512,256]{1,0:T(8,128)(2,1)S(1)}, u32[]{:S(2)}, u32[]{:S(2)}) collective-permute-start(bf16[512,256]{1,0:T(8,128)(2,1)S(1)} %get-tuple-element.131), channel_id=1, source_target_pairs={{0,1},{1,0},{2,3},{3,2},{4,5},{5,4},{6,7},{7,6},{8,9},{9,8},{10,11... | collective-permute-start | bytes 786440 | tf_op jit(solution)/shard_map/ppermute | solution.py:472
  68.7 11.0 %collective-permute-start.17 = (bf16[512,256]{1,0:T(8,128)(2,1)S(1)}, bf16[512,256]{1,0:T(8,128)(2,1)S(1)}, u32[]{:S(2)}, u32[]{:S(2)}) collective-permute-start(bf16[512,256]{1,0:T(8,128)(2,1)S(1)} %add_convert_fusion.7), channel_id=1, source_target_pairs={{0,4},{1,2},{2,1},{3,7},{4,0},{5,6},{6,5},{7,3},{8,12},{9,10},{10,... | collective-permute-start | bytes 786440 | tf_op jit(solution)/shard_map/ppermute | solution.py:484
  68.8 10.9 %collective-permute-start.16 = (bf16[512,256]{1,0:T(8,128)(2,1)S(1)}, bf16[512,256]{1,0:T(8,128)(2,1)S(1)}, u32[]{:S(2)}, u32[]{:S(2)}) collective-permute-start(bf16[512,256]{1,0:T(8,128)(2,1)S(1)} %get-tuple-element.123), channel_id=1, source_target_pairs={{0,1},{1,0},{2,3},{3,2},{4,5},{5,4},{6,7},{7,6},{8,9},{9,8},{10,11... | collective-permute-start | bytes 786440 | tf_op jit(solution)/shard_map/ppermute | solution.py:472
  70.7 12.8 %collective-permute-start.20 = (bf16[512,256]{1,0:T(8,128)(2,1)S(1)}, bf16[512,256]{1,0:T(8,128)(2,1)S(1)}, u32[]{:S(2)}, u32[]{:S(2)}) collective-permute-start(bf16[512,256]{1,0:T(8,128)(2,1)S(1)} %get-tuple-element.130), channel_id=1, source_target_pairs={{0,1},{1,0},{2,3},{3,2},{4,5},{5,4},{6,7},{7,6},{8,9},{9,8},{10,11... | collective-permute-start | bytes 786440 | tf_op jit(solution)/shard_map/ppermute | solution.py:472
  72.6 10.9 %collective-permute-start.22 = (bf16[512,256]{1,0:T(8,128)(2,1)S(1)}, bf16[512,256]{1,0:T(8,128)(2,1)S(1)}, u32[]{:S(2)}, u32[]{:S(2)}) collective-permute-start(bf16[512,256]{1,0:T(8,128)(2,1)S(1)} %add_convert_fusion.4), channel_id=1, source_target_pairs={{0,4},{1,2},{2,1},{3,7},{4,0},{5,6},{6,5},{7,3},{8,12},{9,10},{10,... | collective-permute-start | bytes 786440 | tf_op jit(solution)/shard_map/ppermute | solution.py:484
  80.5 11.9 %collective-permute-start.18 = (bf16[512,256]{1,0:T(8,128)(2,1)S(1)}, bf16[512,256]{1,0:T(8,128)(2,1)S(1)}, u32[]{:S(2)}, u32[]{:S(2)}) collective-permute-start(bf16[512,256]{1,0:T(8,128)(2,1)S(1)} %add_convert_fusion.6), channel_id=1, source_target_pairs={{0,1},{1,0},{2,3},{3,2},{4,5},{5,4},{6,7},{7,6},{8,9},{9,8},{10,11... | collective-permute-start | bytes 786440 | tf_op jit(solution)/shard_map/ppermute | solution.py:472
  82.0 10.3 %collective-permute-start.19 = (bf16[512,256]{1,0:T(8,128)(2,1)S(1)}, bf16[512,256]{1,0:T(8,128)(2,1)S(1)}, u32[]{:S(2)}, u32[]{:S(2)}) collective-permute-start(bf16[512,256]{1,0:T(8,128)(2,1)S(1)} %add_convert_fusion.5), channel_id=1, source_target_pairs={{0,4},{1,2},{2,1},{3,7},{4,0},{5,6},{6,5},{7,3},{8,12},{9,10},{10,... | collective-permute-start | bytes 786440 | tf_op jit(solution)/shard_map/ppermute | solution.py:484
  85.8 8.9 %collective-permute-start.23 = (bf16[512,256]{1,0:T(8,128)(2,1)S(1)}, bf16[512,256]{1,0:T(8,128)(2,1)S(1)}, u32[]{:S(2)}, u32[]{:S(2)}) collective-permute-start(bf16[512,256]{1,0:T(8,128)(2,1)S(1)} %add_convert_fusion.3), channel_id=1, source_target_pairs={{0,1},{1,0},{2,3},{3,2},{4,5},{5,4},{6,7},{7,6},{8,9},{9,8},{10,11... | collective-permute-start | bytes 786440 | tf_op jit(solution)/shard_map/ppermute | solution.py:472
  90.2 5.4 %collective-permute-start.27 = (bf16[512,256]{1,0:T(8,128)(2,1)S(1)}, bf16[512,256]{1,0:T(8,128)(2,1)S(1)}, u32[]{:S(2)}, u32[]{:S(2)}) collective-permute-start(bf16[512,256]{1,0:T(8,128)(2,1)S(1)} %add_convert_fusion.1), channel_id=1, source_target_pairs={{0,4},{1,2},{2,1},{3,7},{4,0},{5,6},{6,5},{7,3},{8,12},{9,10},{10,... | collective-permute-start | bytes 786440 | tf_op jit(solution)/shard_map/ppermute | solution.py:484
  (7 other events, 35.6 us)

commit v6 on v5

--- a/solution.py
+++ b/solution.py
@@ -587,9 +587,7 @@
             )
             last_weight = lax.dynamic_slice(out_weight, (0, last * width), (width, width))
             query, keys, values, saved, product = spread_acts(features, saved_conv)
-            odds[1], kv_halo, last_weight, query, keys, values, saved, product = tie(
-                odds[1], kv_halo, last_weight, query, keys, values, saved, product
-            )
+            odds[1], kv_halo, last_weight = tie(odds[1], kv_halo, last_weight)
     late_conv, late_query, later, late_products = close_gate(
         plan, 1, acc, evens[0], last_weight, query, saved, lam, extra, residues=res
     )

time: 97.1 us -> 96.9 us (level)
  no operation moved by 1% of the time
where the time goes in v6:
time: 96.9 us; the launch traced here: 96.4 us
  Pallas kernels  36.6 us (38%)
  starting transfers between devices  29.3 us (30%)
  waiting for transfers between devices  20.1 us (21%)
  local copies, waits for them, and re-layouts  5.59 us (6%)
  other arithmetic  3.82 us (4%)
  between operations  1.04 us (1%)
    ppermute x12, starting transfers between devices, swap_even(): return lax.ppermute(value, 'chan', [(i, i ^ 1) for i in range(count)])  19.2 us
    ppermute x12, waiting for transfers between devices, swap_even(): return lax.ppermute(value, 'chan', [(i, i ^ 1) for i in range(count)])  14 us
    pallas_call x2, Pallas kernels, project(): pl.pallas_call(functools.partial(project_kernel, at, count, len(sources))...  12.2 us
    pallas_call x3, Pallas kernels, gate_step(): pl.pallas_call(functools.partial(gate_kernel, at, has_acc, shards, len(pi...  10.4 us
    ppermute x7, starting transfers between devices, swap_ctx(): return lax.ppermute(value, 'ctx', [(i, i ^ mask) for i in range(blocks)])  8.39 us
    ppermute x7, waiting for transfers between devices, swap_ctx(): return lax.ppermute(value, 'ctx', [(i, i ^ mask) for i in range(blocks)])  6.08 us
    pallas_call x1, Pallas kernels, scan_block(): pl.pallas_call(functools.partial(scan_kernel, at, taps, len(arrived) + 1)...  5.16 us
    pallas_call x2, Pallas kernels, close_gate(): pl.pallas_call(functools.partial(close_kernel, at, extra, late), in_specs...  4.95 us
  transfers between devices with their start and end apart: 28, of which 14 were waited for; matrix products, arithmetic and copies ran while one was open for 8% of the time, Pallas kernels for 30%

profile of v6, /device:TPU:0, one launch (start us, length us, event | category | flops | bytes accessed | tf_op | source)
XLA Modules:
  0.0 96.4 jit_solution(15751679838485021200)
XLA Ops:
  2.2 4.1 %collective-permute-start = (bf16[128,1024]{1,0:T(8,128)(2,1)S(1)}, bf16[128,1024]{1,0:T(8,128)(2,1)S(1)}, u32[]{:S(2)}, u32[]{:S(2)}) collective-permute-start(bf16[128,1024]{1,0:T(8,128)(2,1)S(1)} %slice.11), channel_id=1, source_target_pairs={{0,1},{1,0},{2,3},{3,2},{4,5},{5,4},{6,7},{7,6},{8,9},{9,8},{10,11... | collective-permute-start | bytes 786440 | tf_op jit(solution)/shard_map/ppermute | solution.py:472
  12.4 1.7 %collective-permute-start.2 = (bf16[128,1024]{1,0:T(8,128)(2,1)S(1)}, bf16[128,1024]{1,0:T(8,128)(2,1)S(1)}, u32[]{:S(2)}, u32[]{:S(2)}) collective-permute-start(bf16[128,1024]{1,0:T(8,128)(2,1)S(1)} %collective-permute-done.1.refs_4_), channel_id=1, source_target_pairs={{0,1},{1,0},{2,3},{3,2},{4,5},{5,4},{6,7},{7,6},{8,9},{9,8},{10,11... | collective-permute-start | bytes 786440 | tf_op jit(solution)/shard_map/ppermute | solution.py:472
  14.1 2.9 %gate_step.3.refs_0_ = f32[256,1024]{1,0:T(8,128)S(1)} custom-call(s32[14]{0:T(128)S(1)} %stack.65.plan, bf16[256,1024]{1,0:T(8,128)(2,1)S(1)} %copy-done, bf16[1024,4096]{1,0:T(8,128)(2,1)} %refs_5_.3), custom_call_target="tpu_custom_call" | custom-call | flops 1 | bytes 1 | tf_op jit(solution)/shard_map/gate_step/pallas_call | solution.py:105
  17.1 2.4 %collective-permute-done.4.refs_1_ = bf16[128,1024]{1,0:T(8,128)(2,1)} collective-permute-done((bf16[128,1024]{1,0:T(8,128)(2,1)S(1)}, bf16[128,1024]{1,0:T(8,128)(2,1)}, u32[]{:S(2)}, u32[]{:S(2)}) %collective-permute-start.4) | collective-permute-done | bytes 262176 | tf_op jit(solution)/shard_map/ppermute | solution.py:472
  19.5 2.0 %collective-permute-start.6 = (bf16[128,1024]{1,0:T(8,128)(2,1)}, bf16[128,1024]{1,0:T(8,128)(2,1)}, u32[]{:S(2)}, u32[]{:S(2)}) collective-permute-start(bf16[128,1024]{1,0:T(8,128)(2,1)} %collective-permute-done.5.refs_3_), channel_id=1, source_target_pairs={{0,1},{1,0},{2,3},{3,2},{4,5},{5,4},{6,7},{7,6},{8,9},{9,8},{10,11... | collective-permute-start | bytes 786440 | tf_op jit(solution)/shard_map/ppermute | solution.py:472
  21.5 4.1 %gate_step.4.refs_0_ = f32[256,1024]{1,0:T(8,128)S(1)} custom-call(s32[14]{0:T(128)S(1)} %stack.65.plan, f32[256,1024]{1,0:T(8,128)S(1)} %gate_step.3.refs_0_, bf16[128,1024]{1,0:T(8,128)(2,1)} %collective-permute-done.4.refs_1_, bf16[128,1024]{1,0:T(8,128)(2,1)S(1)} %collective-permute-done.refs_2_, bf16[128,1024]{1,0:T(8,128)(2,1)} %collective-permute-done.5.refs_3_, ...), custom_call_target="tpu_custom_call" | custom-call | flops 1 | bytes 1 | tf_op jit(solution)/shard_map/gate_step/pallas_call | solution.py:105
  27.1 1.8 %constant_dynamic-slice_fusion.weight = bf16[1024,1024]{1,0:T(8,128)(2,1)S(1)} fusion(bf16[1024,4096]{1,0:T(8,128)(2,1)} %refs_5_.3, s32[]{:T(128)S(6)} %select_n.93), kind=kLoop, calls=%fused_computation.14 | loop fusion | bytes 4194308 | tf_op jit(solution)/shard_map/dynamic_slice | solution.py:588
  28.9 1.7 %collective-permute-start.9 = (bf16[128,1024]{1,0:T(8,128)(2,1)S(1)}, bf16[128,1024]{1,0:T(8,128)(2,1)S(1)}, u32[]{:S(2)}, u32[]{:S(2)}) collective-permute-start(bf16[128,1024]{1,0:T(8,128)(2,1)S(1)} %collective-permute-done.3.refs_4_), channel_id=1, source_target_pairs={{0,1},{1,0},{2,3},{3,2},{4,5},{5,4},{6,7},{7,6},{8,9},{9,8},{10,11... | collective-permute-start | bytes 786440 | tf_op jit(solution)/shard_map/ppermute | solution.py:472
  32.8 3.4 %gate_step.5.acc = f32[256,1024]{1,0:T(8,128)S(1)} custom-call(s32[14]{0:T(128)S(1)} %stack.65.plan, f32[256,1024]{1,0:T(8,128)S(1)} %gate_step.4.refs_0_, bf16[128,1024]{1,0:T(8,128)(2,1)} %collective-permute-done.6.refs_1_, bf16[128,1024]{1,0:T(8,128)(2,1)S(1)} %collective-permute-done.2.refs_2_, bf16[128,1024]{1,0:T(8,128)(2,1)} %collective-permute-done.7.refs_3_, ...), custom_call_target="tpu_custom_call" | custom-call | flops 1 | bytes 1 | tf_op jit(solution)/shard_map/gate_step/pallas_call | solution.py:105
  36.2 1.9 %collective-permute-done.9.piece = bf16[128,1024]{1,0:T(8,128)(2,1)S(1)} collective-permute-done((bf16[128,1024]{1,0:T(8,128)(2,1)S(1)}, bf16[128,1024]{1,0:T(8,128)(2,1)S(1)}, u32[]{:S(2)}, u32[]{:S(2)}) %collective-permute-start.9) | collective-permute-done | bytes 262176 | tf_op jit(solution)/shard_map/ppermute | solution.py:472
  38.1 2.9 %close_gate.2 = (f32[1024,128]{1,0:T(8,128)S(1)}, f32[1024,128]{1,0:T(8,128)S(1)}, f32[16,8,128]{2,1,0:T(8,128)S(1)}, f32[1024,128]{1,0:T(8,128)S(1)}) custom-call(s32[14]{0:T(128)S(1)} %stack.65.plan, f32[256,1024]{1,0:T(8,128)S(1)} %gate_step.5.acc, bf16[128,1024]{1,0:T(8,128)(2,1)S(1)} %collective-permute-done.9.piece, ...), custom_call_target="tpu_custom_call" | custom-call | flops 1 | bytes 1 | tf_op jit(solution)/shard_map/close_gate/pallas_call | solution.py:177
  42.7 2.1 %close_gate.3 = (f32[1024,128]{1,0:T(8,128)S(1)}, f32[1024,128]{1,0:T(8,128)S(1)}, f32[19,8,128]{2,1,0:T(8,128)S(1)}) custom-call(s32[14]{0:T(128)S(1)} %stack.65.plan, f32[256,1024]{1,0:T(8,128)S(1)} %gate_step.5.acc, bf16[128,1024]{1,0:T(8,128)(2,1)S(1)} %collective-permute-done.10.piece, bf16[1024,1024]{1,0:T(8,128)(2,1)S(1)} %constant_dynamic-slice_fusion.weight, ...), custom_call_target="tpu_custom_call" | custom-call | flops 1 | bytes 1 | tf_op jit(solution)/shard_map/close_gate/pallas_call | solution.py:177
  46.6 2.5 %collective-permute-start.14 = (f32[19,8,128]{2,1,0:T(8,128)S(1)}, f32[19,8,128]{2,1,0:T(8,128)S(1)}, u32[]{:S(2)}, u32[]{:S(2)}) collective-permute-start(f32[19,8,128]{2,1,0:T(8,128)S(1)} %fold.1), channel_id=1, source_target_pairs={{0,24},{4,28},{8,16},{12,20},{16,8},{20,12},{24,0},{28,4},{1,25},{... | collective-permute-start | bytes 233480 | tf_op jit(solution)/shard_map/ppermute | solution.py:488
  50.2 1.8 %settle.1 = (f32[1024,128]{1,0:T(8,128)S(1)}, f32[2048,128]{1,0:T(8,128)S(1)}, bf16[256,1024]{1,0:T(8,128)(2,1)S(1)}) custom-call(f32[16,8,128]{2,1,0:T(8,128)S(1)} %get-tuple-element.88.other.later, f32[1024,128]{1,0:T(8,128)S(1)} %get-tuple-element.89.late_conv, f32[1024,128]{1,0:T(8,128)S(1)} %get-tuple-element.90.late_query, ...), custom_call_target="tpu_custom_call" | custom-call | flops 1 | bytes 1 | tf_op jit(solution)/shard_map/settle/pallas_call | solution.py:262
  54.1 5.2 %scan.1 = (bf16[3,256,1024]{2,1,0:T(8,128)(2,1)S(1)}, bf16[512,256]{1,0:T(8,128)(2,1)S(1)}, bf16[512,256]{1,0:T(8,128)(2,1)S(1)}, f32[16,8,128]{2,1,0:T(8,128)S(1)}) custom-call(s32[14]{0:T(128)S(1)} %stack.65.plan, f32[1024,128]{1,0:T(8,128)S(1)} %get-tuple-element.87.late_products, f32[1024,128]{1,0:T(8,128)S(1)} %get-tuple-element.94.early_products, ...), custom_call_target="tpu_custom_call" | custom-call | flops 1 | bytes 1 | tf_op jit(solution)/shard_map/scan/pallas_call | solution.py:359
  61.3 5.2 %project.2 = (f32[16,1024]{1,0:T(8,128)S(1)}, bf16[512,256]{1,0:T(8,128)(2,1)S(1)}, bf16[512,256]{1,0:T(8,128)(2,1)S(1)}) custom-call(s32[14]{0:T(128)S(1)} %stack.65.plan, bf16[3,256,1024]{2,1,0:T(8,128)(2,1)S(1)} %get-tuple-element.110.proj, bf16[3,4096,1024]{2,1,0:T(8,128)(2,1)} %weight.3, f32[2048,128]{1,0:T(8,128)S(1)} %get-tuple-element.104.refs_0_, ...), custom_call_target="tpu_custom_call" | custom-call | flops 1610612736 | bytes 6291456 | tf_op jit(solution)/shard_map/project/pallas_call | solution.py:439
  66.5 2.0 %collective-permute-done.15 = bf16[512,256]{1,0:T(8,128)(2,1)S(1)} collective-permute-done((bf16[512,256]{1,0:T(8,128)(2,1)S(1)}, bf16[512,256]{1,0:T(8,128)(2,1)S(1)}, u32[]{:S(2)}, u32[]{:S(2)}) %collective-permute-start.15) | collective-permute-done | bytes 262176 | tf_op jit(solution)/shard_map/ppermute | solution.py:472
  68.7 1.9 %collective-permute-start.16 = (bf16[512,256]{1,0:T(8,128)(2,1)S(1)}, bf16[512,256]{1,0:T(8,128)(2,1)S(1)}, u32[]{:S(2)}, u32[]{:S(2)}) collective-permute-start(bf16[512,256]{1,0:T(8,128)(2,1)S(1)} %get-tuple-element.113), channel_id=1, source_target_pairs={{0,1},{1,0},{2,3},{3,2},{4,5},{5,4},{6,7},{7,6},{8,9},{9,8},{10,11... | collective-permute-start | bytes 786440 | tf_op jit(solution)/shard_map/ppermute | solution.py:472
  70.8 1.7 %collective-permute-done.21 = bf16[512,256]{1,0:T(8,128)(2,1)S(1)} collective-permute-done((bf16[512,256]{1,0:T(8,128)(2,1)S(1)}, bf16[512,256]{1,0:T(8,128)(2,1)S(1)}, u32[]{:S(2)}, u32[]{:S(2)}) %collective-permute-start.21) | collective-permute-done | bytes 262176 | tf_op jit(solution)/shard_map/ppermute | solution.py:472
  72.6 7.0 %project.3 = (bf16[512,256]{1,0:T(8,128)(2,1)S(1)}, bf16[512,256]{1,0:T(8,128)(2,1)S(1)}, bf16[512,256]{1,0:T(8,128)(2,1)S(1)}, bf16[512,256]{1,0:T(8,128)(2,1)S(1)}) custom-call(s32[14]{0:T(128)S(1)} %stack.65.plan, bf16[3,256,1024]{2,1,0:T(8,128)(2,1)S(1)} %get-tuple-element.110.proj, bf16[3,4096,1024]{2,1,0:T(8,128)(2,1)} %weight.3), custom_call_target="tpu_custom_call" | custom-call | flops 3221225472 | bytes 12582912 | tf_op jit(solution)/shard_map/project/pallas_call | solution.py:439
  83.5 2.1 %collective-permute-start.25 = (f32[16,1024]{1,0:T(8,128)S(1)}, f32[16,1024]{1,0:T(8,128)S(1)}, u32[]{:S(2)}, u32[]{:S(2)}) collective-permute-start(f32[16,1024]{1,0:T(8,128)S(1)} %add.95), channel_id=1, source_target_pairs={{0,8},{4,12},{8,0},{12,4},{16,24},{20,28},{24,16},{28,20},{1,9},{5... | collective-permute-start | bytes 196616 | tf_op jit(solution)/shard_map/ppermute | solution.py:488
  87.8 2.1 %collective-permute-start.26 = (f32[16,1024]{1,0:T(8,128)S(1)}, f32[16,1024]{1,0:T(8,128)S(1)}, u32[]{:S(2)}, u32[]{:S(2)}) collective-permute-start(f32[16,1024]{1,0:T(8,128)S(1)} %add.96), channel_id=1, source_target_pairs={{0,16},{4,20},{8,24},{12,28},{16,0},{20,4},{24,8},{28,12},{1,17},{... | collective-permute-start | bytes 196616 | tf_op jit(solution)/shard_map/ppermute | solution.py:488
  90.1 2.1 %collective-permute-done.26 = f32[16,1024]{1,0:T(8,128)S(1)} collective-permute-done((f32[16,1024]{1,0:T(8,128)S(1)}, f32[16,1024]{1,0:T(8,128)S(1)}, u32[]{:S(2)}, u32[]{:S(2)}) %collective-permute-start.26) | collective-permute-done | bytes 65568 | tf_op jit(solution)/shard_map/ppermute | solution.py:488
  92.2 2.4 %collective-permute-done.23 = bf16[512,256]{1,0:T(8,128)(2,1)S(1)} collective-permute-done((bf16[512,256]{1,0:T(8,128)(2,1)S(1)}, bf16[512,256]{1,0:T(8,128)(2,1)S(1)}, u32[]{:S(2)}, u32[]{:S(2)}) %collective-permute-start.23) | collective-permute-done | bytes 262176 | tf_op jit(solution)/shard_map/ppermute | solution.py:472
  (72 shorter events, 28.1 us)
Async XLA Ops:
  1.7 10.2 %collective-permute-start.1 = (bf16[128,1024]{1,0:T(8,128)(2,1)S(1)}, bf16[128,1024]{1,0:T(8,128)(2,1)S(1)}, u32[]{:S(2)}, u32[]{:S(2)}) collective-permute-start(bf16[128,1024]{1,0:T(8,128)(2,1)S(1)} %slice.11), channel_id=1, source_target_pairs={{0,4},{1,2},{2,1},{3,7},{4,0},{5,6},{6,5},{7,3},{8,12},{9,10},{10,... | collective-permute-start | bytes 786440 | tf_op jit(solution)/shard_map/ppermute | solution.py:484
  2.2 10.2 %collective-permute-start = (bf16[128,1024]{1,0:T(8,128)(2,1)S(1)}, bf16[128,1024]{1,0:T(8,128)(2,1)S(1)}, u32[]{:S(2)}, u32[]{:S(2)}) collective-permute-start(bf16[128,1024]{1,0:T(8,128)(2,1)S(1)} %slice.11), channel_id=1, source_target_pairs={{0,1},{1,0},{2,3},{3,2},{4,5},{5,4},{6,7},{7,6},{8,9},{9,8},{10,11... | collective-permute-start | bytes 786440 | tf_op jit(solution)/shard_map/ppermute | solution.py:472
  10.1 6.9 %collective-permute-start.5 = (bf16[128,1024]{1,0:T(8,128)(2,1)S(1)}, bf16[128,1024]{1,0:T(8,128)(2,1)}, u32[]{:S(2)}, u32[]{:S(2)}) collective-permute-start(bf16[128,1024]{1,0:T(8,128)(2,1)S(1)} %slice.12), channel_id=1, source_target_pairs={{0,4},{1,2},{2,1},{3,7},{4,0},{5,6},{6,5},{7,3},{8,12},{9,10},{10,... | collective-permute-start | bytes 786440 | tf_op jit(solution)/shard_map/ppermute | solution.py:484
  10.2 9.3 %collective-permute-start.4 = (bf16[128,1024]{1,0:T(8,128)(2,1)S(1)}, bf16[128,1024]{1,0:T(8,128)(2,1)}, u32[]{:S(2)}, u32[]{:S(2)}) collective-permute-start(bf16[128,1024]{1,0:T(8,128)(2,1)S(1)} %slice.12), channel_id=1, source_target_pairs={{0,1},{1,0},{2,3},{3,2},{4,5},{5,4},{6,7},{7,6},{8,9},{9,8},{10,11... | collective-permute-start | bytes 786440 | tf_op jit(solution)/shard_map/ppermute | solution.py:472
  12.4 13.3 %collective-permute-start.2 = (bf16[128,1024]{1,0:T(8,128)(2,1)S(1)}, bf16[128,1024]{1,0:T(8,128)(2,1)S(1)}, u32[]{:S(2)}, u32[]{:S(2)}) collective-permute-start(bf16[128,1024]{1,0:T(8,128)(2,1)S(1)} %collective-permute-done.1.refs_4_), channel_id=1, source_target_pairs={{0,1},{1,0},{2,3},{3,2},{4,5},{5,4},{6,7},{7,6},{8,9},{9,8},{10,11... | collective-permute-start | bytes 786440 | tf_op jit(solution)/shard_map/ppermute | solution.py:472
  14.1 11.5 %collective-permute-start.3 = (bf16[128,1024]{1,0:T(8,128)(2,1)S(1)}, bf16[128,1024]{1,0:T(8,128)(2,1)S(1)}, u32[]{:S(2)}, u32[]{:S(2)}) collective-permute-start(bf16[128,1024]{1,0:T(8,128)(2,1)S(1)} %collective-permute-done.refs_2_), channel_id=1, source_target_pairs={{0,4},{1,2},{2,1},{3,7},{4,0},{5,6},{6,5},{7,3},{8,12},{9,10},{10,... | collective-permute-start | bytes 786440 | tf_op jit(solution)/shard_map/ppermute | solution.py:484
  19.5 11.1 %collective-permute-start.7 = (bf16[128,1024]{1,0:T(8,128)(2,1)}, bf16[128,1024]{1,0:T(8,128)(2,1)}, u32[]{:S(2)}, u32[]{:S(2)}) collective-permute-start(bf16[128,1024]{1,0:T(8,128)(2,1)} %collective-permute-done.4.refs_1_), channel_id=1, source_target_pairs={{0,4},{1,2},{2,1},{3,7},{4,0},{5,6},{6,5},{7,3},{8,12},{9,10},{10,... | collective-permute-start | bytes 786440 | tf_op jit(solution)/shard_map/ppermute | solution.py:484
  19.5 11.1 %collective-permute-start.6 = (bf16[128,1024]{1,0:T(8,128)(2,1)}, bf16[128,1024]{1,0:T(8,128)(2,1)}, u32[]{:S(2)}, u32[]{:S(2)}) collective-permute-start(bf16[128,1024]{1,0:T(8,128)(2,1)} %collective-permute-done.5.refs_3_), channel_id=1, source_target_pairs={{0,1},{1,0},{2,3},{3,2},{4,5},{5,4},{6,7},{7,6},{8,9},{9,8},{10,11... | collective-permute-start | bytes 786440 | tf_op jit(solution)/shard_map/ppermute | solution.py:472
  28.9 9.3 %collective-permute-start.9 = (bf16[128,1024]{1,0:T(8,128)(2,1)S(1)}, bf16[128,1024]{1,0:T(8,128)(2,1)S(1)}, u32[]{:S(2)}, u32[]{:S(2)}) collective-permute-start(bf16[128,1024]{1,0:T(8,128)(2,1)S(1)} %collective-permute-done.3.refs_4_), channel_id=1, source_target_pairs={{0,1},{1,0},{2,3},{3,2},{4,5},{5,4},{6,7},{7,6},{8,9},{9,8},{10,11... | collective-permute-start | bytes 786440 | tf_op jit(solution)/shard_map/ppermute | solution.py:472
  30.6 12.1 %collective-permute-start.10 = (bf16[128,1024]{1,0:T(8,128)(2,1)}, bf16[128,1024]{1,0:T(8,128)(2,1)S(1)}, u32[]{:S(2)}, u32[]{:S(2)}) collective-permute-start(bf16[128,1024]{1,0:T(8,128)(2,1)} %collective-permute-done.7.refs_3_), channel_id=1, source_target_pairs={{0,1},{1,0},{2,3},{3,2},{4,5},{5,4},{6,7},{7,6},{8,9},{9,8},{10,11... | collective-permute-start | bytes 786440 | tf_op jit(solution)/shard_map/ppermute | solution.py:472
  46.6 5.4 %collective-permute-start.14 = (f32[19,8,128]{2,1,0:T(8,128)S(1)}, f32[19,8,128]{2,1,0:T(8,128)S(1)}, u32[]{:S(2)}, u32[]{:S(2)}) collective-permute-start(f32[19,8,128]{2,1,0:T(8,128)S(1)} %fold.1), channel_id=1, source_target_pairs={{0,24},{4,28},{8,16},{12,20},{16,8},{20,12},{24,0},{28,4},{1,25},{... | collective-permute-start | bytes 233480 | tf_op jit(solution)/shard_map/ppermute | solution.py:488
  49.1 4.5 %collective-permute-start.13 = (f32[19,8,128]{2,1,0:T(8,128)S(1)}, f32[19,8,128]{2,1,0:T(8,128)S(1)}, u32[]{:S(2)}, u32[]{:S(2)}) collective-permute-start(f32[19,8,128]{2,1,0:T(8,128)S(1)} %fold.1), channel_id=1, source_target_pairs={{0,16},{4,20},{8,24},{12,28},{16,0},{20,4},{24,8},{28,12},{1,17},{... | collective-permute-start | bytes 233480 | tf_op jit(solution)/shard_map/ppermute | solution.py:488
  49.7 4.4 %collective-permute-start.12 = (f32[19,8,128]{2,1,0:T(8,128)S(1)}, f32[19,8,128]{2,1,0:T(8,128)S(1)}, u32[]{:S(2)}, u32[]{:S(2)}) collective-permute-start(f32[19,8,128]{2,1,0:T(8,128)S(1)} %fold.1), channel_id=1, source_target_pairs={{0,8},{4,12},{8,0},{12,4},{16,24},{20,28},{24,16},{28,20},{1,9},{5... | collective-permute-start | bytes 233480 | tf_op jit(solution)/shard_map/ppermute | solution.py:488
  59.2 9.3 %collective-permute-start.15 = (bf16[512,256]{1,0:T(8,128)(2,1)S(1)}, bf16[512,256]{1,0:T(8,128)(2,1)S(1)}, u32[]{:S(2)}, u32[]{:S(2)}) collective-permute-start(bf16[512,256]{1,0:T(8,128)(2,1)S(1)} %get-tuple-element.102), channel_id=1, source_target_pairs={{0,1},{1,0},{2,3},{3,2},{4,5},{5,4},{6,7},{7,6},{8,9},{9,8},{10,11... | collective-permute-start | bytes 786440 | tf_op jit(solution)/shard_map/ppermute | solution.py:472
  60.3 12.2 %collective-permute-start.21 = (bf16[512,256]{1,0:T(8,128)(2,1)S(1)}, bf16[512,256]{1,0:T(8,128)(2,1)S(1)}, u32[]{:S(2)}, u32[]{:S(2)}) collective-permute-start(bf16[512,256]{1,0:T(8,128)(2,1)S(1)} %get-tuple-element.121), channel_id=1, source_target_pairs={{0,1},{1,0},{2,3},{3,2},{4,5},{5,4},{6,7},{7,6},{8,9},{9,8},{10,11... | collective-permute-start | bytes 786440 | tf_op jit(solution)/shard_map/ppermute | solution.py:472
  68.6 11.0 %collective-permute-start.17 = (bf16[512,256]{1,0:T(8,128)(2,1)S(1)}, bf16[512,256]{1,0:T(8,128)(2,1)S(1)}, u32[]{:S(2)}, u32[]{:S(2)}) collective-permute-start(bf16[512,256]{1,0:T(8,128)(2,1)S(1)} %add_convert_fusion.7), channel_id=1, source_target_pairs={{0,4},{1,2},{2,1},{3,7},{4,0},{5,6},{6,5},{7,3},{8,12},{9,10},{10,... | collective-permute-start | bytes 786440 | tf_op jit(solution)/shard_map/ppermute | solution.py:484
  68.7 11.0 %collective-permute-start.16 = (bf16[512,256]{1,0:T(8,128)(2,1)S(1)}, bf16[512,256]{1,0:T(8,128)(2,1)S(1)}, u32[]{:S(2)}, u32[]{:S(2)}) collective-permute-start(bf16[512,256]{1,0:T(8,128)(2,1)S(1)} %get-tuple-element.113), channel_id=1, source_target_pairs={{0,1},{1,0},{2,3},{3,2},{4,5},{5,4},{6,7},{7,6},{8,9},{9,8},{10,11... | collective-permute-start | bytes 786440 | tf_op jit(solution)/shard_map/ppermute | solution.py:472
  70.6 12.8 %collective-permute-start.20 = (bf16[512,256]{1,0:T(8,128)(2,1)S(1)}, bf16[512,256]{1,0:T(8,128)(2,1)S(1)}, u32[]{:S(2)}, u32[]{:S(2)}) collective-permute-start(bf16[512,256]{1,0:T(8,128)(2,1)S(1)} %get-tuple-element.120), channel_id=1, source_target_pairs={{0,1},{1,0},{2,3},{3,2},{4,5},{5,4},{6,7},{7,6},{8,9},{9,8},{10,11... | collective-permute-start | bytes 786440 | tf_op jit(solution)/shard_map/ppermute | solution.py:472
  72.5 10.9 %collective-permute-start.22 = (bf16[512,256]{1,0:T(8,128)(2,1)S(1)}, bf16[512,256]{1,0:T(8,128)(2,1)S(1)}, u32[]{:S(2)}, u32[]{:S(2)}) collective-permute-start(bf16[512,256]{1,0:T(8,128)(2,1)S(1)} %add_convert_fusion.4), channel_id=1, source_target_pairs={{0,4},{1,2},{2,1},{3,7},{4,0},{5,6},{6,5},{7,3},{8,12},{9,10},{10,... | collective-permute-start | bytes 786440 | tf_op jit(solution)/shard_map/ppermute | solution.py:484
  80.4 11.8 %collective-permute-start.18 = (bf16[512,256]{1,0:T(8,128)(2,1)S(1)}, bf16[512,256]{1,0:T(8,128)(2,1)S(1)}, u32[]{:S(2)}, u32[]{:S(2)}) collective-permute-start(bf16[512,256]{1,0:T(8,128)(2,1)S(1)} %add_convert_fusion.6), channel_id=1, source_target_pairs={{0,1},{1,0},{2,3},{3,2},{4,5},{5,4},{6,7},{7,6},{8,9},{9,8},{10,11... | collective-permute-start | bytes 786440 | tf_op jit(solution)/shard_map/ppermute | solution.py:472
  81.9 10.3 %collective-permute-start.19 = (bf16[512,256]{1,0:T(8,128)(2,1)S(1)}, bf16[512,256]{1,0:T(8,128)(2,1)S(1)}, u32[]{:S(2)}, u32[]{:S(2)}) collective-permute-start(bf16[512,256]{1,0:T(8,128)(2,1)S(1)} %add_convert_fusion.5), channel_id=1, source_target_pairs={{0,4},{1,2},{2,1},{3,7},{4,0},{5,6},{6,5},{7,3},{8,12},{9,10},{10,... | collective-permute-start | bytes 786440 | tf_op jit(solution)/shard_map/ppermute | solution.py:484
  83.5 4.4 %collective-permute-start.25 = (f32[16,1024]{1,0:T(8,128)S(1)}, f32[16,1024]{1,0:T(8,128)S(1)}, u32[]{:S(2)}, u32[]{:S(2)}) collective-permute-start(f32[16,1024]{1,0:T(8,128)S(1)} %add.95), channel_id=1, source_target_pairs={{0,8},{4,12},{8,0},{12,4},{16,24},{20,28},{24,16},{28,20},{1,9},{5... | collective-permute-start | bytes 196616 | tf_op jit(solution)/shard_map/ppermute | solution.py:488
  85.7 9.0 %collective-permute-start.23 = (bf16[512,256]{1,0:T(8,128)(2,1)S(1)}, bf16[512,256]{1,0:T(8,128)(2,1)S(1)}, u32[]{:S(2)}, u32[]{:S(2)}) collective-permute-start(bf16[512,256]{1,0:T(8,128)(2,1)S(1)} %add_convert_fusion.3), channel_id=1, source_target_pairs={{0,1},{1,0},{2,3},{3,2},{4,5},{5,4},{6,7},{7,6},{8,9},{9,8},{10,11... | collective-permute-start | bytes 786440 | tf_op jit(solution)/shard_map/ppermute | solution.py:472
  90.0 5.4 %collective-permute-start.27 = (bf16[512,256]{1,0:T(8,128)(2,1)S(1)}, bf16[512,256]{1,0:T(8,128)(2,1)S(1)}, u32[]{:S(2)}, u32[]{:S(2)}) collective-permute-start(bf16[512,256]{1,0:T(8,128)(2,1)S(1)} %add_convert_fusion.1), channel_id=1, source_target_pairs={{0,4},{1,2},{2,1},{3,7},{4,0},{5,6},{6,5},{7,3},{8,12},{9,10},{10,... | collective-permute-start | bytes 786440 | tf_op jit(solution)/shard_map/ppermute | solution.py:484
  (7 other events, 36.8 us)

commit v7 on v6

--- a/solution.py
+++ b/solution.py
@@ -156,7 +156,7 @@
         state = (jnp.zeros((ROWS, LANES), jnp.float32),) * poles
     else:
         state = tuple(later[m] for m in range(poles))
-    state = lax.fori_loop(0, tokens, body, state, unroll=8)
+    state = lax.fori_loop(0, tokens, body, state, unroll=16)
     for m in range(poles):
         packet[m] = state[m]
     if not late:
@@ -237,7 +237,7 @@
         return (now,) + after[:-1]
 
     after = tuple(late_query[tile(half - TAIL + row), :] for row in range(extra))
-    after = lax.fori_loop(0, half - TAIL, late_body, after, unroll=8)
+    after = lax.fori_loop(0, half - TAIL, late_body, after, unroll=16)
 
     def body(n, carry):
         state, after = carry
@@ -252,7 +252,7 @@
         return state, (now,) + after[:-1]
 
     state = tuple(later[m] for m in range(poles))
-    lax.fori_loop(0, half, body, (state, after), unroll=8)
+    lax.fori_loop(0, half, body, (state, after), unroll=16)
     gather_rows(spread, queries, 0, 2 * half - TAIL)
 
 
@@ -345,7 +345,7 @@
 
     carry = (parts, (tuple(keys), tuple(values)))
     for first, products in ((half, late_products), (0, early_products)):
-        carry = lax.fori_loop(0, half, functools.partial(body, first, products), carry, unroll=8)
+        carry = lax.fori_loop(0, half, functools.partial(body, first, products), carry, unroll=16)
     for which in range(1, 3):
         gather_rows(spread.at[which], proj.at[which], 0, tokens)
     copy.wait()
@@ -405,7 +405,7 @@
 
     state = tuple(entering[m] for m in range(poles))
     zero = jnp.zeros((ROWS, LANES), jnp.float32)
-    _, sums = lax.fori_loop(0, tokens, body, (state, (zero,) * poles), unroll=8)
+    _, sums = lax.fori_loop(0, tokens, body, (state, (zero,) * poles), unroll=16)
     for m in range(poles):
         tiles_of[pl.ds(m * ROWS, ROWS), :] = sums[m]
     gather_rows(tiles_of, total, 0, poles)

time: 96.9 us -> 96.9 us (level)
  no operation moved by 1% of the time
where the time goes in v7:
time: 96.9 us; the launch traced here: 96.3 us
  Pallas kernels  36.4 us (38%)
  starting transfers between devices  29.2 us (30%)
  waiting for transfers between devices  20.3 us (21%)
  local copies, waits for them, and re-layouts  5.59 us (6%)
  other arithmetic  3.82 us (4%)
  between operations  1.04 us (1%)
    ppermute x12, starting transfers between devices, swap_even(): return lax.ppermute(value, 'chan', [(i, i ^ 1) for i in range(count)])  19.2 us
    ppermute x12, waiting for transfers between devices, swap_even(): return lax.ppermute(value, 'chan', [(i, i ^ 1) for i in range(count)])  14.2 us
    pallas_call x2, Pallas kernels, project(): pl.pallas_call(functools.partial(project_kernel, at, count, len(sources))...  12.2 us
    pallas_call x3, Pallas kernels, gate_step(): pl.pallas_call(functools.partial(gate_kernel, at, has_acc, shards, len(pi...  10.4 us
    ppermute x7, starting transfers between devices, swap_ctx(): return lax.ppermute(value, 'ctx', [(i, i ^ mask) for i in range(blocks)])  8.37 us
    ppermute x7, waiting for transfers between devices, swap_ctx(): return lax.ppermute(value, 'ctx', [(i, i ^ mask) for i in range(blocks)])  6.1 us
    pallas_call x1, Pallas kernels, scan_block(): pl.pallas_call(functools.partial(scan_kernel, at, taps, len(arrived) + 1)...  5.17 us
    pallas_call x2, Pallas kernels, close_gate(): pl.pallas_call(functools.partial(close_kernel, at, extra, late), in_specs...  4.83 us
  transfers between devices with their start and end apart: 28, of which 14 were waited for; matrix products, arithmetic and copies ran while one was open for 8% of the time, Pallas kernels for 30%

profile of v7, /device:TPU:0, one launch (start us, length us, event | category | flops | bytes accessed | tf_op | source)
XLA Modules:
  0.0 96.3 jit_solution(15139190226436785969)
XLA Ops:
  2.2 4.1 %collective-permute-start = (bf16[128,1024]{1,0:T(8,128)(2,1)S(1)}, bf16[128,1024]{1,0:T(8,128)(2,1)S(1)}, u32[]{:S(2)}, u32[]{:S(2)}) collective-permute-start(bf16[128,1024]{1,0:T(8,128)(2,1)S(1)} %slice.11), channel_id=1, source_target_pairs={{0,1},{1,0},{2,3},{3,2},{4,5},{5,4},{6,7},{7,6},{8,9},{9,8},{10,11... | collective-permute-start | bytes 786440 | tf_op jit(solution)/shard_map/ppermute | solution.py:472
  12.4 1.7 %collective-permute-start.2 = (bf16[128,1024]{1,0:T(8,128)(2,1)S(1)}, bf16[128,1024]{1,0:T(8,128)(2,1)S(1)}, u32[]{:S(2)}, u32[]{:S(2)}) collective-permute-start(bf16[128,1024]{1,0:T(8,128)(2,1)S(1)} %collective-permute-done.1.refs_4_), channel_id=1, source_target_pairs={{0,1},{1,0},{2,3},{3,2},{4,5},{5,4},{6,7},{7,6},{8,9},{9,8},{10,11... | collective-permute-start | bytes 786440 | tf_op jit(solution)/shard_map/ppermute | solution.py:472
  14.1 2.9 %gate_step.3.refs_0_ = f32[256,1024]{1,0:T(8,128)S(1)} custom-call(s32[14]{0:T(128)S(1)} %stack.65.plan, bf16[256,1024]{1,0:T(8,128)(2,1)S(1)} %copy-done, bf16[1024,4096]{1,0:T(8,128)(2,1)} %refs_5_.3), custom_call_target="tpu_custom_call" | custom-call | flops 1 | bytes 1 | tf_op jit(solution)/shard_map/gate_step/pallas_call | solution.py:105
  17.1 2.4 %collective-permute-done.4.refs_1_ = bf16[128,1024]{1,0:T(8,128)(2,1)} collective-permute-done((bf16[128,1024]{1,0:T(8,128)(2,1)S(1)}, bf16[128,1024]{1,0:T(8,128)(2,1)}, u32[]{:S(2)}, u32[]{:S(2)}) %collective-permute-start.4) | collective-permute-done | bytes 262176 | tf_op jit(solution)/shard_map/ppermute | solution.py:472
  19.5 2.0 %collective-permute-start.6 = (bf16[128,1024]{1,0:T(8,128)(2,1)}, bf16[128,1024]{1,0:T(8,128)(2,1)}, u32[]{:S(2)}, u32[]{:S(2)}) collective-permute-start(bf16[128,1024]{1,0:T(8,128)(2,1)} %collective-permute-done.5.refs_3_), channel_id=1, source_target_pairs={{0,1},{1,0},{2,3},{3,2},{4,5},{5,4},{6,7},{7,6},{8,9},{9,8},{10,11... | collective-permute-start | bytes 786440 | tf_op jit(solution)/shard_map/ppermute | solution.py:472
  21.5 4.1 %gate_step.4.refs_0_ = f32[256,1024]{1,0:T(8,128)S(1)} custom-call(s32[14]{0:T(128)S(1)} %stack.65.plan, f32[256,1024]{1,0:T(8,128)S(1)} %gate_step.3.refs_0_, bf16[128,1024]{1,0:T(8,128)(2,1)} %collective-permute-done.4.refs_1_, bf16[128,1024]{1,0:T(8,128)(2,1)S(1)} %collective-permute-done.refs_2_, bf16[128,1024]{1,0:T(8,128)(2,1)} %collective-permute-done.5.refs_3_, ...), custom_call_target="tpu_custom_call" | custom-call | flops 1 | bytes 1 | tf_op jit(solution)/shard_map/gate_step/pallas_call | solution.py:105
  27.1 1.8 %constant_dynamic-slice_fusion.weight = bf16[1024,1024]{1,0:T(8,128)(2,1)S(1)} fusion(bf16[1024,4096]{1,0:T(8,128)(2,1)} %refs_5_.3, s32[]{:T(128)S(6)} %select_n.93), kind=kLoop, calls=%fused_computation.14 | loop fusion | bytes 4194308 | tf_op jit(solution)/shard_map/dynamic_slice | solution.py:588
  28.9 1.7 %collective-permute-start.9 = (bf16[128,1024]{1,0:T(8,128)(2,1)S(1)}, bf16[128,1024]{1,0:T(8,128)(2,1)S(1)}, u32[]{:S(2)}, u32[]{:S(2)}) collective-permute-start(bf16[128,1024]{1,0:T(8,128)(2,1)S(1)} %collective-permute-done.3.refs_4_), channel_id=1, source_target_pairs={{0,1},{1,0},{2,3},{3,2},{4,5},{5,4},{6,7},{7,6},{8,9},{9,8},{10,11... | collective-permute-start | bytes 786440 | tf_op jit(solution)/shard_map/ppermute | solution.py:472
  32.8 3.4 %gate_step.5.acc = f32[256,1024]{1,0:T(8,128)S(1)} custom-call(s32[14]{0:T(128)S(1)} %stack.65.plan, f32[256,1024]{1,0:T(8,128)S(1)} %gate_step.4.refs_0_, bf16[128,1024]{1,0:T(8,128)(2,1)} %collective-permute-done.6.refs_1_, bf16[128,1024]{1,0:T(8,128)(2,1)S(1)} %collective-permute-done.2.refs_2_, bf16[128,1024]{1,0:T(8,128)(2,1)} %collective-permute-done.7.refs_3_, ...), custom_call_target="tpu_custom_call" | custom-call | flops 1 | bytes 1 | tf_op jit(solution)/shard_map/gate_step/pallas_call | solution.py:105
  36.2 1.9 %collective-permute-done.9.piece = bf16[128,1024]{1,0:T(8,128)(2,1)S(1)} collective-permute-done((bf16[128,1024]{1,0:T(8,128)(2,1)S(1)}, bf16[128,1024]{1,0:T(8,128)(2,1)S(1)}, u32[]{:S(2)}, u32[]{:S(2)}) %collective-permute-start.9) | collective-permute-done | bytes 262176 | tf_op jit(solution)/shard_map/ppermute | solution.py:472
  38.1 2.8 %close_gate.2 = (f32[1024,128]{1,0:T(8,128)S(1)}, f32[1024,128]{1,0:T(8,128)S(1)}, f32[16,8,128]{2,1,0:T(8,128)S(1)}, f32[1024,128]{1,0:T(8,128)S(1)}) custom-call(s32[14]{0:T(128)S(1)} %stack.65.plan, f32[256,1024]{1,0:T(8,128)S(1)} %gate_step.5.acc, bf16[128,1024]{1,0:T(8,128)(2,1)S(1)} %collective-permute-done.9.piece, ...), custom_call_target="tpu_custom_call" | custom-call | flops 1 | bytes 1 | tf_op jit(solution)/shard_map/close_gate/pallas_call | solution.py:177
  40.9 1.7 %collective-permute-done.10.piece = bf16[128,1024]{1,0:T(8,128)(2,1)S(1)} collective-permute-done((bf16[128,1024]{1,0:T(8,128)(2,1)}, bf16[128,1024]{1,0:T(8,128)(2,1)S(1)}, u32[]{:S(2)}, u32[]{:S(2)}) %collective-permute-start.10) | collective-permute-done | bytes 262176 | tf_op jit(solution)/shard_map/ppermute | solution.py:472
  42.7 2.0 %close_gate.3 = (f32[1024,128]{1,0:T(8,128)S(1)}, f32[1024,128]{1,0:T(8,128)S(1)}, f32[19,8,128]{2,1,0:T(8,128)S(1)}) custom-call(s32[14]{0:T(128)S(1)} %stack.65.plan, f32[256,1024]{1,0:T(8,128)S(1)} %gate_step.5.acc, bf16[128,1024]{1,0:T(8,128)(2,1)S(1)} %collective-permute-done.10.piece, bf16[1024,1024]{1,0:T(8,128)(2,1)S(1)} %constant_dynamic-slice_fusion.weight, ...), custom_call_target="tpu_custom_call" | custom-call | flops 1 | bytes 1 | tf_op jit(solution)/shard_map/close_gate/pallas_call | solution.py:177
  46.6 2.5 %collective-permute-start.14 = (f32[19,8,128]{2,1,0:T(8,128)S(1)}, f32[19,8,128]{2,1,0:T(8,128)S(1)}, u32[]{:S(2)}, u32[]{:S(2)}) collective-permute-start(f32[19,8,128]{2,1,0:T(8,128)S(1)} %fold.1), channel_id=1, source_target_pairs={{0,24},{4,28},{8,16},{12,20},{16,8},{20,12},{24,0},{28,4},{1,25},{... | collective-permute-start | bytes 233480 | tf_op jit(solution)/shard_map/ppermute | solution.py:488
  50.2 1.8 %settle.1 = (f32[1024,128]{1,0:T(8,128)S(1)}, f32[2048,128]{1,0:T(8,128)S(1)}, bf16[256,1024]{1,0:T(8,128)(2,1)S(1)}) custom-call(f32[16,8,128]{2,1,0:T(8,128)S(1)} %get-tuple-element.88.other.later, f32[1024,128]{1,0:T(8,128)S(1)} %get-tuple-element.89.late_conv, f32[1024,128]{1,0:T(8,128)S(1)} %get-tuple-element.90.late_query, ...), custom_call_target="tpu_custom_call" | custom-call | flops 1 | bytes 1 | tf_op jit(solution)/shard_map/settle/pallas_call | solution.py:262
  54.0 5.2 %scan.1 = (bf16[3,256,1024]{2,1,0:T(8,128)(2,1)S(1)}, bf16[512,256]{1,0:T(8,128)(2,1)S(1)}, bf16[512,256]{1,0:T(8,128)(2,1)S(1)}, f32[16,8,128]{2,1,0:T(8,128)S(1)}) custom-call(s32[14]{0:T(128)S(1)} %stack.65.plan, f32[1024,128]{1,0:T(8,128)S(1)} %get-tuple-element.87.late_products, f32[1024,128]{1,0:T(8,128)S(1)} %get-tuple-element.94.early_products, ...), custom_call_target="tpu_custom_call" | custom-call | flops 1 | bytes 1 | tf_op jit(solution)/shard_map/scan/pallas_call | solution.py:359
  61.3 5.2 %project.2 = (f32[16,1024]{1,0:T(8,128)S(1)}, bf16[512,256]{1,0:T(8,128)(2,1)S(1)}, bf16[512,256]{1,0:T(8,128)(2,1)S(1)}) custom-call(s32[14]{0:T(128)S(1)} %stack.65.plan, bf16[3,256,1024]{2,1,0:T(8,128)(2,1)S(1)} %get-tuple-element.110.proj, bf16[3,4096,1024]{2,1,0:T(8,128)(2,1)} %weight.3, f32[2048,128]{1,0:T(8,128)S(1)} %get-tuple-element.104.refs_0_, ...), custom_call_target="tpu_custom_call" | custom-call | flops 1610612736 | bytes 6291456 | tf_op jit(solution)/shard_map/project/pallas_call | solution.py:439
  66.5 2.0 %collective-permute-done.15 = bf16[512,256]{1,0:T(8,128)(2,1)S(1)} collective-permute-done((bf16[512,256]{1,0:T(8,128)(2,1)S(1)}, bf16[512,256]{1,0:T(8,128)(2,1)S(1)}, u32[]{:S(2)}, u32[]{:S(2)}) %collective-permute-start.15) | collective-permute-done | bytes 262176 | tf_op jit(solution)/shard_map/ppermute | solution.py:472
  68.7 1.9 %collective-permute-start.16 = (bf16[512,256]{1,0:T(8,128)(2,1)S(1)}, bf16[512,256]{1,0:T(8,128)(2,1)S(1)}, u32[]{:S(2)}, u32[]{:S(2)}) collective-permute-start(bf16[512,256]{1,0:T(8,128)(2,1)S(1)} %get-tuple-element.113), channel_id=1, source_target_pairs={{0,1},{1,0},{2,3},{3,2},{4,5},{5,4},{6,7},{7,6},{8,9},{9,8},{10,11... | collective-permute-start | bytes 786440 | tf_op jit(solution)/shard_map/ppermute | solution.py:472
  72.6 7.0 %project.3 = (bf16[512,256]{1,0:T(8,128)(2,1)S(1)}, bf16[512,256]{1,0:T(8,128)(2,1)S(1)}, bf16[512,256]{1,0:T(8,128)(2,1)S(1)}, bf16[512,256]{1,0:T(8,128)(2,1)S(1)}) custom-call(s32[14]{0:T(128)S(1)} %stack.65.plan, bf16[3,256,1024]{2,1,0:T(8,128)(2,1)S(1)} %get-tuple-element.110.proj, bf16[3,4096,1024]{2,1,0:T(8,128)(2,1)} %weight.3), custom_call_target="tpu_custom_call" | custom-call | flops 3221225472 | bytes 12582912 | tf_op jit(solution)/shard_map/project/pallas_call | solution.py:439
  83.5 2.1 %collective-permute-start.25 = (f32[16,1024]{1,0:T(8,128)S(1)}, f32[16,1024]{1,0:T(8,128)S(1)}, u32[]{:S(2)}, u32[]{:S(2)}) collective-permute-start(f32[16,1024]{1,0:T(8,128)S(1)} %add.95), channel_id=1, source_target_pairs={{0,8},{4,12},{8,0},{12,4},{16,24},{20,28},{24,16},{28,20},{1,9},{5... | collective-permute-start | bytes 196616 | tf_op jit(solution)/shard_map/ppermute | solution.py:488
  87.8 2.1 %collective-permute-start.26 = (f32[16,1024]{1,0:T(8,128)S(1)}, f32[16,1024]{1,0:T(8,128)S(1)}, u32[]{:S(2)}, u32[]{:S(2)}) collective-permute-start(f32[16,1024]{1,0:T(8,128)S(1)} %add.96), channel_id=1, source_target_pairs={{0,16},{4,20},{8,24},{12,28},{16,0},{20,4},{24,8},{28,12},{1,17},{... | collective-permute-start | bytes 196616 | tf_op jit(solution)/shard_map/ppermute | solution.py:488
  90.1 2.1 %collective-permute-done.26 = f32[16,1024]{1,0:T(8,128)S(1)} collective-permute-done((f32[16,1024]{1,0:T(8,128)S(1)}, f32[16,1024]{1,0:T(8,128)S(1)}, u32[]{:S(2)}, u32[]{:S(2)}) %collective-permute-start.26) | collective-permute-done | bytes 65568 | tf_op jit(solution)/shard_map/ppermute | solution.py:488
  92.2 2.4 %collective-permute-done.23 = bf16[512,256]{1,0:T(8,128)(2,1)S(1)} collective-permute-done((bf16[512,256]{1,0:T(8,128)(2,1)S(1)}, bf16[512,256]{1,0:T(8,128)(2,1)S(1)}, u32[]{:S(2)}, u32[]{:S(2)}) %collective-permute-start.23) | collective-permute-done | bytes 262176 | tf_op jit(solution)/shard_map/ppermute | solution.py:472
  (72 shorter events, 28.2 us)
Async XLA Ops:
  1.7 10.2 %collective-permute-start.1 = (bf16[128,1024]{1,0:T(8,128)(2,1)S(1)}, bf16[128,1024]{1,0:T(8,128)(2,1)S(1)}, u32[]{:S(2)}, u32[]{:S(2)}) collective-permute-start(bf16[128,1024]{1,0:T(8,128)(2,1)S(1)} %slice.11), channel_id=1, source_target_pairs={{0,4},{1,2},{2,1},{3,7},{4,0},{5,6},{6,5},{7,3},{8,12},{9,10},{10,... | collective-permute-start | bytes 786440 | tf_op jit(solution)/shard_map/ppermute | solution.py:484
  2.2 10.2 %collective-permute-start = (bf16[128,1024]{1,0:T(8,128)(2,1)S(1)}, bf16[128,1024]{1,0:T(8,128)(2,1)S(1)}, u32[]{:S(2)}, u32[]{:S(2)}) collective-permute-start(bf16[128,1024]{1,0:T(8,128)(2,1)S(1)} %slice.11), channel_id=1, source_target_pairs={{0,1},{1,0},{2,3},{3,2},{4,5},{5,4},{6,7},{7,6},{8,9},{9,8},{10,11... | collective-permute-start | bytes 786440 | tf_op jit(solution)/shard_map/ppermute | solution.py:472
  10.1 6.9 %collective-permute-start.5 = (bf16[128,1024]{1,0:T(8,128)(2,1)S(1)}, bf16[128,1024]{1,0:T(8,128)(2,1)}, u32[]{:S(2)}, u32[]{:S(2)}) collective-permute-start(bf16[128,1024]{1,0:T(8,128)(2,1)S(1)} %slice.12), channel_id=1, source_target_pairs={{0,4},{1,2},{2,1},{3,7},{4,0},{5,6},{6,5},{7,3},{8,12},{9,10},{10,... | collective-permute-start | bytes 786440 | tf_op jit(solution)/shard_map/ppermute | solution.py:484
  10.2 9.3 %collective-permute-start.4 = (bf16[128,1024]{1,0:T(8,128)(2,1)S(1)}, bf16[128,1024]{1,0:T(8,128)(2,1)}, u32[]{:S(2)}, u32[]{:S(2)}) collective-permute-start(bf16[128,1024]{1,0:T(8,128)(2,1)S(1)} %slice.12), channel_id=1, source_target_pairs={{0,1},{1,0},{2,3},{3,2},{4,5},{5,4},{6,7},{7,6},{8,9},{9,8},{10,11... | collective-permute-start | bytes 786440 | tf_op jit(solution)/shard_map/ppermute | solution.py:472
  12.4 13.3 %collective-permute-start.2 = (bf16[128,1024]{1,0:T(8,128)(2,1)S(1)}, bf16[128,1024]{1,0:T(8,128)(2,1)S(1)}, u32[]{:S(2)}, u32[]{:S(2)}) collective-permute-start(bf16[128,1024]{1,0:T(8,128)(2,1)S(1)} %collective-permute-done.1.refs_4_), channel_id=1, source_target_pairs={{0,1},{1,0},{2,3},{3,2},{4,5},{5,4},{6,7},{7,6},{8,9},{9,8},{10,11... | collective-permute-start | bytes 786440 | tf_op jit(solution)/shard_map/ppermute | solution.py:472
  14.1 11.5 %collective-permute-start.3 = (bf16[128,1024]{1,0:T(8,128)(2,1)S(1)}, bf16[128,1024]{1,0:T(8,128)(2,1)S(1)}, u32[]{:S(2)}, u32[]{:S(2)}) collective-permute-start(bf16[128,1024]{1,0:T(8,128)(2,1)S(1)} %collective-permute-done.refs_2_), channel_id=1, source_target_pairs={{0,4},{1,2},{2,1},{3,7},{4,0},{5,6},{6,5},{7,3},{8,12},{9,10},{10,... | collective-permute-start | bytes 786440 | tf_op jit(solution)/shard_map/ppermute | solution.py:484
  19.5 11.1 %collective-permute-start.7 = (bf16[128,1024]{1,0:T(8,128)(2,1)}, bf16[128,1024]{1,0:T(8,128)(2,1)}, u32[]{:S(2)}, u32[]{:S(2)}) collective-permute-start(bf16[128,1024]{1,0:T(8,128)(2,1)} %collective-permute-done.4.refs_1_), channel_id=1, source_target_pairs={{0,4},{1,2},{2,1},{3,7},{4,0},{5,6},{6,5},{7,3},{8,12},{9,10},{10,... | collective-permute-start | bytes 786440 | tf_op jit(solution)/shard_map/ppermute | solution.py:484
  19.5 11.1 %collective-permute-start.6 = (bf16[128,1024]{1,0:T(8,128)(2,1)}, bf16[128,1024]{1,0:T(8,128)(2,1)}, u32[]{:S(2)}, u32[]{:S(2)}) collective-permute-start(bf16[128,1024]{1,0:T(8,128)(2,1)} %collective-permute-done.5.refs_3_), channel_id=1, source_target_pairs={{0,1},{1,0},{2,3},{3,2},{4,5},{5,4},{6,7},{7,6},{8,9},{9,8},{10,11... | collective-permute-start | bytes 786440 | tf_op jit(solution)/shard_map/ppermute | solution.py:472
  28.9 9.3 %collective-permute-start.9 = (bf16[128,1024]{1,0:T(8,128)(2,1)S(1)}, bf16[128,1024]{1,0:T(8,128)(2,1)S(1)}, u32[]{:S(2)}, u32[]{:S(2)}) collective-permute-start(bf16[128,1024]{1,0:T(8,128)(2,1)S(1)} %collective-permute-done.3.refs_4_), channel_id=1, source_target_pairs={{0,1},{1,0},{2,3},{3,2},{4,5},{5,4},{6,7},{7,6},{8,9},{9,8},{10,11... | collective-permute-start | bytes 786440 | tf_op jit(solution)/shard_map/ppermute | solution.py:472
  30.6 12.1 %collective-permute-start.10 = (bf16[128,1024]{1,0:T(8,128)(2,1)}, bf16[128,1024]{1,0:T(8,128)(2,1)S(1)}, u32[]{:S(2)}, u32[]{:S(2)}) collective-permute-start(bf16[128,1024]{1,0:T(8,128)(2,1)} %collective-permute-done.7.refs_3_), channel_id=1, source_target_pairs={{0,1},{1,0},{2,3},{3,2},{4,5},{5,4},{6,7},{7,6},{8,9},{9,8},{10,11... | collective-permute-start | bytes 786440 | tf_op jit(solution)/shard_map/ppermute | solution.py:472
  46.6 5.4 %collective-permute-start.14 = (f32[19,8,128]{2,1,0:T(8,128)S(1)}, f32[19,8,128]{2,1,0:T(8,128)S(1)}, u32[]{:S(2)}, u32[]{:S(2)}) collective-permute-start(f32[19,8,128]{2,1,0:T(8,128)S(1)} %fold.1), channel_id=1, source_target_pairs={{0,24},{4,28},{8,16},{12,20},{16,8},{20,12},{24,0},{28,4},{1,25},{... | collective-permute-start | bytes 233480 | tf_op jit(solution)/shard_map/ppermute | solution.py:488
  49.1 4.5 %collective-permute-start.13 = (f32[19,8,128]{2,1,0:T(8,128)S(1)}, f32[19,8,128]{2,1,0:T(8,128)S(1)}, u32[]{:S(2)}, u32[]{:S(2)}) collective-permute-start(f32[19,8,128]{2,1,0:T(8,128)S(1)} %fold.1), channel_id=1, source_target_pairs={{0,16},{4,20},{8,24},{12,28},{16,0},{20,4},{24,8},{28,12},{1,17},{... | collective-permute-start | bytes 233480 | tf_op jit(solution)/shard_map/ppermute | solution.py:488
  49.6 4.4 %collective-permute-start.12 = (f32[19,8,128]{2,1,0:T(8,128)S(1)}, f32[19,8,128]{2,1,0:T(8,128)S(1)}, u32[]{:S(2)}, u32[]{:S(2)}) collective-permute-start(f32[19,8,128]{2,1,0:T(8,128)S(1)} %fold.1), channel_id=1, source_target_pairs={{0,8},{4,12},{8,0},{12,4},{16,24},{20,28},{24,16},{28,20},{1,9},{5... | collective-permute-start | bytes 233480 | tf_op jit(solution)/shard_map/ppermute | solution.py:488
  59.2 9.3 %collective-permute-start.15 = (bf16[512,256]{1,0:T(8,128)(2,1)S(1)}, bf16[512,256]{1,0:T(8,128)(2,1)S(1)}, u32[]{:S(2)}, u32[]{:S(2)}) collective-permute-start(bf16[512,256]{1,0:T(8,128)(2,1)S(1)} %get-tuple-element.102), channel_id=1, source_target_pairs={{0,1},{1,0},{2,3},{3,2},{4,5},{5,4},{6,7},{7,6},{8,9},{9,8},{10,11... | collective-permute-start | bytes 786440 | tf_op jit(solution)/shard_map/ppermute | solution.py:472
  60.3 12.2 %collective-permute-start.21 = (bf16[512,256]{1,0:T(8,128)(2,1)S(1)}, bf16[512,256]{1,0:T(8,128)(2,1)S(1)}, u32[]{:S(2)}, u32[]{:S(2)}) collective-permute-start(bf16[512,256]{1,0:T(8,128)(2,1)S(1)} %get-tuple-element.121), channel_id=1, source_target_pairs={{0,1},{1,0},{2,3},{3,2},{4,5},{5,4},{6,7},{7,6},{8,9},{9,8},{10,11... | collective-permute-start | bytes 786440 | tf_op jit(solution)/shard_map/ppermute | solution.py:472
  68.6 11.1 %collective-permute-start.17 = (bf16[512,256]{1,0:T(8,128)(2,1)S(1)}, bf16[512,256]{1,0:T(8,128)(2,1)S(1)}, u32[]{:S(2)}, u32[]{:S(2)}) collective-permute-start(bf16[512,256]{1,0:T(8,128)(2,1)S(1)} %add_convert_fusion.7), channel_id=1, source_target_pairs={{0,4},{1,2},{2,1},{3,7},{4,0},{5,6},{6,5},{7,3},{8,12},{9,10},{10,... | collective-permute-start | bytes 786440 | tf_op jit(solution)/shard_map/ppermute | solution.py:484
  68.7 11.0 %collective-permute-start.16 = (bf16[512,256]{1,0:T(8,128)(2,1)S(1)}, bf16[512,256]{1,0:T(8,128)(2,1)S(1)}, u32[]{:S(2)}, u32[]{:S(2)}) collective-permute-start(bf16[512,256]{1,0:T(8,128)(2,1)S(1)} %get-tuple-element.113), channel_id=1, source_target_pairs={{0,1},{1,0},{2,3},{3,2},{4,5},{5,4},{6,7},{7,6},{8,9},{9,8},{10,11... | collective-permute-start | bytes 786440 | tf_op jit(solution)/shard_map/ppermute | solution.py:472
  70.6 12.9 %collective-permute-start.20 = (bf16[512,256]{1,0:T(8,128)(2,1)S(1)}, bf16[512,256]{1,0:T(8,128)(2,1)S(1)}, u32[]{:S(2)}, u32[]{:S(2)}) collective-permute-start(bf16[512,256]{1,0:T(8,128)(2,1)S(1)} %get-tuple-element.120), channel_id=1, source_target_pairs={{0,1},{1,0},{2,3},{3,2},{4,5},{5,4},{6,7},{7,6},{8,9},{9,8},{10,11... | collective-permute-start | bytes 786440 | tf_op jit(solution)/shard_map/ppermute | solution.py:472
  72.5 10.9 %collective-permute-start.22 = (bf16[512,256]{1,0:T(8,128)(2,1)S(1)}, bf16[512,256]{1,0:T(8,128)(2,1)S(1)}, u32[]{:S(2)}, u32[]{:S(2)}) collective-permute-start(bf16[512,256]{1,0:T(8,128)(2,1)S(1)} %add_convert_fusion.4), channel_id=1, source_target_pairs={{0,4},{1,2},{2,1},{3,7},{4,0},{5,6},{6,5},{7,3},{8,12},{9,10},{10,... | collective-permute-start | bytes 786440 | tf_op jit(solution)/shard_map/ppermute | solution.py:484
  80.4 11.8 %collective-permute-start.18 = (bf16[512,256]{1,0:T(8,128)(2,1)S(1)}, bf16[512,256]{1,0:T(8,128)(2,1)S(1)}, u32[]{:S(2)}, u32[]{:S(2)}) collective-permute-start(bf16[512,256]{1,0:T(8,128)(2,1)S(1)} %add_convert_fusion.6), channel_id=1, source_target_pairs={{0,1},{1,0},{2,3},{3,2},{4,5},{5,4},{6,7},{7,6},{8,9},{9,8},{10,11... | collective-permute-start | bytes 786440 | tf_op jit(solution)/shard_map/ppermute | solution.py:472
  81.9 10.3 %collective-permute-start.19 = (bf16[512,256]{1,0:T(8,128)(2,1)S(1)}, bf16[512,256]{1,0:T(8,128)(2,1)S(1)}, u32[]{:S(2)}, u32[]{:S(2)}) collective-permute-start(bf16[512,256]{1,0:T(8,128)(2,1)S(1)} %add_convert_fusion.5), channel_id=1, source_target_pairs={{0,4},{1,2},{2,1},{3,7},{4,0},{5,6},{6,5},{7,3},{8,12},{9,10},{10,... | collective-permute-start | bytes 786440 | tf_op jit(solution)/shard_map/ppermute | solution.py:484
  85.6 9.0 %collective-permute-start.23 = (bf16[512,256]{1,0:T(8,128)(2,1)S(1)}, bf16[512,256]{1,0:T(8,128)(2,1)S(1)}, u32[]{:S(2)}, u32[]{:S(2)}) collective-permute-start(bf16[512,256]{1,0:T(8,128)(2,1)S(1)} %add_convert_fusion.3), channel_id=1, source_target_pairs={{0,1},{1,0},{2,3},{3,2},{4,5},{5,4},{6,7},{7,6},{8,9},{9,8},{10,11... | collective-permute-start | bytes 786440 | tf_op jit(solution)/shard_map/ppermute | solution.py:472
  87.8 4.4 %collective-permute-start.26 = (f32[16,1024]{1,0:T(8,128)S(1)}, f32[16,1024]{1,0:T(8,128)S(1)}, u32[]{:S(2)}, u32[]{:S(2)}) collective-permute-start(f32[16,1024]{1,0:T(8,128)S(1)} %add.96), channel_id=1, source_target_pairs={{0,16},{4,20},{8,24},{12,28},{16,0},{20,4},{24,8},{28,12},{1,17},{... | collective-permute-start | bytes 196616 | tf_op jit(solution)/shard_map/ppermute | solution.py:488
  90.0 5.4 %collective-permute-start.27 = (bf16[512,256]{1,0:T(8,128)(2,1)S(1)}, bf16[512,256]{1,0:T(8,128)(2,1)S(1)}, u32[]{:S(2)}, u32[]{:S(2)}) collective-permute-start(bf16[512,256]{1,0:T(8,128)(2,1)S(1)} %add_convert_fusion.1), channel_id=1, source_target_pairs={{0,4},{1,2},{2,1},{3,7},{4,0},{5,6},{6,5},{7,3},{8,12},{9,10},{10,... | collective-permute-start | bytes 786440 | tf_op jit(solution)/shard_map/ppermute | solution.py:484
  (7 other events, 36.8 us)
